TPU v7x, 32 devices: a whole 2x2x4 slice. The times are simulated.
32 devices in a mesh: sky: 16 (over z, y, core), loop: 2 (over x).
Axes of the slice: x: 2, y: 2, z: 4, core: 2. Of those that a mesh axis runs over, the one named last changes fastest.
Arguments:
- queries: bfloat16 [24576, 256], P(('sky', 'loop')), may hold values from -1 to 1
- keys: bfloat16 [24576, 256], P(('sky', 'loop')), may hold values from -1 to 1
- partner_owner: int32 [24576, 4], P(('sky', 'loop')), may hold values from 0 to 15, as said below
- partner_row: int32 [24576, 4], P(('sky', 'loop')), may hold values from 0 to 767
- partner_count: int32 [24576], P(('sky', 'loop')), may hold values from 1 to 4, as said below
Outputs:
- loss: float32 [24576], P(('sky', 'loop'))
- grad_queries: float32 [24576, 256], P(('sky', 'loop'))
- grad_keys: float32 [24576, 256], P(('sky', 'loop'))
Inputs may be any that keep to these rules, and one draw needn't show every extreme that they name: `partner_owner`: each row names 4 different sky indices, never its own device's sky index; among the rows of one device no index is named more than 384 times, and on every device some index is named exactly 384 times. `partner_count`: some anchor has 4 live partners and some has one.
All inputs are finite; a program needn't handle non-finite values.
Results may differ from a plain program's by a relative error of at most 0.004.
Values may be sent and summed in bfloat16 or wider, within the bound.
No kernel may reach another device: no remote copies, remote signals or barrier semaphores. Data moves between devices by JAX's collectives and lax.ppermute only.
A program may use at most 64 MiB of HBM per device.

v0:
```python
import jax
import jax.numpy as jnp
from jax import lax
from jax.sharding import PartitionSpec as P

SCALE = 10.0
EPS = 1e-06


def unit_rows(rows):
    wide = rows.astype(jnp.float32)
    norms = jnp.sqrt(jnp.sum(wide * wide, axis=1, keepdims=True) + EPS)
    return (wide / norms, norms)


def back_unit(unit, norms, grad):
    return (grad - unit * jnp.sum(unit * grad, axis=1, keepdims=True)) / norms


def fold_blocks(carry, pieces, step):
    total_rows = pieces[0].shape[0]
    size = 512
    number = total_rows // size
    split = tuple((piece.reshape((number, size) + piece.shape[1:]) for piece in pieces))
    offsets = size * jnp.arange(number, dtype=jnp.int32)

    def one_turn(summed, item):
        return (step(summed, item[0], item[1]), None)

    result, unused = lax.scan(one_turn, carry, (split, offsets))
    return result


def shards(queries, keys, partner_owner, partner_row, partner_count):
    anchors, width = queries.shape
    slots = partner_owner.shape[1]
    sky_count = lax.axis_size("sky")
    bucket = 2 * anchors * slots // sky_count
    unit_q, norm_q = unit_rows(queries)
    unit_k, norm_k = unit_rows(keys)
    query_rows = unit_q.astype(jnp.bfloat16)
    key_rows = unit_k.astype(jnp.bfloat16)
    mine = lax.axis_index("loop") * anchors + jnp.arange(anchors, dtype=jnp.int32)
    valid = jnp.arange(slots, dtype=jnp.int32)[None, :] < partner_count[:, None]
    inverse = 1.0 / (1.0 + partner_count.astype(jnp.float32))
    flat_owner = partner_owner.reshape(-1)
    owner_hits = (flat_owner[:, None] == jnp.arange(sky_count, dtype=jnp.int32)[None, :]).astype(
        jnp.int32
    )
    earlier = jnp.sum((jnp.cumsum(owner_hits, axis=0) - owner_hits) * owner_hits, axis=1)
    slot_index = flat_owner * bucket + earlier
    requests = (
        jnp.zeros((sky_count * bucket,), jnp.int32).at[slot_index].set(partner_row.reshape(-1))
    )
    incoming = lax.all_to_all(
        requests.reshape(sky_count, bucket), "sky", split_axis=0, concat_axis=0, tiled=True
    )
    wanted = incoming.reshape(-1)
    replies = jnp.take(key_rows, wanted, axis=0)
    answered = lax.all_to_all(
        replies.reshape(sky_count, bucket, width), "sky", split_axis=0, concat_axis=0, tiled=True
    )
    partner_keys = jnp.take(answered.reshape(-1, width), slot_index, axis=0).reshape(
        anchors, slots, width
    )
    outgoing = (
        jnp.zeros((sky_count * bucket, width), jnp.bfloat16)
        .at[slot_index]
        .set(jnp.repeat(query_rows, slots, axis=0))
    )
    partner_logits = SCALE * jnp.einsum(
        "apd,ad->ap", partner_keys, query_rows, preferred_element_type=jnp.float32
    )

    def add_exp(total, block, offset):
        scores = SCALE * jnp.dot(query_rows, block[0].T, preferred_element_type=jnp.float32)
        return total + jnp.sum(jnp.exp(scores), axis=1)

    start_sum = jnp.zeros((anchors,), jnp.float32)
    group_keys = lax.all_gather(key_rows, "loop", axis=0, tiled=True)
    total = fold_blocks(start_sum, (group_keys,), add_exp)
    log_total = jnp.log(total + jnp.sum(jnp.where(valid, jnp.exp(partner_logits), 0.0), axis=1))
    own_logits = SCALE * jnp.sum(
        query_rows.astype(jnp.float32) * key_rows.astype(jnp.float32), axis=1
    )
    loss = log_total - inverse * (
        own_logits + jnp.sum(jnp.where(valid, partner_logits, 0.0), axis=1)
    )
    partner_weights = jnp.where(
        valid, jnp.exp(partner_logits - log_total[:, None]) - inverse[:, None], 0.0
    ).astype(jnp.bfloat16)

    def add_grad(summed, block, offset):
        piece = block[0]
        scores = SCALE * jnp.dot(query_rows, piece.T, preferred_element_type=jnp.float32)
        columns = offset + jnp.arange(piece.shape[0], dtype=jnp.int32)
        target = jnp.where(mine[:, None] == columns[None, :], inverse[:, None], 0.0)
        weights = (jnp.exp(scores - log_total[:, None]) - target).astype(jnp.bfloat16)
        return summed + jnp.dot(weights, piece, preferred_element_type=jnp.float32)

    empty = jnp.zeros((anchors, width), jnp.float32)
    summed_q = fold_blocks(empty, (group_keys,), add_grad)
    grad_unit_q = SCALE * (
        summed_q
        + jnp.einsum(
            "ap,apd->ad", partner_weights, partner_keys, preferred_element_type=jnp.float32
        )
    )
    grad_queries = back_unit(unit_q, norm_q, grad_unit_q)
    all_log_total, all_inverse = (
        lax.all_gather(log_total, "loop", axis=0, tiled=True),
        lax.all_gather(inverse, "loop", axis=0, tiled=True),
    )

    def add_key_grad(summed, block, offset):
        piece = block[0]
        number = piece.shape[0]
        scores = SCALE * jnp.dot(piece, key_rows.T, preferred_element_type=jnp.float32)
        piece_log = lax.dynamic_slice_in_dim(all_log_total, offset, number)
        piece_inverse = lax.dynamic_slice_in_dim(all_inverse, offset, number)
        row_ids = offset + jnp.arange(number, dtype=jnp.int32)
        target = jnp.where(row_ids[:, None] == mine[None, :], piece_inverse[:, None], 0.0)
        weights = (jnp.exp(scores - piece_log[:, None]) - target).astype(jnp.bfloat16)
        return summed + lax.dot_general(
            weights, piece, (((0,), (0,)), ((), ())), preferred_element_type=jnp.float32
        )

    summed_k = fold_blocks(
        empty, (lax.all_gather(query_rows, "loop", axis=0, tiled=True),), add_key_grad
    )
    slot_weights = (
        jnp.zeros((sky_count * bucket,), jnp.bfloat16)
        .at[slot_index]
        .set(partner_weights.reshape(-1))
    )
    got_rows, got_weights = (
        lax.all_to_all(
            outgoing.reshape(sky_count, bucket, width),
            "sky",
            split_axis=0,
            concat_axis=0,
            tiled=True,
        ),
        lax.all_to_all(
            slot_weights.reshape(sky_count, bucket), "sky", split_axis=0, concat_axis=0, tiled=True
        ),
    )
    back_rows = got_rows.reshape(-1, width)
    back_weights = got_weights.reshape(-1)
    partner_grad = jax.ops.segment_sum(
        back_weights.astype(jnp.float32)[:, None] * back_rows.astype(jnp.float32),
        wanted,
        num_segments=anchors,
    )
    grad_keys = back_unit(unit_k, norm_k, SCALE * (summed_k + partner_grad))
    return (loss, grad_queries, grad_keys)


def solution(mesh):
    in_specs = (
        P(("sky", "loop"), None),
        P(("sky", "loop"), None),
        P(("sky", "loop"), None),
        P(("sky", "loop"), None),
        P(("sky", "loop")),
    )
    out_specs = (P(("sky", "loop")), P(("sky", "loop"), None), P(("sky", "loop"), None))
    return jax.shard_map(shards, mesh=mesh, in_specs=in_specs, out_specs=out_specs, check_vma=False)
```

profile of v0, /device:TPU:0, one launch (start us, length us, event | category | flops | bytes accessed | tf_op | source)
XLA Modules:
  0.0 341.2 jit_solution(8015863860894997079)
XLA Ops:
  3.2 4.6 %reduce-window.6 = s32[16,24,128]{2,1,0:T(8,128)S(1)} reduce-window(s32[16,24,128]{2,1,0:T(8,128)S(1)} %fusion.56, s32[]{:T(128)} %constant.48.clone.1), window={size=1x1x128 pad=0_0x0_0x127_0}, to_apply=%region_5.6 | reduce-window | flops 6242304 | bytes 393220 | tf_op jit(solution)/shard_map/reduce-window
  9.1 12.4 %scatter_custom_fusion = s32[6144]{0:T(1024)} fusion(s32[3072]{0:T(1024)S(1)} %bitcast.110, s32[3072]{0:T(1024)S(1)} %reshape.223, s32[]{:T(128)} %constant.48.clone.1), kind=kCustom, calls=%fused_computation.91 | custom fusion | bytes 24580 | tf_op jit(solution)/shard_map/scatter | solution.py:53
  21.4 7.4 %all-to-all-start = ((s32[16,1,384]{2,1,0:T(1,128)}), s32[16,1,384]{2,1,0:T(1,128)S(1)}, u32[]{:S(2)}, u32[]{:S(2)}) async-start(s32[16,1,384]{2,1,0:T(1,128)} %bitcast.4), calls=%async_computation | async-start | bytes 49152 | tf_op jit(solution)/shard_map/all_to_all | solution.py:55
  31.5 3.9 %all-to-all-done = s32[16,1,384]{2,1,0:T(1,128)S(1)} async-done(((s32[16,1,384]{2,1,0:T(1,128)}), s32[16,1,384]{2,1,0:T(1,128)S(1)}, u32[]{:S(2)}, u32[]{:S(2)}) %all-to-all-start) | async-done | bytes 24608 | tf_op jit(solution)/shard_map/all_to_all | solution.py:55
  36.1 24.7 %gather_fusion = bf16[6144,256]{1,0:T(8,128)(2,1)S(1)} fusion(bf16[768,256]{1,0:T(8,128)(2,1)S(1)} %get-tuple-element.411, s32[6144]{0:T(1024)} %broadcast_clamp_fusion), kind=kCustom, calls=%fused_computation | custom fusion | bytes 6316032 | tf_op jit(solution)/shard_map/jit(_take)/gather | solution.py:59
  64.3 3.9 %all-to-all-start.1 = ((bf16[16,384,256]{2,1,0:T(8,128)(2,1)}), bf16[16,384,256]{2,1,0:T(8,128)(2,1)S(1)}, u32[]{:S(2)}, u32[]{:S(2)}) async-start(bf16[16,384,256]{2,1,0:T(8,128)(2,1)} %broadcast_select_fusion), calls=%async_computation.1 | async-start | bytes 6291456 | tf_op jit(solution)/shard_map/all_to_all | solution.py:60
  74.6 12.3 %all_gather.12 = bf16[1536,256]{1,0:T(8,128)(2,1)} all-gather(bf16[768,256]{1,0:T(8,128)(2,1)S(1)} %get-tuple-element.411), channel_id=1, replica_groups=mesh['sky'=16,'loop'=2] {'loop'}, dimensions={0}, use_global_device_ids=true | all-gather | bytes 1179648 | tf_op jit(solution)/shard_map/all_gather | solution.py:80
  88.2 4.6 %while.33 = (s32[]{:T(128)}, f32[768]{0:T(1024)S(1)}, bf16[3,512,256]{2,1,0:T(8,128)(2,1)}, bf16[768,256]{1,0:T(8,128)(2,1)}, s32[]{:T(128)}, /*index=5*/s32[]{:T(128)}) while((s32[]{:T(128)}, f32[768]{0:T(1024)S(1)}, bf16[3,512,256]{2,1,0:T(8,128)(2,1)}, bf16[768,256]{1,0:T(8,128)(2,1)}, s32[]{:T(128)}, /*index=5*/s32[]{:T(128)}) %tuple.76), condition=%wide.region_4.5_spmd.clone, body=%wide.region_2.4_spmd.clone.sunk | while | flops 202113792 | bytes 667739 | solution.py:30
  92.8 34.7 %all-to-all-done.1 = bf16[16,384,256]{2,1,0:T(8,128)(2,1)S(1)} async-done(((bf16[16,384,256]{2,1,0:T(8,128)(2,1)}), bf16[16,384,256]{2,1,0:T(8,128)(2,1)S(1)}, u32[]{:S(2)}, u32[]{:S(2)}) %all-to-all-start.1) | async-done | bytes 3145760 | tf_op jit(solution)/shard_map/all_to_all | solution.py:60
  127.5 14.0 %gather_fusion.1 = bf16[3072,256]{1,0:T(8,128)(2,1)} fusion(bf16[6144,256]{1,0:T(8,128)(2,1)S(1)} %bitcast.95, s32[3072]{0:T(1024)} %broadcast_clamp_fusion.1), kind=kCustom, calls=%fused_computation.1 | custom fusion | bytes 3158016 | tf_op jit(solution)/shard_map/jit(_take)/gather | solution.py:63
  144.0 6.5 %fusion.45 = f32[768,1,4]{2,1,0:T(1,128)S(1)} fusion(bf16[768,4,256]{2,1,0:T(4,128)(2,1)S(1)} %gather.15, pred[768,4]{1,0:T(8,128)(4,1)S(1)} %copy-done.13, bf16[768,256,1]{1,0,2:T(8,128)(2,1)S(1)} %bitcast.101), kind=kOutput, calls=%fused_computation.54 | convolution fusion | flops 2359296 | bytes 1981440 | tf_op jit(solution)/shard_map/apd,ad->ap/dot_general | solution.py:71
  152.2 21.7 %scatter_custom_fusion.1 = bf16[6144]{0:T(1024)(128)(2,1)S(1)} fusion(s32[3072]{0:T(1024)} %bitcast.112, bf16[3072]{0:T(1024)(128)(2,1)S(1)} %reshape.231, bf16[]{:T(256)} %constant.95.clone.1), kind=kCustom, calls=%fused_computation.95 | custom fusion | bytes 12800 | tf_op jit(solution)/shard_map/scatter | solution.py:134
  175.8 15.5 %all-to-all-start.2 = ((bf16[16,2,192]{2,1,0:T(2,128)(2,1)}), bf16[16,2,192]{2,1,0:T(2,128)(2,1)}, u32[]{:S(2)}, u32[]{:S(2)}) async-start(bf16[16,2,192]{2,1,0:T(2,128)(2,1)} %reshape.271), calls=%async_computation.2 | async-start | bytes 32768 | tf_op jit(solution)/shard_map/all_to_all | solution.py:144
  192.1 15.9 %scatter_custom_fusion.2 = bf16[6144,256]{1,0:T(8,128)(2,1)} fusion(s32[3072]{0:T(1024)} %bitcast.113, bf16[3072,256]{1,0:T(8,128)(2,1)S(1)} %reshape.239, bf16[]{:T(256)} %constant.95.clone.1), kind=kCustom, calls=%fused_computation.50 | custom fusion | bytes 3146240 | tf_op jit(solution)/shard_map/scatter | solution.py:69
  208.0 6.0 %all-to-all-start.3 = ((bf16[16,384,256]{2,1,0:T(8,128)(2,1)}), bf16[16,384,256]{2,1,0:T(8,128)(2,1)S(1)}, u32[]{:S(2)}, u32[]{:S(2)}) async-start(bf16[16,384,256]{2,1,0:T(8,128)(2,1)} %bitcast.17), calls=%async_computation.3 | async-start | bytes 6291456 | tf_op jit(solution)/shard_map/all_to_all | solution.py:137
  214.5 14.1 %all_gather.13 = bf16[1536,256]{1,0:T(8,128)(2,1)} all-gather(bf16[768,256]{1,0:T(8,128)(2,1)} %get-tuple-element.445), channel_id=1, replica_groups=mesh['sky'=16,'loop'=2] {'loop'}, dimensions={0}, use_global_device_ids=true | all-gather | bytes 1179648 | tf_op jit(solution)/shard_map/all_gather | solution.py:129
  228.6 4.4 %all-gather = f32[2,1,768]{2,1,0:T(1,128)} all-gather(f32[1,1,768]{2,1,0:T(1,128)S(1)} %reshape.252), channel_id=1, replica_groups=mesh['sky'=16,'loop'=2] {'loop'}, dimensions={0}, use_global_device_ids=true | all-gather | bytes 9216 | tf_op jit(solution)/shard_map/all_gather | solution.py:111
  235.6 4.4 %all-gather.1 = f32[2,1,768]{2,1,0:T(1,128)} all-gather(f32[1,1,768]{2,1,0:T(1,128)S(1)} %reshape.254), channel_id=1, replica_groups=mesh['sky'=16,'loop'=2] {'loop'}, dimensions={0}, use_global_device_ids=true | all-gather | bytes 9216 | tf_op jit(solution)/shard_map/all_gather | solution.py:112
  244.0 5.3 %fusion.44 = f32[768,1,256]{2,1,0:T(1,128)} fusion(bf16[768,4,256]{2,1,0:T(4,128)(2,1)} %copy-done.9, pred[768,4]{1,0:T(8,128)(4,1)} %copy.21, bf16[768,4,1]{1,0,2:T(8,128)(2,1)S(1)} %fusion.70), kind=kOutput, calls=%fused_computation.53 | convolution fusion | flops 2359296 | bytes 2368512 | tf_op jit(solution)/shard_map/ap,apd->ad/dot_general | solution.py:105
  249.3 17.1 %while.34 = (s32[]{:T(128)}, f32[768,256]{1,0:T(8,128)}, bf16[3,512,256]{2,1,0:T(8,128)(2,1)}, bf16[768,256]{1,0:T(8,128)(2,1)}, f32[768]{0:T(1024)S(1)}, /*inde...) while((s32[]{:T(128)}, f32[768,256]{1,0:T(8,128)}, ...), condition=%wide.region_13.14_spmd.clone, body=%wide.region_12.13_spmd.clone.sunk | while | flops 405406976 | bytes 2508426 | solution.py:30
  257.3 3.3 fusion.86
  263.1 3.3 fusion.86
  269.7 25.2 %while.35 = (s32[]{:T(128)}, f32[768,256]{1,0:T(8,128)}, bf16[3,512,256]{2,1,0:T(8,128)(2,1)}, bf16[768,256]{1,0:T(8,128)(2,1)S(1)}, s32[3]{0:T(128)}, /*index=5...) while((s32[]{:T(128)}, f32[768,256]{1,0:T(8,128)}, ...), condition=%wide.region_16.17_spmd.clone, body=%wide.region_15.16_spmd.clone.sunk | while | flops 405406976 | bytes 2514620 | solution.py:30
  296.3 42.2 %scatter_custom_fusion.3 = f32[768,256]{1,0:T(8,128)} fusion(f32[768,256]{1,0:T(8,128)} %get-tuple-element.111, s32[6144]{0:T(1024)} %bitcast.106, bf16[6144,256]{1,0:T(8,128)(2,1)S(1)} %bitcast.97, f32[6144]{0:T(1024)} %bitcast.108), kind=kCustom, calls=%fused_computation.47 | custom fusion | flops 4718592 | bytes 3956736 | tf_op jit(solution)/shard_map/scatter-add | solution.py:150
  (135 shorter events, 73.9 us)
Async XLA Ops:
  1.3 7.2 %copy-start.21 = (s32[768,4]{0,1:T(4,128)S(1)}, s32[768,4]{0,1:T(4,128)}, u32[]{:S(2)}) copy-start(s32[768,4]{0,1:T(4,128)} %param.14) | copy-start | bytes 36868
  2.7 26.2 %copy-start.2 = (bf16[768,256]{1,0:T(8,128)(2,1)S(1)}, bf16[768,256]{1,0:T(8,128)(2,1)}, u32[]{:S(2)}) copy-start(bf16[768,256]{1,0:T(8,128)(2,1)} %param.11) | copy-start | bytes 1179652
  2.9 26.2 %copy-start = (bf16[768,256]{1,0:T(8,128)(2,1)S(1)}, bf16[768,256]{1,0:T(8,128)(2,1)}, u32[]{:S(2)}) copy-start(bf16[768,256]{1,0:T(8,128)(2,1)} %param.12) | copy-start | bytes 1179652
  9.0 20.2 %copy-start.12 = (s32[3072]{0:T(1024)}, s32[3072]{0:T(1024)S(1)}, u32[]{:S(2)}) copy-start(s32[3072]{0:T(1024)S(1)} %fusion.55) | copy-start | bytes 36868
  9.1 12.4 %copy-start.19 = (s32[3072,1]{0,1:T(1,128)}, s32[3072,1]{0,1:T(1,128)S(1)}, u32[]{:S(2)}) copy-start(s32[3072,1]{0,1:T(1,128)S(1)} %compare_select_fusion.1) | copy-start | bytes 36868
  21.4 14.0 %all-to-all-start = ((s32[16,1,384]{2,1,0:T(1,128)}), s32[16,1,384]{2,1,0:T(1,128)S(1)}, u32[]{:S(2)}, u32[]{:S(2)}) async-start(s32[16,1,384]{2,1,0:T(1,128)} %bitcast.4), calls=%async_computation | async-start | bytes 49152 | tf_op jit(solution)/shard_map/all_to_all | solution.py:55
  35.4 0.6 copy-start.10
  64.3 7.5 %copy-start.11 = (s32[768,4]{0,1:T(4,128)S(1)}, s32[768,4]{0,1:T(4,128)}, u32[]{:S(2)}) copy-start(s32[768,4]{0,1:T(4,128)} %param.13) | copy-start | bytes 36868
  64.3 63.2 %all-to-all-start.1 = ((bf16[16,384,256]{2,1,0:T(8,128)(2,1)}), bf16[16,384,256]{2,1,0:T(8,128)(2,1)S(1)}, u32[]{:S(2)}, u32[]{:S(2)}) async-start(bf16[16,384,256]{2,1,0:T(8,128)(2,1)} %broadcast_select_fusion), calls=%async_computation.1 | async-start | bytes 6291456 | tf_op jit(solution)/shard_map/all_to_all | solution.py:60
  141.5 2.4 copy-start.5
  141.5 2.4 copy-start.13
  143.9 6.6 %copy-start.9 = (bf16[768,4,256]{2,1,0:T(4,128)(2,1)}, bf16[768,4,256]{2,1,0:T(4,128)(2,1)S(1)}, u32[]{:S(2)}) copy-start(bf16[768,4,256]{2,1,0:T(4,128)(2,1)S(1)} %gather.15) | copy-start | bytes 4718596
  143.9 6.6 %copy-start.18 = (s32[768]{0:T(1024)S(1)}, s32[768]{0:T(1024)}, u32[]{:S(2)}) copy-start(s32[768]{0:T(1024)} %param.15) | copy-start | bytes 9220
  143.9 7.0 %copy-start.20 = (f32[768]{0:T(1024)S(1)}, f32[768]{0:T(1024)}, u32[]{:S(2)}) copy-start(f32[768]{0:T(1024)} %get-tuple-element.231) | copy-start | bytes 9220
  150.5 1.0 copy-start.4
  175.8 32.2 %all-to-all-start.2 = ((bf16[16,2,192]{2,1,0:T(2,128)(2,1)}), bf16[16,2,192]{2,1,0:T(2,128)(2,1)}, u32[]{:S(2)}, u32[]{:S(2)}) async-start(bf16[16,2,192]{2,1,0:T(2,128)(2,1)} %reshape.271), calls=%async_computation.2 | async-start | bytes 32768 | tf_op jit(solution)/shard_map/all_to_all | solution.py:144
  208.0 88.3 %all-to-all-start.3 = ((bf16[16,384,256]{2,1,0:T(8,128)(2,1)}), bf16[16,384,256]{2,1,0:T(8,128)(2,1)S(1)}, u32[]{:S(2)}, u32[]{:S(2)}) async-start(bf16[16,384,256]{2,1,0:T(8,128)(2,1)} %bitcast.17), calls=%async_computation.3 | async-start | bytes 6291456 | tf_op jit(solution)/shard_map/all_to_all | solution.py:137
  249.3 17.1 %copy-start.17 = (f32[768]{0:T(1024)S(1)}, f32[768]{0:T(1024)}, u32[]{:S(2)}) copy-start(f32[768]{0:T(1024)} %copy-done.16) | copy-start | bytes 9220
  266.4 2.0 copy-start.3
  266.4 2.0 copy-start.7
  266.4 2.1 copy-start.8
  296.3 42.2 %copy-start.1 = (bf16[768,256]{1,0:T(8,128)(2,1)S(1)}, bf16[768,256]{1,0:T(8,128)(2,1)}, u32[]{:S(2)}) copy-start(bf16[768,256]{1,0:T(8,128)(2,1)} %param.12) | copy-start | bytes 1179652
  296.3 42.2 %copy-start.15 = (f32[768]{0:T(1024)S(1)}, f32[768]{0:T(1024)}, u32[]{:S(2)}) copy-start(f32[768]{0:T(1024)} %copy-done.14) | copy-start | bytes 9220
  338.5 1.6 copy-start.6
  (2 other events, 1.2 us)
where the time goes:
time: 345 us; the launch traced here: 341 us
  local copies, waits for them, and re-layouts  117 us (34%)
  other arithmetic  75.5 us (22%)
  waiting for transfers between devices  38.6 us (11%)
  blocking collectives  35.2 us (10%)
  matrix products  35.2 us (10%)
  starting transfers between devices  32.7 us (9%)
  loops' own time  5.97 us (2%)
    scatter-add x1, other arithmetic, shards(): jax.ops.segment_sum(back_weights.astype(jnp.float32)[:, None] * back_rows...  42.2 us
    all_to_all x1, waiting for transfers between devices, shards(): lax.all_to_all(replies.reshape(sky_count, bucket, width), 'sky', split_ax...  34.7 us
    gather x1, local copies, waits for them, and re-layouts, shards(): replies = jnp.take(key_rows, wanted, axis=0)  24.7 us
    scatter x1, local copies, waits for them, and re-layouts, shards(): slot_weights = jnp.zeros((sky_count * bucket,), jnp.bfloat16).at[slot_ind...  21.7 us
    gather x2, local copies, waits for them, and re-layouts, shards(): jnp.take(answered.reshape(-1, width), slot_index, axis=0)  16.4 us
    scatter x1, local copies, waits for them, and re-layouts, shards(): outgoing = jnp.zeros((sky_count * bucket, width), jnp.bfloat16).at[slot_i...  15.9 us
    all_to_all x1, starting transfers between devices, shards(): lax.all_to_all(slot_weights.reshape(sky_count, bucket), 'sky', split_axis...  15.5 us
    all_gather x1, blocking collectives, shards(): lax.all_gather(query_rows, 'loop', axis=0, tiled=True)  14.1 us
  transfers between devices with their start and end apart: 4, of which 2 were waited for; matrix products, arithmetic and copies ran while one was open for 25% of the time, Pallas kernels for 0%

commit v1 on v0

v1 whole, which is shorter than its diff:
```python
import functools

import jax
import jax.numpy as jnp
import numpy as np
from jax import lax
from jax.experimental import pallas as pl
from jax.experimental.pallas import tpu as pltpu
from jax.sharding import PartitionSpec as P

SCALE = 10.0
EPS = 1e-06
F32 = jnp.float32
BF16 = jnp.bfloat16
VMEM_BYTES = 40 * 1024 * 1024


def chip_ring(chips):
    width = 2 if chips <= 8 else 4
    if chips % width or (chips // width) % 2:
        return list(range(chips))
    height = chips // width
    order = []
    for row in range(height):
        columns = range(1, width) if row % 2 == 0 else range(width - 1, 0, -1)
        order += [row * width + column for column in columns]
    order += [row * width for row in range(height - 1, -1, -1)]
    return order


def call(kernel, outs, operands, flops, smem=(), aliases=None):
    moved = sum(x.size * x.dtype.itemsize for x in operands)
    moved += sum(int(np.prod(o.shape)) * o.dtype.itemsize for o in outs)
    specs = [
        pl.BlockSpec(memory_space=pltpu.SMEM if i in smem else pltpu.VMEM)
        for i in range(len(operands))
    ]
    return pl.pallas_call(
        kernel,
        out_shape=list(outs),
        in_specs=specs,
        out_specs=[pl.BlockSpec(memory_space=pltpu.VMEM)] * len(outs),
        compiler_params=pltpu.CompilerParams(vmem_limit_bytes=VMEM_BYTES),
        cost_estimate=pl.CostEstimate(
            flops=int(flops), bytes_accessed=int(moved), transcendentals=0
        ),
    )(*operands)


def shape(dims, dtype=F32):
    return jax.ShapeDtypeStruct(dims, dtype)


def unit_of(rows):
    wide = rows.astype(F32)
    norms = jnp.sqrt(jnp.sum(wide * wide, axis=1, keepdims=True) + EPS)
    return wide / norms, norms


def back_unit(unit, norms, grad):
    return (grad - unit * jnp.sum(unit * grad, axis=1, keepdims=True)) / norms


def dot_t(a, b):
    return lax.dot_general(a, b, (((1,), (1,)), ((), ())), preferred_element_type=F32)


def dot(a, b):
    return jnp.dot(a, b, preferred_element_type=F32)


def row_ids(rows, columns, offset=0):
    return (lax.broadcasted_iota(jnp.int32, (rows, columns), 0) + offset).astype(F32)


def column_ids(rows, columns, offset=0):
    return (lax.broadcasted_iota(jnp.int32, (rows, columns), 1) + offset).astype(F32)


def unit_kernel(x_ref, whole_ref, first_ref, second_ref):
    unit = unit_of(x_ref[...])[0].astype(BF16)
    half = first_ref.shape[0]
    whole_ref[...] = unit
    first_ref[...] = unit[:half]
    second_ref[...] = unit[half:]


def codes_kernel(me_ref, table_ref, owner_ref, row_ref, count_ref, codes_ref, inverse_ref):
    slots = owner_ref.shape[0]
    count = count_ref[...]
    inverse_ref[...] = 1.0 / (1.0 + count.astype(F32))
    me = me_ref[0]
    for place in range(codes_ref.shape[0]):
        owner = table_ref[me, place]
        code = jnp.full(count.shape, -1, jnp.int32)
        for slot in range(slots):
            here = (owner_ref[slot : slot + 1, :] == owner) & (slot < count)
            code = jnp.where(here, row_ref[slot : slot + 1, :], code)
        codes_ref[place : place + 1, :] = code.astype(F32)


def group_forward_kernel(me_ref, q_ref, keys_ref, total_ref, diag_ref):
    anchors = q_ref.shape[0]
    blocks = keys_ref.shape[0] // anchors
    step = 256
    for start in range(0, anchors, step):
        q = q_ref[start : start + step, :]
        total = jnp.zeros((1, step), F32)
        diag = jnp.zeros((1, step), F32)
        same = row_ids(anchors, step) == column_ids(anchors, step, start)
        for block in range(blocks):
            scores = SCALE * dot_t(keys_ref[block * anchors : (block + 1) * anchors, :], q)
            total += jnp.sum(jnp.exp(scores), axis=0, keepdims=True)
            own = jnp.sum(jnp.where(same, scores, 0.0), axis=0, keepdims=True)
            diag = jnp.where(me_ref[0] == block, own, diag)
        total_ref[:, start : start + step] = total
        diag_ref[:, start : start + step] = diag


def logits_kernel(places, *refs):
    pieces = refs[: len(places)]
    q_ref, s_ref, own_ref, sib_ref, out_ref = refs[len(places) :]
    anchors = q_ref.shape[0]
    step = 256
    order = sorted(set(place for place, _ in places))
    for side, (rows_ref, code_ref) in enumerate(((q_ref, own_ref), (s_ref, sib_ref))):
        for start in range(0, anchors, step):
            q = rows_ref[start : start + step, :]
            for slot, place in enumerate(order):
                code = code_ref[place : place + 1, start : start + step]
                total = jnp.zeros((1, step), F32)
                for (where, offset), piece in zip(places, pieces):
                    if where != place:
                        continue
                    number = piece.shape[0]
                    scores = dot_t(piece[...], q)
                    hit = row_ids(number, step) == code - offset
                    total += jnp.sum(jnp.where(hit, scores, 0.0), axis=0, keepdims=True)
                begin = side * anchors + start
                out_ref[slot : slot + 1, begin : begin + step] = SCALE * total


def totals_kernel(counts, *refs):
    parts = refs[: len(counts)]
    own_ref, sib_ref, group_ref, logits_ref, payload_ref = refs[len(counts) :]
    chips = sib_ref.shape[0]
    anchors = own_ref.shape[1]
    partial = jnp.zeros((1, anchors), F32)
    for part, places in zip(parts, counts):
        for slot, place in enumerate(places):
            logit = part[slot : slot + 1, :anchors]
            logits_ref[place : place + 1, :] = part[slot : slot + 1, :]
            payload_ref[place : place + 1, :] = part[slot : slot + 1, anchors:]
            live = own_ref[place : place + 1, :] >= 0
            partial += jnp.where(live, jnp.exp(logit), 0.0)
    payload_ref[chips : chips + 1, :] = partial + group_ref[...]


def weights_kernel(
    logits_ref,
    payload_ref,
    other_ref,
    own_ref,
    sib_ref,
    inv_ref,
    inv_sib_ref,
    diag_ref,
    loss_ref,
    log_ref,
    weights_ref,
    columns_ref,
    sib_columns_ref,
):
    chips, anchors = sib_ref.shape
    total = payload_ref[chips : chips + 1, :]
    sib_total = other_ref[chips : chips + 1, :]
    chosen = jnp.zeros((1, anchors), F32)
    for place in range(chips):
        here = other_ref[place : place + 1, :]
        live = own_ref[chips + place : chips + place + 1, :] >= 0
        total += jnp.where(live, jnp.exp(here), 0.0)
        chosen += jnp.where(live, here, 0.0)
        live = own_ref[place : place + 1, :] >= 0
        chosen += jnp.where(live, logits_ref[place : place + 1, :anchors], 0.0)
        live = sib_ref[place : place + 1, :] >= 0
        sib_total += jnp.where(live, jnp.exp(logits_ref[place : place + 1, anchors:]), 0.0)
    log_total = jnp.log(total)
    sib_log = jnp.log(sib_total)
    inverse = inv_ref[...]
    loss_ref[...] = log_total - inverse * (diag_ref[...] + chosen)
    log_ref[...] = log_total
    sib_rows = []
    for place in range(chips):
        near = jnp.exp(logits_ref[place : place + 1, :anchors] - log_total) - inverse
        far = jnp.exp(other_ref[place : place + 1, :] - log_total) - inverse
        near = jnp.where(own_ref[place : place + 1, :] >= 0, near, 0.0)
        far = jnp.where(own_ref[chips + place : chips + place + 1, :] >= 0, far, 0.0)
        weights_ref[place : place + 1, :] = near
        weights_ref[chips + place : chips + place + 1, :] = far
        sib = jnp.exp(logits_ref[place : place + 1, anchors:] - sib_log) - inv_sib_ref[...]
        sib_rows.append(jnp.where(sib_ref[place : place + 1, :] >= 0, sib, 0.0))
    own = jnp.concatenate(
        [own_ref[:chips, :], weights_ref[:chips, :], log_total, inverse, jnp.zeros((6, anchors), F32)],
        axis=0,
    )
    columns_ref[...] = own.T
    sib_columns_ref[...] = jnp.concatenate([sib_ref[...]] + sib_rows, axis=0).T


def grad_query_kernel(places, *refs):
    pieces = refs[: len(places)]
    me_ref, q_ref, keys_ref, columns_ref, sib_columns_ref, own_ref, sib_ref = refs[len(places) :]
    anchors = q_ref.shape[0]
    blocks = keys_ref.shape[0] // anchors
    chips = sib_columns_ref.shape[1] // 2
    step = 256

    def partner(columns):
        total = jnp.zeros((step, q_ref.shape[1]), F32)
        for (place, offset), piece in zip(places, pieces):
            number = piece.shape[0]
            code = columns[:, place : place + 1] - offset
            weight = columns[:, chips + place : chips + place + 1]
            spread = jnp.where(code == column_ids(step, number), weight, 0.0).astype(BF16)
            total += dot(spread, piece[...])
        return total

    def turn(index, unused):
        start = pl.multiple_of(index * step, step)
        rows = pl.ds(start, step)
        sib_ref[rows, :] = partner(sib_columns_ref[rows, :])
        columns = columns_ref[rows, :]
        total = partner(columns)
        q = q_ref[rows, :]
        log_total = columns[:, 2 * chips : 2 * chips + 1]
        inverse = columns[:, 2 * chips + 1 : 2 * chips + 2]
        same = row_ids(step, anchors, start) == column_ids(step, anchors)
        for block in range(blocks):
            keys = keys_ref[block * anchors : (block + 1) * anchors, :]
            here = jnp.where(me_ref[0] == block, inverse, 0.0)
            scores = SCALE * dot_t(q, keys)
            weights = jnp.exp(scores - log_total) - jnp.where(same, here, 0.0)
            total += dot(weights.astype(BF16), keys)
        own_ref[rows, :] = total
        return unused

    lax.fori_loop(0, anchors // step, turn, 0)


def finish_kernel(x_ref, own_ref, other_ref, out_ref):
    unit, norms = unit_of(x_ref[...])
    out_ref[...] = back_unit(unit, norms, SCALE * (own_ref[...] + other_ref[...]))


def group_key_kernel(me_ref, k_ref, queries_ref, log_ref, inv_ref, out_ref):
    anchors = k_ref.shape[0]
    blocks = queries_ref.shape[0] // anchors
    step = 256

    def turn(index, unused):
        start = pl.multiple_of(index * step, step)
        rows = pl.ds(start, step)
        total = jnp.zeros((step, k_ref.shape[1]), F32)
        same = row_ids(step, anchors, start) == column_ids(step, anchors)
        for block in range(blocks):
            q = queries_ref[block * anchors : (block + 1) * anchors, :]
            here = jnp.where(me_ref[0] == block, inv_ref[...], 0.0)
            scores = SCALE * dot_t(k_ref[rows, :], q)
            weights = jnp.exp(scores - log_ref[block]) - jnp.where(same, here, 0.0)
            total += dot(weights.astype(BF16), q)
        out_ref[rows, :] = total
        return unused

    lax.fori_loop(0, anchors // step, turn, 0)


def grad_key_kernel(places, carried, *refs):
    pieces = refs[: len(places)]
    rest = refs[len(places) :]
    message_ref = rest[0]
    so_far = rest[1 : 1 + carried]
    own_ref, sib_ref = rest[1 + carried :]
    anchors = own_ref.shape[0]
    step = 256

    def turn(index, unused):
        start = pl.multiple_of(index * step, step)
        rows = pl.ds(start, step)
        for side, out in ((0, own_ref), (1, sib_ref)):
            if side < carried:
                total = so_far[side][rows, :]
            else:
                total = jnp.zeros((step, out.shape[1]), F32)
            for (place, offset), piece in zip(places, pieces):
                number = piece.shape[0]
                code = message_ref[place, side : side + 1, offset : offset + number]
                weight = message_ref[place, 2 + side : 3 + side, offset : offset + number]
                spread = jnp.where(row_ids(step, number, start) == code, weight, 0.0)
                total += dot(spread.astype(BF16), piece[...])
            out[rows, :] = total
        return unused

    lax.fori_loop(0, anchors // step, turn, 0)


def shards(queries, keys, partner_owner, partner_row, partner_count):
    anchors, width = queries.shape
    sky = lax.axis_size("sky")
    loop = lax.axis_size("loop")
    chips = sky // 2
    half = anchors // 2
    order = chip_ring(chips)
    position = {chip: place for place, chip in enumerate(order)}
    table = np.zeros((sky, sky), np.int32)
    for device in range(sky):
        for place in range(chips):
            chip = order[(position[device // 2] - place) % chips]
            table[device, place] = chip * 2 + device % 2
            table[device, chips + place] = chip * 2 + 1 - device % 2
    siblings = [(i, i ^ 1) for i in range(sky)]

    def around(x, shift):
        pairs = []
        for place, chip in enumerate(order):
            other = order[(place + shift) % chips]
            pairs += [(chip * 2 + core, other * 2 + core) for core in range(2)]
        return lax.ppermute(x, "sky", pairs)

    def swap(x):
        return lax.ppermute(x, "sky", siblings)

    def ring(first, second):
        got = {0: [(0, first), (half, second)]}
        right, left = [first, second], [first, second]
        for step in range(1, chips // 2):
            right = [around(x, 1) for x in right]
            left = [around(x, -1) for x in left]
            got[step] = [(0, right[0]), (half, right[1])]
            got[chips - step] = [(0, left[0]), (half, left[1])]
        got[chips // 2] = [(0, around(right[0], 1)), (half, around(left[1], -1))]
        return got

    me = lax.axis_index("sky").reshape(1).astype(jnp.int32)
    place_in_loop = lax.axis_index("loop").reshape(1).astype(jnp.int32)
    block = [shape((anchors, width), BF16), shape((half, width), BF16), shape((half, width), BF16)]
    key_rows, key_a, key_b = call(unit_kernel, block, [keys], 5 * keys.size)
    query_rows, query_a, query_b = call(unit_kernel, block, [queries], 5 * queries.size)
    key_pieces = ring(key_a, key_b)
    query_pieces = ring(query_a, query_b)
    codes, inverse = call(
        codes_kernel,
        [shape((sky, anchors)), shape((1, anchors))],
        [me, jnp.asarray(table), partner_owner.T, partner_row.T, partner_count.reshape(1, anchors)],
        1e6,
        smem=(0, 1),
    )
    sib_queries = swap(query_rows)
    sib_codes = swap(jnp.concatenate([codes[chips:], inverse], axis=0))
    sib_codes, sib_inverse = sib_codes[:chips], sib_codes[chips:]
    group_keys = lax.all_gather(key_rows, "loop", axis=0, tiled=True)
    group_queries = lax.all_gather(query_rows, "loop", axis=0, tiled=True)
    one_block = 2 * anchors * anchors * width
    group_total, diag = call(
        group_forward_kernel,
        [shape((1, anchors))] * 2,
        [place_in_loop, query_rows, group_keys],
        loop * one_block,
        smem=(0,),
    )

    batches = [[0]] + [[s, chips - s] for s in range(1, chips // 2)] + [[chips // 2]]
    batches = [sorted(b) for b in batches]
    parts = []
    for batch in batches:
        places = [(place, offset) for place in batch for offset, _ in key_pieces[place]]
        pieces = [piece for place in batch for _, piece in key_pieces[place]]
        (part,) = call(
            functools.partial(logits_kernel, places),
            [shape((len(batch), 2 * anchors))],
            pieces + [query_rows, sib_queries, codes, sib_codes],
            2 * len(batch) * one_block,
        )
        parts.append(part)
    logits, payload = call(
        functools.partial(totals_kernel, batches),
        [shape((chips, 2 * anchors)), shape((chips + 1, anchors))],
        parts + [codes, sib_codes, group_total],
        1e6,
    )
    other = swap(payload)
    loss, log_total, weights, columns, sib_columns = call(
        weights_kernel,
        [
            shape((1, anchors)),
            shape((1, anchors)),
            shape((sky, anchors)),
            shape((anchors, 2 * chips + 8)),
            shape((anchors, 2 * chips)),
        ],
        [logits, payload, other, codes, sib_codes, inverse, sib_inverse, diag],
        1e6,
    )
    all_log = lax.all_gather(log_total, "loop", axis=0)

    message = jnp.concatenate([codes, weights], axis=0).reshape(4, chips, anchors).transpose(1, 0, 2)
    chip = me[0] // 2
    place_of = jnp.asarray(np.array([position[c] for c in range(chips)], np.int32))
    to_place = (place_of[chip] - place_of) % chips
    from_chip = jnp.asarray(table)[me[0], :chips] // 2
    groups = [[c * 2 + core for c in range(chips)] for core in range(2)]
    arrived = lax.all_to_all(
        jnp.take(message, to_place, axis=0),
        "sky",
        split_axis=0,
        concat_axis=0,
        axis_index_groups=groups,
        tiled=True,
    )
    messages = jnp.take(arrived, from_chip, axis=0)

    places = [(place, offset) for place in range(chips) for offset, _ in key_pieces[place]]
    pieces = [piece for place in range(chips) for _, piece in key_pieces[place]]
    summed_q, sib_summed_q = call(
        functools.partial(grad_query_kernel, places),
        [shape((anchors, width))] * 2,
        pieces + [place_in_loop, query_rows, group_keys, columns, sib_columns],
        (2 * chips + 2 * loop) * one_block,
        smem=(len(pieces),),
    )
    (grad_queries,) = call(
        finish_kernel,
        [shape((anchors, width))],
        [queries, summed_q, swap(sib_summed_q)],
        1e6,
    )
    (group_k,) = call(
        group_key_kernel,
        [shape((anchors, width))],
        [place_in_loop, key_rows, group_queries, all_log, inverse],
        2 * loop * one_block,
        smem=(0,),
    )
    summed_k = [group_k]
    early = [p for p in range(chips) if min(p, chips - p) < chips // 2 - 1]
    late = [p for p in range(chips) if p not in early]
    for batch in (early, late):
        places = [(place, offset) for place in batch for offset, _ in query_pieces[place]]
        pieces = [piece for place in batch for _, piece in query_pieces[place]]
        summed_k = call(
            functools.partial(grad_key_kernel, places, len(summed_k)),
            [shape((anchors, width))] * 2,
            pieces + [messages] + list(summed_k),
            2 * len(batch) * one_block,
        )
    (grad_keys,) = call(
        finish_kernel,
        [shape((anchors, width))],
        [keys, summed_k[0], swap(summed_k[1])],
        1e6,
    )
    return (loss.reshape(anchors), grad_queries, grad_keys)


def solution(mesh):
    in_specs = (
        P(("sky", "loop"), None),
        P(("sky", "loop"), None),
        P(("sky", "loop"), None),
        P(("sky", "loop"), None),
        P(("sky", "loop")),
    )
    out_specs = (P(("sky", "loop")), P(("sky", "loop"), None), P(("sky", "loop"), None))
    return jax.shard_map(shards, mesh=mesh, in_specs=in_specs, out_specs=out_specs, check_vma=False)
```

time: 345 us -> 131 us (0.38)
  local copies, waits for them, and re-layouts: 117 us -> 19 us
  other arithmetic: 75.5 us -> 2.7 us
  Pallas kernels: 0 us -> 39.9 us
  matrix products: 35.2 us -> 0 us
  waiting for transfers between devices: 38.6 us -> 4.88 us
  blocking collectives: 35.2 us -> 23.8 us
  starting transfers between devices: 32.7 us -> 38.7 us
  loops' own time: 5.97 us -> 0 us
    scatter x3 -> x0, local copies, waits for them, and re-layouts: 50 us -> none  [the longest x1 21.7 us: shards(): slot_weights = jnp.zeros((sky_count * bucket,), jnp.bfloat16).at[slot_ind...]
    scatter-add x1 -> x0, other arithmetic: 42.2 us -> none  [shards(): jax.ops.segment_sum(back_weights.astype(jnp.float32)[:, None] * back_rows...]
    pallas_call x0 -> x17, Pallas kernels: none -> 39.9 us  [call(): pl.pallas_call(kernel, out_shape=list(outs), in_specs=specs, out_specs=[p...]
    gather x3 -> x2, local copies, waits for them, and re-layouts: 41 us -> 2.15 us  [the longest x1 1.55 us: shards(): messages = jnp.take(arrived, from_chip, axis=0)]
    all_to_all x4 -> x1, waiting for transfers between devices: 38.6 us -> 0.01 us  [shards(): lax.all_to_all(jnp.take(message, to_place, axis=0), 'sky', split_axis=0,...]
    dot_general x11 -> x0, matrix products: 35.2 us -> none  [the longest x3 9.61 us: add_grad(): return summed + jnp.dot(weights, piece, preferred_element_type=jnp.float32)]
    ppermute x0 -> x33, starting transfers between devices: none -> 33.3 us  [the longest x28 32.6 us: around(): return lax.ppermute(x, 'sky', pairs)]
    all_to_all x4 -> x1, starting transfers between devices: 32.7 us -> 5.43 us  [shards(): lax.all_to_all(jnp.take(message, to_place, axis=0), 'sky', split_axis=0,...]
  transfers between devices with their start and end apart: 4 -> 34, of which waited for: 2 -> 6; matrix products, arithmetic and copies ran while one was open for 25% -> 5% of each run, Pallas kernels for 0% -> 29%
where the time goes in v1:
time: 131 us; the launch traced here: 130 us
  Pallas kernels  39.9 us (30%)
  starting transfers between devices  38.7 us (30%)
  blocking collectives  23.8 us (18%)
  local copies, waits for them, and re-layouts  19 us (15%)
  waiting for transfers between devices  4.88 us (4%)
  other arithmetic  2.7 us (2%)
    pallas_call x17, Pallas kernels, call(): pl.pallas_call(kernel, out_shape=list(outs), in_specs=specs, out_specs=[p...  39.9 us
    ppermute x28, starting transfers between devices, around(): return lax.ppermute(x, 'sky', pairs)  32.6 us
    unnamed x86, local copies, waits for them, and re-layouts  15.5 us
    all_gather x1, blocking collectives, shards(): group_queries = lax.all_gather(query_rows, 'loop', axis=0, tiled=True)  10.8 us
    all_gather x1, blocking collectives, shards(): group_keys = lax.all_gather(key_rows, 'loop', axis=0, tiled=True)  8.65 us
    all_to_all x1, starting transfers between devices, shards(): lax.all_to_all(jnp.take(message, to_place, axis=0), 'sky', split_axis=0,...  5.43 us
    ppermute x28, waiting for transfers between devices, around(): return lax.ppermute(x, 'sky', pairs)  4.34 us
    all_gather x1, blocking collectives, shards(): all_log = lax.all_gather(log_total, 'loop', axis=0)  4.32 us
  transfers between devices with their start and end apart: 34, of which 6 were waited for; matrix products, arithmetic and copies ran while one was open for 5% of the time, Pallas kernels for 29%

profile of v1, /device:TPU:0, one launch (start us, length us, event | category | flops | bytes accessed | tf_op | source)
XLA Modules:
  0.0 130.2 jit_solution(15016573543780082014)
XLA Ops:
  1.9 3.0 %collective-permute-start.2 = (bf16[384,256]{1,0:T(8,128)(2,1)S(1)}, bf16[384,256]{1,0:T(8,128)(2,1)}, u32[]{:S(2)}, u32[]{:S(2)}) collective-permute-start(bf16[384,256]{1,0:T(8,128)(2,1)S(1)} %get-tuple-element.27.refs_0_), channel_id=1, source_target_pairs={{4,12},{6,14},{12,20},{14,22},{20,28},{22,30},{28,24},{30,26},{24,... | collective-permute-start | bytes 589832 | tf_op jit(solution)/shard_map/ppermute | solution.py:327
  5.1 1.9 %collective-permute-start.3 = (bf16[384,256]{1,0:T(8,128)(2,1)S(1)}, bf16[384,256]{1,0:T(8,128)(2,1)}, u32[]{:S(2)}, u32[]{:S(2)}) collective-permute-start(bf16[384,256]{1,0:T(8,128)(2,1)S(1)} %get-tuple-element.28.refs_1_), channel_id=1, source_target_pairs={{4,12},{6,14},{12,20},{14,22},{20,28},{22,30},{28,24},{30,26},{24,... | collective-permute-start | bytes 589832 | tf_op jit(solution)/shard_map/ppermute | solution.py:327
  12.1 1.9 %collective-permute-start.18 = (bf16[384,256]{1,0:T(8,128)(2,1)S(1)}, bf16[384,256]{1,0:T(8,128)(2,1)}, u32[]{:S(2)}, u32[]{:S(2)}) collective-permute-start(bf16[384,256]{1,0:T(8,128)(2,1)S(1)} %get-tuple-element.42.refs_0_), channel_id=1, source_target_pairs={{4,12},{6,14},{12,20},{14,22},{20,28},{22,30},{28,24},{30,26},{24,... | collective-permute-start | bytes 589832 | tf_op jit(solution)/shard_map/ppermute | solution.py:327
  14.2 1.7 %collective-permute-start.21 = (bf16[384,256]{1,0:T(8,128)(2,1)S(1)}, bf16[384,256]{1,0:T(8,128)(2,1)S(1)}, u32[]{:S(2)}, u32[]{:S(2)}) collective-permute-start(bf16[384,256]{1,0:T(8,128)(2,1)S(1)} %get-tuple-element.43.refs_1_), channel_id=1, source_target_pairs={{4,12},{6,14},{12,20},{14,22},{20,28},{22,30},{28,24},{30,26},{24,... | collective-permute-start | bytes 589832 | tf_op jit(solution)/shard_map/ppermute | solution.py:327
  15.9 10.8 %all_gather.13.queries_ref = bf16[1536,256]{1,0:T(8,128)(2,1)S(1)} all-gather(bf16[768,256]{1,0:T(8,128)(2,1)S(1)} %get-tuple-element.29.refs_2_.refs_4_.q_ref.refs_17_), channel_id=1, replica_groups=mesh['sky'=16,'loop'=2] {'loop'}, dimensions={0}, use_global_device_ids=true | all-gather | bytes 1179648 | tf_op jit(solution)/shard_map/all_gather | solution.py:361
  30.4 8.6 %all_gather.12.keys_ref.refs_18_ = bf16[1536,256]{1,0:T(8,128)(2,1)S(1)} all-gather(bf16[768,256]{1,0:T(8,128)(2,1)S(1)} %get-tuple-element.32.k_ref), channel_id=1, replica_groups=mesh['sky'=16,'loop'=2] {'loop'}, dimensions={0}, use_global_device_ids=true | all-gather | bytes 1179648 | tf_op jit(solution)/shard_map/all_gather | solution.py:360
  42.6 1.6 %collective-permute-start.10 = (bf16[384,256]{1,0:T(8,128)(2,1)}, bf16[384,256]{1,0:T(8,128)(2,1)}, u32[]{:S(2)}, u32[]{:S(2)}) collective-permute-start(bf16[384,256]{1,0:T(8,128)(2,1)} %collective-permute-done.6.refs_0_.refs_4_), channel_id=1, source_target_pairs={{4,12},{6,14},{12,20},{14,22},{20,28},{22,30},{28,24},{30,26},{24,... | collective-permute-start | bytes 589832 | tf_op jit(solution)/shard_map/ppermute | solution.py:327
  48.7 1.6 %collective-permute-start.11 = (bf16[384,256]{1,0:T(8,128)(2,1)}, bf16[384,256]{1,0:T(8,128)(2,1)S(1)}, u32[]{:S(2)}, u32[]{:S(2)}) collective-permute-start(bf16[384,256]{1,0:T(8,128)(2,1)} %collective-permute-done.7.refs_1_.refs_5_), channel_id=1, source_target_pairs={{4,12},{6,14},{12,20},{14,22},{20,28},{22,30},{28,24},{30,26},{24,... | collective-permute-start | bytes 589832 | tf_op jit(solution)/shard_map/ppermute | solution.py:327
  52.8 2.1 %collective-permute-done.10.refs_0_.refs_6_ = bf16[384,256]{1,0:T(8,128)(2,1)} collective-permute-done((bf16[384,256]{1,0:T(8,128)(2,1)}, bf16[384,256]{1,0:T(8,128)(2,1)}, u32[]{:S(2)}, u32[]{:S(2)}) %collective-permute-start.10) | collective-permute-done | bytes 196640 | tf_op jit(solution)/shard_map/ppermute | solution.py:327
  54.9 1.9 %collective-permute-start.14 = (bf16[384,256]{1,0:T(8,128)(2,1)}, bf16[384,256]{1,0:T(8,128)(2,1)S(1)}, u32[]{:S(2)}, u32[]{:S(2)}) collective-permute-start(bf16[384,256]{1,0:T(8,128)(2,1)} %collective-permute-done.10.refs_0_.refs_6_), channel_id=1, source_target_pairs={{4,12},{6,14},{12,20},{14,22},{20,28},{22,30},{28,24},{30,26},{24,... | collective-permute-start | bytes 589832 | tf_op jit(solution)/shard_map/ppermute | solution.py:327
  56.8 2.6 %shard_map.98.refs_1_ = f32[2,1536]{1,0:T(2,128)S(1)} custom-call(bf16[384,256]{1,0:T(8,128)(2,1)} %collective-permute-done.2.refs_0_.refs_2_, bf16[384,256]{1,0:T(8,128)(2,1)} %collective-permute-done.3.refs_1_.refs_3_, bf16[384,256]{1,0:T(8,128)(2,1)} %collective-permute-done.4.refs_2_.refs_14_, bf16[384,256]{1,0:T(8,128)(2,1)} %collective-permute-done.5.refs_3_.refs_15_, ...), custom_call_target="tpu_custom_call" | custom-call | flops 1207959552 | bytes 1658880 | tf_op jit(solution)/shard_map/pallas_call | solution.py:38
  59.6 2.7 %shard_map.99.refs_2_ = f32[2,1536]{1,0:T(2,128)S(1)} custom-call(bf16[384,256]{1,0:T(8,128)(2,1)} %collective-permute-done.6.refs_0_.refs_4_, bf16[384,256]{1,0:T(8,128)(2,1)} %collective-permute-done.7.refs_1_.refs_5_, bf16[384,256]{1,0:T(8,128)(2,1)} %collective-permute-done.8.refs_2_.refs_12_, bf16[384,256]{1,0:T(8,128)(2,1)} %collective-permute-done.9.refs_3_.refs_13_, ...), custom_call_target="tpu_custom_call" | custom-call | flops 1207959552 | bytes 1658880 | tf_op jit(solution)/shard_map/pallas_call | solution.py:38
  63.3 1.9 %collective-permute-start.22 = (bf16[384,256]{1,0:T(8,128)(2,1)S(1)}, bf16[384,256]{1,0:T(8,128)(2,1)}, u32[]{:S(2)}, u32[]{:S(2)}) collective-permute-start(bf16[384,256]{1,0:T(8,128)(2,1)S(1)} %copy-done.20), channel_id=1, source_target_pairs={{4,12},{6,14},{12,20},{14,22},{20,28},{22,30},{28,24},{30,26},{24,... | collective-permute-start | bytes 589832 | tf_op jit(solution)/shard_map/ppermute | solution.py:327
  65.4 1.9 %collective-permute-start.20 = (bf16[384,256]{1,0:T(8,128)(2,1)}, bf16[384,256]{1,0:T(8,128)(2,1)}, u32[]{:S(2)}, u32[]{:S(2)}) collective-permute-start(bf16[384,256]{1,0:T(8,128)(2,1)} %collective-permute-done.19.refs_4_), channel_id=1, source_target_pairs={{4,12},{6,14},{12,20},{14,22},{20,28},{22,30},{28,24},{30,26},{24,... | collective-permute-start | bytes 589832 | tf_op jit(solution)/shard_map/ppermute | solution.py:327
  67.4 2.5 %shard_map.100.refs_3_ = f32[2,1536]{1,0:T(2,128)S(1)} custom-call(bf16[384,256]{1,0:T(8,128)(2,1)} %collective-permute-done.10.refs_0_.refs_6_, bf16[384,256]{1,0:T(8,128)(2,1)S(1)} %collective-permute-done.11.refs_1_.refs_7_, bf16[384,256]{1,0:T(8,128)(2,1)S(1)} %collective-permute-done.12.refs_2_.refs_10_, ...), custom_call_target="tpu_custom_call" | custom-call | flops 1207959552 | bytes 1658880 | tf_op jit(solution)/shard_map/pallas_call | solution.py:38
  70.9 1.9 %collective-permute-start.23 = (bf16[384,256]{1,0:T(8,128)(2,1)}, bf16[384,256]{1,0:T(8,128)(2,1)}, u32[]{:S(2)}, u32[]{:S(2)}) collective-permute-start(bf16[384,256]{1,0:T(8,128)(2,1)} %collective-permute-done.22.refs_5_), channel_id=1, source_target_pairs={{4,12},{6,14},{12,20},{14,22},{20,28},{22,30},{28,24},{30,26},{24,... | collective-permute-start | bytes 589832 | tf_op jit(solution)/shard_map/ppermute | solution.py:327
  73.0 1.9 %collective-permute-start.24 = (bf16[384,256]{1,0:T(8,128)(2,1)}, bf16[384,256]{1,0:T(8,128)(2,1)}, u32[]{:S(2)}, u32[]{:S(2)}) collective-permute-start(bf16[384,256]{1,0:T(8,128)(2,1)} %collective-permute-done.20.refs_0_), channel_id=1, source_target_pairs={{4,12},{6,14},{12,20},{14,22},{20,28},{22,30},{28,24},{30,26},{24,... | collective-permute-start | bytes 589832 | tf_op jit(solution)/shard_map/ppermute | solution.py:327
  77.5 5.4 %all-to-all-start = ((f32[8,4,768]{2,1,0:T(4,128)}), f32[8,4,768]{2,1,0:T(4,128)}, u32[]{:S(2)}, u32[]{:S(2)}) async-start(f32[8,4,768]{2,1,0:T(4,128)} %broadcast_select_fusion.1), calls=%async_computation | async-start | bytes 196608 | tf_op jit(solution)/shard_map/all_to_all | solution.py:411
  90.5 11.2 %shard_map.105 = (f32[768,256]{1,0:T(8,128)S(1)}, f32[768,256]{1,0:T(8,128)}) custom-call(bf16[384,256]{1,0:T(8,128)(2,1)S(1)} %copy-done.11, bf16[384,256]{1,0:T(8,128)(2,1)S(1)} %copy-done.14, bf16[384,256]{1,0:T(8,128)(2,1)} %collective-permute-done.2.refs_0_.refs_2_, bf16[384,256]{1,0:T(8,128)(2,1)} %collective-permute-done.3.refs_1_.refs_3_, ...), custom_call_target="tpu_custom_call" | custom-call | flops 6039797760 | bytes 6021124 | tf_op jit(solution)/shard_map/pallas_call | solution.py:38
  101.7 4.3 %all-gather.1.log_ref = f32[2,1,768]{2,1,0:T(1,128)S(1)} all-gather(f32[1,1,768]{2,1,0:T(1,128)S(1)} %bitcast.24), channel_id=2, replica_groups=mesh['sky'=16,'loop'=2] {'loop'}, dimensions={0}, use_global_device_ids=true | all-gather | bytes 9216 | tf_op jit(solution)/shard_map/all_gather | solution.py:403
  106.1 2.8 %shard_map.107.refs_11_ = f32[768,256]{1,0:T(8,128)S(1)} custom-call(s32[1]{0:T(128)} %bitcast.3.me_ref.refs_16_, bf16[768,256]{1,0:T(8,128)(2,1)S(1)} %get-tuple-element.32.k_ref, bf16[1536,256]{1,0:T(8,128)(2,1)S(1)} %all_gather.13.queries_ref, f32[2,1,768]{2,1,0:T(1,128)S(1)} %all-gather.1.log_ref, f32[1,768]{1,0:T(1,128)S(1)} %get-tuple-element.31.inv_ref), custom_call_target="tpu_custom_call" | custom-call | flops 1207959552 | bytes 1975300 | tf_op jit(solution)/shard_map/pallas_call | solution.py:38
  109.7 1.5 %gather_fusion.1 = f32[8,4,768]{2,1,0:T(4,128)S(1)} fusion(f32[8,4,768]{2,1,0:T(4,128)} %all-to-all-done, s32[1024]{0:T(1024)S(1)} %pad_clamp_fusion), kind=kCustom, calls=%fused_computation.1.clone | custom fusion | bytes 196640 | tf_op jit(solution)/shard_map/jit(_take)/gather | solution.py:419
  115.3 5.8 %shard_map.108 = (f32[768,256]{1,0:T(8,128)S(1)}, f32[768,256]{1,0:T(8,128)S(1)}) custom-call(bf16[384,256]{1,0:T(8,128)(2,1)S(1)} %copy-done.16, bf16[384,256]{1,0:T(8,128)(2,1)S(1)} %copy-done.18, bf16[384,256]{1,0:T(8,128)(2,1)} %collective-permute-done.18.refs_2_, bf16[384,256]{1,0:T(8,128)(2,1)S(1)} %copy-done.21, ...), custom_call_target="tpu_custom_call" | custom-call | flops 3019898880 | bytes 4423680 | tf_op jit(solution)/shard_map/pallas_call | solution.py:38
  121.1 5.2 %shard_map.109 = (f32[768,256]{1,0:T(8,128)S(1)}, f32[768,256]{1,0:T(8,128)}) custom-call(bf16[384,256]{1,0:T(8,128)(2,1)} %collective-permute-done.20.refs_0_, bf16[384,256]{1,0:T(8,128)(2,1)} %collective-permute-done.23.refs_1_, bf16[384,256]{1,0:T(8,128)(2,1)} %collective-permute-done.24.refs_2_, bf16[384,256]{1,0:T(8,128)(2,1)} %collective-permute-done.28.refs_3_, ...), custom_call_target="tpu_custom_call" | custom-call | flops 1811939328 | bytes 4423680 | tf_op jit(solution)/shard_map/pallas_call | solution.py:38
  (167 shorter events, 42.4 us)
Async XLA Ops:
  1.9 10.1 %collective-permute-start.2 = (bf16[384,256]{1,0:T(8,128)(2,1)S(1)}, bf16[384,256]{1,0:T(8,128)(2,1)}, u32[]{:S(2)}, u32[]{:S(2)}) collective-permute-start(bf16[384,256]{1,0:T(8,128)(2,1)S(1)} %get-tuple-element.27.refs_0_), channel_id=1, source_target_pairs={{4,12},{6,14},{12,20},{14,22},{20,28},{22,30},{28,24},{30,26},{24,... | collective-permute-start | bytes 589832 | tf_op jit(solution)/shard_map/ppermute | solution.py:327
  5.0 21.8 %collective-permute-start.4 = (bf16[384,256]{1,0:T(8,128)(2,1)S(1)}, bf16[384,256]{1,0:T(8,128)(2,1)}, u32[]{:S(2)}, u32[]{:S(2)}) collective-permute-start(bf16[384,256]{1,0:T(8,128)(2,1)S(1)} %get-tuple-element.27.refs_0_), channel_id=1, source_target_pairs={{4,0},{6,2},{12,4},{14,6},{20,12},{22,14},{28,20},{30,22},{24,28},... | collective-permute-start | bytes 589832 | tf_op jit(solution)/shard_map/ppermute | solution.py:327
  7.0 20.2 %collective-permute-start.5 = (bf16[384,256]{1,0:T(8,128)(2,1)S(1)}, bf16[384,256]{1,0:T(8,128)(2,1)}, u32[]{:S(2)}, u32[]{:S(2)}) collective-permute-start(bf16[384,256]{1,0:T(8,128)(2,1)S(1)} %get-tuple-element.28.refs_1_), channel_id=1, source_target_pairs={{4,0},{6,2},{12,4},{14,6},{20,12},{22,14},{28,20},{30,22},{24,28},... | collective-permute-start | bytes 589832 | tf_op jit(solution)/shard_map/ppermute | solution.py:327
  11.5 29.6 %collective-permute-start = (bf16[768,256]{1,0:T(8,128)(2,1)S(1)}, bf16[768,256]{1,0:T(8,128)(2,1)S(1)}, u32[]{:S(2)}, u32[]{:S(2)}) collective-permute-start(bf16[768,256]{1,0:T(8,128)(2,1)S(1)} %get-tuple-element.29.refs_2_.refs_4_.q_ref.refs_17_), channel_id=1, source_target_pairs={{0,2},{2,0},{4,6},{6,4},{8,10},{10,8},{12,14},{14,12},{16,18},{18,... | collective-permute-start | bytes 1179656 | tf_op jit(solution)/shard_map/ppermute | solution.py:330
  12.1 16.3 %collective-permute-start.18 = (bf16[384,256]{1,0:T(8,128)(2,1)S(1)}, bf16[384,256]{1,0:T(8,128)(2,1)}, u32[]{:S(2)}, u32[]{:S(2)}) collective-permute-start(bf16[384,256]{1,0:T(8,128)(2,1)S(1)} %get-tuple-element.42.refs_0_), channel_id=1, source_target_pairs={{4,12},{6,14},{12,20},{14,22},{20,28},{22,30},{28,24},{30,26},{24,... | collective-permute-start | bytes 589832 | tf_op jit(solution)/shard_map/ppermute | solution.py:327
  14.2 15.0 %collective-permute-start.21 = (bf16[384,256]{1,0:T(8,128)(2,1)S(1)}, bf16[384,256]{1,0:T(8,128)(2,1)S(1)}, u32[]{:S(2)}, u32[]{:S(2)}) collective-permute-start(bf16[384,256]{1,0:T(8,128)(2,1)S(1)} %get-tuple-element.43.refs_1_), channel_id=1, source_target_pairs={{4,12},{6,14},{12,20},{14,22},{20,28},{22,30},{28,24},{30,26},{24,... | collective-permute-start | bytes 589832 | tf_op jit(solution)/shard_map/ppermute | solution.py:327
  26.7 12.3 %collective-permute-start.25 = (bf16[384,256]{1,0:T(8,128)(2,1)S(1)}, bf16[384,256]{1,0:T(8,128)(2,1)S(1)}, u32[]{:S(2)}, u32[]{:S(2)}) collective-permute-start(bf16[384,256]{1,0:T(8,128)(2,1)S(1)} %get-tuple-element.43.refs_1_), channel_id=1, source_target_pairs={{4,0},{6,2},{12,4},{14,6},{20,12},{22,14},{28,20},{30,22},{24,28},... | collective-permute-start | bytes 589832 | tf_op jit(solution)/shard_map/ppermute | solution.py:327
  27.2 13.4 %collective-permute-start.29 = (bf16[384,256]{1,0:T(8,128)(2,1)S(1)}, bf16[384,256]{1,0:T(8,128)(2,1)S(1)}, u32[]{:S(2)}, u32[]{:S(2)}) collective-permute-start(bf16[384,256]{1,0:T(8,128)(2,1)S(1)} %get-tuple-element.42.refs_0_), channel_id=1, source_target_pairs={{4,0},{6,2},{12,4},{14,6},{20,12},{22,14},{28,20},{30,22},{24,28},... | collective-permute-start | bytes 589832 | tf_op jit(solution)/shard_map/ppermute | solution.py:327
  28.4 14.2 %collective-permute-start.6 = (bf16[384,256]{1,0:T(8,128)(2,1)}, bf16[384,256]{1,0:T(8,128)(2,1)}, u32[]{:S(2)}, u32[]{:S(2)}) collective-permute-start(bf16[384,256]{1,0:T(8,128)(2,1)} %collective-permute-done.2.refs_0_.refs_2_), channel_id=1, source_target_pairs={{4,12},{6,14},{12,20},{14,22},{20,28},{22,30},{28,24},{30,26},{24,... | collective-permute-start | bytes 589832 | tf_op jit(solution)/shard_map/ppermute | solution.py:327
  29.2 14.9 %collective-permute-start.9 = (bf16[384,256]{1,0:T(8,128)(2,1)}, bf16[384,256]{1,0:T(8,128)(2,1)}, u32[]{:S(2)}, u32[]{:S(2)}) collective-permute-start(bf16[384,256]{1,0:T(8,128)(2,1)} %collective-permute-done.5.refs_3_.refs_15_), channel_id=1, source_target_pairs={{4,0},{6,2},{12,4},{14,6},{20,12},{22,14},{28,20},{30,22},{24,28},... | collective-permute-start | bytes 589832 | tf_op jit(solution)/shard_map/ppermute | solution.py:327
  41.1 10.3 %collective-permute-start.19 = (bf16[384,256]{1,0:T(8,128)(2,1)}, bf16[384,256]{1,0:T(8,128)(2,1)}, u32[]{:S(2)}, u32[]{:S(2)}) collective-permute-start(bf16[384,256]{1,0:T(8,128)(2,1)} %collective-permute-done.18.refs_2_), channel_id=1, source_target_pairs={{4,12},{6,14},{12,20},{14,22},{20,28},{22,30},{28,24},{30,26},{24,... | collective-permute-start | bytes 589832 | tf_op jit(solution)/shard_map/ppermute | solution.py:327
  42.6 12.3 %collective-permute-start.10 = (bf16[384,256]{1,0:T(8,128)(2,1)}, bf16[384,256]{1,0:T(8,128)(2,1)}, u32[]{:S(2)}, u32[]{:S(2)}) collective-permute-start(bf16[384,256]{1,0:T(8,128)(2,1)} %collective-permute-done.6.refs_0_.refs_4_), channel_id=1, source_target_pairs={{4,12},{6,14},{12,20},{14,22},{20,28},{22,30},{28,24},{30,26},{24,... | collective-permute-start | bytes 589832 | tf_op jit(solution)/shard_map/ppermute | solution.py:327
  44.2 15.2 %collective-permute-start.13 = (bf16[384,256]{1,0:T(8,128)(2,1)}, bf16[384,256]{1,0:T(8,128)(2,1)}, u32[]{:S(2)}, u32[]{:S(2)}) collective-permute-start(bf16[384,256]{1,0:T(8,128)(2,1)} %collective-permute-done.9.refs_3_.refs_13_), channel_id=1, source_target_pairs={{4,0},{6,2},{12,4},{14,6},{20,12},{22,14},{28,20},{30,22},{24,28},... | collective-permute-start | bytes 589832 | tf_op jit(solution)/shard_map/ppermute | solution.py:327
  47.2 16.0 %collective-permute-start.26 = (bf16[384,256]{1,0:T(8,128)(2,1)S(1)}, bf16[384,256]{1,0:T(8,128)(2,1)S(1)}, u32[]{:S(2)}, u32[]{:S(2)}) collective-permute-start(bf16[384,256]{1,0:T(8,128)(2,1)S(1)} %copy-done.23), channel_id=1, source_target_pairs={{4,0},{6,2},{12,4},{14,6},{20,12},{22,14},{28,20},{30,22},{24,28},... | collective-permute-start | bytes 589832 | tf_op jit(solution)/shard_map/ppermute | solution.py:327
  48.7 16.4 %collective-permute-start.11 = (bf16[384,256]{1,0:T(8,128)(2,1)}, bf16[384,256]{1,0:T(8,128)(2,1)S(1)}, u32[]{:S(2)}, u32[]{:S(2)}) collective-permute-start(bf16[384,256]{1,0:T(8,128)(2,1)} %collective-permute-done.7.refs_1_.refs_5_), channel_id=1, source_target_pairs={{4,12},{6,14},{12,20},{14,22},{20,28},{22,30},{28,24},{30,26},{24,... | collective-permute-start | bytes 589832 | tf_op jit(solution)/shard_map/ppermute | solution.py:327
  51.4 13.9 %collective-permute-start.12 = (bf16[384,256]{1,0:T(8,128)(2,1)}, bf16[384,256]{1,0:T(8,128)(2,1)S(1)}, u32[]{:S(2)}, u32[]{:S(2)}) collective-permute-start(bf16[384,256]{1,0:T(8,128)(2,1)} %collective-permute-done.8.refs_2_.refs_12_), channel_id=1, source_target_pairs={{4,0},{6,2},{12,4},{14,6},{20,12},{22,14},{28,20},{30,22},{24,28},... | collective-permute-start | bytes 589832 | tf_op jit(solution)/shard_map/ppermute | solution.py:327
  54.9 12.3 %collective-permute-start.14 = (bf16[384,256]{1,0:T(8,128)(2,1)}, bf16[384,256]{1,0:T(8,128)(2,1)S(1)}, u32[]{:S(2)}, u32[]{:S(2)}) collective-permute-start(bf16[384,256]{1,0:T(8,128)(2,1)} %collective-permute-done.10.refs_0_.refs_6_), channel_id=1, source_target_pairs={{4,12},{6,14},{12,20},{14,22},{20,28},{22,30},{28,24},{30,26},{24,... | collective-permute-start | bytes 589832 | tf_op jit(solution)/shard_map/ppermute | solution.py:327
  59.4 10.5 %collective-permute-start.15 = (bf16[384,256]{1,0:T(8,128)(2,1)}, bf16[384,256]{1,0:T(8,128)(2,1)S(1)}, u32[]{:S(2)}, u32[]{:S(2)}) collective-permute-start(bf16[384,256]{1,0:T(8,128)(2,1)} %collective-permute-done.13.refs_3_.refs_11_), channel_id=1, source_target_pairs={{4,0},{6,2},{12,4},{14,6},{20,12},{22,14},{28,20},{30,22},{24,28},... | collective-permute-start | bytes 589832 | tf_op jit(solution)/shard_map/ppermute | solution.py:327
  70.9 50.1 %collective-permute-start.23 = (bf16[384,256]{1,0:T(8,128)(2,1)}, bf16[384,256]{1,0:T(8,128)(2,1)}, u32[]{:S(2)}, u32[]{:S(2)}) collective-permute-start(bf16[384,256]{1,0:T(8,128)(2,1)} %collective-permute-done.22.refs_5_), channel_id=1, source_target_pairs={{4,12},{6,14},{12,20},{14,22},{20,28},{22,30},{28,24},{30,26},{24,... | collective-permute-start | bytes 589832 | tf_op jit(solution)/shard_map/ppermute | solution.py:327
  72.8 48.3 %collective-permute-start.31 = (bf16[384,256]{1,0:T(8,128)(2,1)}, bf16[384,256]{1,0:T(8,128)(2,1)}, u32[]{:S(2)}, u32[]{:S(2)}) collective-permute-start(bf16[384,256]{1,0:T(8,128)(2,1)} %collective-permute-done.30.refs_6_), channel_id=1, source_target_pairs={{4,0},{6,2},{12,4},{14,6},{20,12},{22,14},{28,20},{30,22},{24,28},... | collective-permute-start | bytes 589832 | tf_op jit(solution)/shard_map/ppermute | solution.py:327
  73.0 48.1 %collective-permute-start.24 = (bf16[384,256]{1,0:T(8,128)(2,1)}, bf16[384,256]{1,0:T(8,128)(2,1)}, u32[]{:S(2)}, u32[]{:S(2)}) collective-permute-start(bf16[384,256]{1,0:T(8,128)(2,1)} %collective-permute-done.20.refs_0_), channel_id=1, source_target_pairs={{4,12},{6,14},{12,20},{14,22},{20,28},{22,30},{28,24},{30,26},{24,... | collective-permute-start | bytes 589832 | tf_op jit(solution)/shard_map/ppermute | solution.py:327
  74.9 46.2 %collective-permute-start.28 = (bf16[384,256]{1,0:T(8,128)(2,1)}, bf16[384,256]{1,0:T(8,128)(2,1)}, u32[]{:S(2)}, u32[]{:S(2)}) collective-permute-start(bf16[384,256]{1,0:T(8,128)(2,1)} %collective-permute-done.27.refs_5_), channel_id=1, source_target_pairs={{4,0},{6,2},{12,4},{14,6},{20,12},{22,14},{28,20},{30,22},{24,28},... | collective-permute-start | bytes 589832 | tf_op jit(solution)/shard_map/ppermute | solution.py:327
  77.5 32.2 %all-to-all-start = ((f32[8,4,768]{2,1,0:T(4,128)}), f32[8,4,768]{2,1,0:T(4,128)}, u32[]{:S(2)}, u32[]{:S(2)}) async-start(f32[8,4,768]{2,1,0:T(4,128)} %broadcast_select_fusion.1), calls=%async_computation | async-start | bytes 196608 | tf_op jit(solution)/shard_map/all_to_all | solution.py:411
  101.7 25.2 %collective-permute-start.17 = (f32[768,256]{1,0:T(8,128)}, f32[768,256]{1,0:T(8,128)S(1)}, u32[]{:S(2)}, u32[]{:S(2)}) collective-permute-start(f32[768,256]{1,0:T(8,128)} %get-tuple-element.41), channel_id=1, source_target_pairs={{0,2},{2,0},{4,6},{6,4},{8,10},{10,8},{12,14},{14,12},{16,18},{18,... | collective-permute-start | bytes 2359304 | tf_op jit(solution)/shard_map/ppermute | solution.py:330
  (53 other events, 261.1 us)

commit v2 on v1

v2 whole, which is shorter than its diff:
```python
import functools

import jax
import jax.numpy as jnp
import numpy as np
from jax import lax
from jax.experimental import pallas as pl
from jax.experimental.pallas import tpu as pltpu
from jax.sharding import PartitionSpec as P

SCALE = 10.0
EPS = 1e-06
F32 = jnp.float32
BF16 = jnp.bfloat16
SPARE_BYTES = 6 * 1024 * 1024


def chip_ring(chips):
    width = 2 if chips <= 8 else 4
    if chips % width or (chips // width) % 2:
        return list(range(chips))
    height = chips // width
    order = []
    for row in range(height):
        columns = range(1, width) if row % 2 == 0 else range(width - 1, 0, -1)
        order += [row * width + column for column in columns]
    order += [row * width for row in range(height - 1, -1, -1)]
    return order


def padded(x):
    dims = (1, 1) + tuple(x.shape)
    size = jnp.dtype(x.dtype).itemsize
    rows = 32 // size
    tile = -(-dims[-2] // rows) * rows * -(-dims[-1] // 128) * 128
    return int(np.prod(dims[:-2])) * tile * size


def call(kernel, outs, operands, flops, smem=()):
    moved = sum(padded(x) for x in list(operands) + list(outs))
    specs = [
        pl.BlockSpec(memory_space=pltpu.SMEM if i in smem else pltpu.VMEM)
        for i in range(len(operands))
    ]
    return pl.pallas_call(
        kernel,
        out_shape=list(outs),
        in_specs=specs,
        out_specs=[pl.BlockSpec(memory_space=pltpu.VMEM)] * len(outs),
        compiler_params=pltpu.CompilerParams(vmem_limit_bytes=moved + SPARE_BYTES),
        cost_estimate=pl.CostEstimate(flops=int(flops), bytes_accessed=moved, transcendentals=0),
    )(*operands)


def shape(dims, dtype=F32):
    return jax.ShapeDtypeStruct(dims, dtype)


def unit_of(rows):
    wide = rows.astype(F32)
    norms = jnp.sqrt(jnp.sum(wide * wide, axis=1, keepdims=True) + EPS)
    return wide / norms, norms


def back_unit(unit, norms, grad):
    return (grad - unit * jnp.sum(unit * grad, axis=1, keepdims=True)) / norms


def dot_t(a, b):
    return lax.dot_general(a, b, (((1,), (1,)), ((), ())), preferred_element_type=F32)


def dot(a, b):
    return jnp.dot(a, b, preferred_element_type=F32)


def row_ids(rows, columns, offset=0):
    return (lax.broadcasted_iota(jnp.int32, (rows, columns), 0) + offset).astype(F32)


def column_ids(rows, columns, offset=0):
    return (lax.broadcasted_iota(jnp.int32, (rows, columns), 1) + offset).astype(F32)


def unit_kernel(x_ref, whole_ref, first_ref, second_ref):
    unit = unit_of(x_ref[...])[0].astype(BF16)
    half = first_ref.shape[0]
    whole_ref[...] = unit
    first_ref[...] = unit[:half]
    second_ref[...] = unit[half:]


def codes_kernel(
    me_ref, table_ref, owner_ref, row_ref, count_ref, codes_ref, inverse_ref, payload_ref
):
    slots = owner_ref.shape[0]
    chips = codes_ref.shape[0] // 2
    count = count_ref[...]
    inverse = 1.0 / (1.0 + count.astype(F32))
    inverse_ref[...] = inverse
    payload_ref[chips : chips + 1, :] = inverse
    me = me_ref[0]
    for place in range(2 * chips):
        owner = table_ref[me, place]
        code = jnp.full(count.shape, -1, jnp.int32)
        for slot in range(slots):
            here = (owner_ref[slot : slot + 1, :] == owner) & (slot < count)
            code = jnp.where(here, row_ref[slot : slot + 1, :], code)
        codes_ref[place : place + 1, :] = code.astype(F32)
        if place >= chips:
            payload_ref[place - chips : place - chips + 1, :] = code.astype(F32)


def group_forward_kernel(blocks, *refs):
    keys = refs[:blocks]
    q_ref, total_ref, diag_ref = refs[blocks:]
    anchors = q_ref.shape[0]
    step = 256
    for start in range(0, anchors, step):
        q = q_ref[start : start + step, :]
        total = jnp.zeros((1, step), F32)
        for block in range(blocks):
            scores = SCALE * dot_t(keys[block][...], q)
            total += jnp.sum(jnp.exp(scores), axis=0, keepdims=True)
            if block == 0:
                same = row_ids(anchors, step) == column_ids(anchors, step, start)
                diag = jnp.sum(jnp.where(same, scores, 0.0), axis=0, keepdims=True)
        total_ref[:, start : start + step] = total
        diag_ref[:, start : start + step] = diag


def joined(refs):
    parts = [ref[...] for ref in refs]
    return parts[0] if len(parts) == 1 else jnp.concatenate(parts, axis=0)


def take_blocks(counts, refs):
    blocks, at = [], 0
    for count in counts:
        blocks.append(refs[at : at + count])
        at += count
    return blocks, refs[at:]


def logits_kernel(places, counts, *refs):
    blocks, rest = take_blocks(counts, refs)
    q_ref, s_ref, own_ref, sib_ref, out_ref = rest
    anchors = q_ref.shape[0]
    step = 256
    for slot, (place, block) in enumerate(zip(places, blocks)):
        keys = joined(block)
        for side, (rows_ref, code_ref) in enumerate(((q_ref, own_ref), (s_ref, sib_ref))):
            for start in range(0, anchors, step):
                code = code_ref[place : place + 1, start : start + step]
                scores = dot_t(keys, rows_ref[start : start + step, :])
                hit = row_ids(anchors, step) == code
                total = jnp.sum(jnp.where(hit, scores, 0.0), axis=0, keepdims=True)
                begin = side * anchors + start
                out_ref[slot : slot + 1, begin : begin + step] = SCALE * total


def totals_kernel(batches, *refs):
    parts = refs[: len(batches)]
    own_ref, group_ref, logits_ref, payload_ref = refs[len(batches) :]
    chips = own_ref.shape[0] // 2
    anchors = own_ref.shape[1]
    partial = jnp.zeros((1, anchors), F32)
    for part, places in zip(parts, batches):
        for slot, place in enumerate(places):
            logit = part[slot : slot + 1, :anchors]
            logits_ref[place : place + 1, :] = part[slot : slot + 1, :]
            payload_ref[place : place + 1, :] = part[slot : slot + 1, anchors:]
            live = own_ref[place : place + 1, :] >= 0
            partial += jnp.where(live, jnp.exp(logit), 0.0)
    payload_ref[chips : chips + 1, :] = partial + group_ref[...]


def weights_kernel(
    me_ref,
    table_ref,
    logits_ref,
    payload_ref,
    other_ref,
    own_ref,
    sib_ref,
    inv_ref,
    diag_ref,
    loss_ref,
    log_ref,
    message_ref,
    columns_ref,
    sib_columns_ref,
):
    chips = sib_ref.shape[0] - 1
    anchors = sib_ref.shape[1]
    me = me_ref[0]
    total = payload_ref[chips : chips + 1, :]
    sib_total = other_ref[chips : chips + 1, :]
    chosen = jnp.zeros((1, anchors), F32)
    for place in range(chips):
        here = other_ref[place : place + 1, :]
        live = own_ref[chips + place : chips + place + 1, :] >= 0
        total += jnp.where(live, jnp.exp(here), 0.0)
        chosen += jnp.where(live, here, 0.0)
        live = own_ref[place : place + 1, :] >= 0
        chosen += jnp.where(live, logits_ref[place : place + 1, :anchors], 0.0)
        live = sib_ref[place : place + 1, :] >= 0
        sib_total += jnp.where(live, jnp.exp(logits_ref[place : place + 1, anchors:]), 0.0)
    log_total = jnp.log(total)
    sib_log = jnp.log(sib_total)
    inverse = inv_ref[...]
    sib_inverse = sib_ref[chips : chips + 1, :]
    loss_ref[...] = log_total - inverse * (diag_ref[...] + chosen)
    log_ref[...] = log_total
    own_rows, sib_rows = [], []
    for place in range(chips):
        chip = table_ref[me, place] // 2
        near_code = own_ref[place : place + 1, :]
        far_code = own_ref[chips + place : chips + place + 1, :]
        sib_code = sib_ref[place : place + 1, :]
        near = jnp.exp(logits_ref[place : place + 1, :anchors] - log_total) - inverse
        far = jnp.exp(other_ref[place : place + 1, :] - log_total) - inverse
        sib = jnp.exp(logits_ref[place : place + 1, anchors:] - sib_log) - sib_inverse
        near = jnp.where(near_code >= 0, near, 0.0)
        far = jnp.where(far_code >= 0, far, 0.0)
        own_rows.append(near)
        sib_rows.append(jnp.where(sib_code >= 0, sib, 0.0))
        message_ref[chip] = jnp.concatenate([near_code, far_code, near, far], axis=0)
    filler = jnp.zeros((6, anchors), F32)
    own = [own_ref[:chips, :]] + own_rows + [log_total, inverse, filler]
    columns_ref[...] = jnp.concatenate(own, axis=0).T
    sib_columns_ref[...] = jnp.concatenate([sib_ref[:chips, :]] + sib_rows, axis=0).T


def grad_query_kernel(counts, groups, *refs):
    blocks, rest = take_blocks(counts, refs)
    group_keys, rest = rest[:groups], rest[groups:]
    q_ref, columns_ref, sib_columns_ref, own_ref, sib_ref = rest
    anchors, width = q_ref.shape
    chips = len(counts)
    step = 256

    def partner(columns):
        total = jnp.zeros((step, width), F32)
        for place, block in enumerate(blocks):
            code = columns[:, place : place + 1]
            weight = columns[:, chips + place : chips + place + 1]
            spread = jnp.where(code == column_ids(step, anchors), weight, 0.0).astype(BF16)
            total += dot(spread, joined(block))
        return total

    for start in range(0, anchors, step):
        rows = slice(start, start + step)
        sib_ref[rows, :] = partner(sib_columns_ref[rows, :])
        columns = columns_ref[rows, :]
        total = partner(columns)
        q = q_ref[rows, :]
        log_total = columns[:, 2 * chips : 2 * chips + 1]
        inverse = columns[:, 2 * chips + 1 : 2 * chips + 2]
        for index, keys in enumerate(group_keys):
            scores = SCALE * dot_t(q, keys[...])
            weights = jnp.exp(scores - log_total)
            if index == 0:
                same = row_ids(step, anchors, start) == column_ids(step, anchors)
                weights -= jnp.where(same, inverse, 0.0)
            total += dot(weights.astype(BF16), keys[...])
        own_ref[rows, :] = total


def finish_kernel(x_ref, own_ref, other_ref, out_ref):
    unit, norms = unit_of(x_ref[...])
    out_ref[...] = back_unit(unit, norms, SCALE * (own_ref[...] + other_ref[...]))


def group_key_kernel(groups, *refs):
    queries, logs = refs[:groups], refs[groups : 2 * groups]
    k_ref, inv_ref, out_ref = refs[2 * groups :]
    anchors, width = k_ref.shape
    step = 256
    for start in range(0, anchors, step):
        rows = slice(start, start + step)
        total = jnp.zeros((step, width), F32)
        for index in range(groups):
            q = queries[index][...]
            scores = SCALE * dot_t(k_ref[rows, :], q)
            weights = jnp.exp(scores - logs[index][...])
            if index == 0:
                same = row_ids(step, anchors, start) == column_ids(step, anchors)
                weights -= jnp.where(same, inv_ref[...], 0.0)
            total += dot(weights.astype(BF16), q)
        out_ref[rows, :] = total


def grad_key_kernel(places, counts, carried, me_ref, table_ref, *refs):
    blocks, rest = take_blocks(counts, refs)
    message_ref = rest[0]
    so_far = rest[1 : 1 + carried]
    outs = rest[1 + carried :]
    anchors, width = outs[0].shape
    step = 256
    chip = [table_ref[me_ref[0], place] // 2 for place in places]
    for side, out in enumerate(outs):
        for start in range(0, anchors, step):
            rows = slice(start, start + step)
            total = so_far[side][rows, :] if side < carried else jnp.zeros((step, width), F32)
            for at, block in zip(chip, blocks):
                code = message_ref[at, side : side + 1, :]
                weight = message_ref[at, 2 + side : 3 + side, :]
                spread = jnp.where(row_ids(step, anchors, start) == code, weight, 0.0)
                total += dot(spread.astype(BF16), joined(block))
            out[rows, :] = total


def shards(queries, keys, partner_owner, partner_row, partner_count):
    anchors, width = queries.shape
    sky = lax.axis_size("sky")
    loop = lax.axis_size("loop")
    chips = sky // 2
    half = anchors // 2
    order = chip_ring(chips)
    position = {chip: place for place, chip in enumerate(order)}
    table = np.zeros((sky, sky), np.int32)
    for device in range(sky):
        for place in range(chips):
            chip = order[(position[device // 2] - place) % chips]
            table[device, place] = chip * 2 + device % 2
            table[device, chips + place] = chip * 2 + 1 - device % 2
    siblings = [(i, i ^ 1) for i in range(sky)]

    def around(x, shift):
        pairs = []
        for place, chip in enumerate(order):
            other = order[(place + shift) % chips]
            pairs += [(chip * 2 + core, other * 2 + core) for core in range(2)]
        return lax.ppermute(x, "sky", pairs)

    def swap(x):
        return lax.ppermute(x, "sky", siblings)

    def ring(first, second):
        got = {0: [first, second]}
        right, left = [first, second], [first, second]
        for step in range(1, chips // 2):
            right = [around(x, 1) for x in right]
            left = [around(x, -1) for x in left]
            got[step] = right
            got[chips - step] = left
        got[chips // 2] = [around(right[0], 1), around(left[1], -1)]
        return got

    def group(x):
        shifts = [[(i, (i + s) % loop) for i in range(loop)] for s in range(1, loop)]
        return [x] + [lax.ppermute(x, "loop", pairs) for pairs in shifts]

    me = lax.axis_index("sky").reshape(1).astype(jnp.int32)
    where = [me, jnp.asarray(table)]
    block = [shape((anchors, width), BF16), shape((half, width), BF16), shape((half, width), BF16)]
    one_block = 2 * anchors * anchors * width
    key_rows, key_a, key_b = call(unit_kernel, block, [keys], 5 * keys.size)
    query_rows, query_a, query_b = call(unit_kernel, block, [queries], 5 * queries.size)
    key_pieces = ring(key_a, key_b)
    key_pieces[0] = [key_rows]
    query_pieces = ring(query_a, query_b)
    query_pieces[0] = [query_rows]
    codes, inverse, for_sibling = call(
        codes_kernel,
        [shape((sky, anchors)), shape((1, anchors)), shape((chips + 1, anchors))],
        where + [partner_owner.T, partner_row.T, partner_count.reshape(1, anchors)],
        1e6,
        smem=(0, 1),
    )
    sib_queries = swap(query_rows)
    sib_codes = swap(for_sibling)
    group_keys = group(key_rows)
    group_queries = group(query_rows)
    group_total, diag = call(
        functools.partial(group_forward_kernel, loop),
        [shape((1, anchors))] * 2,
        group_keys + [query_rows],
        loop * one_block,
    )

    def flat(pieces, places):
        return [piece for place in places for piece in pieces[place]]

    batches = [[0]] + [[s, chips - s] for s in range(1, chips // 2)] + [[chips // 2]]
    parts = []
    for batch in batches:
        counts = [len(key_pieces[place]) for place in batch]
        (part,) = call(
            functools.partial(logits_kernel, batch, counts),
            [shape((len(batch), 2 * anchors))],
            flat(key_pieces, batch) + [query_rows, sib_queries, codes, sib_codes],
            2 * len(batch) * one_block,
        )
        parts.append(part)
    logits, payload = call(
        functools.partial(totals_kernel, batches),
        [shape((chips, 2 * anchors)), shape((chips + 1, anchors))],
        parts + [codes, group_total],
        1e6,
    )
    other = swap(payload)
    loss, log_total, message, columns, sib_columns = call(
        weights_kernel,
        [
            shape((1, anchors)),
            shape((1, anchors)),
            shape((chips, 4, anchors)),
            shape((anchors, 2 * chips + 8)),
            shape((anchors, 2 * chips)),
        ],
        where + [logits, payload, other, codes, sib_codes, inverse, diag],
        1e6,
        smem=(0, 1),
    )
    group_logs = group(log_total)

    groups = [[c * 2 + core for c in range(chips)] for core in range(2)]
    messages = lax.all_to_all(
        message, "sky", split_axis=0, concat_axis=0, axis_index_groups=groups, tiled=True
    )
    counts = [len(key_pieces[place]) for place in range(chips)]
    summed_q, sib_summed_q = call(
        functools.partial(grad_query_kernel, counts, loop),
        [shape((anchors, width))] * 2,
        flat(key_pieces, range(chips)) + group_keys + [query_rows, columns, sib_columns],
        (2 * chips + 2 * loop) * one_block,
    )
    (grad_queries,) = call(
        finish_kernel,
        [shape((anchors, width))],
        [queries, summed_q, swap(sib_summed_q)],
        1e6,
    )
    summed_k = call(
        functools.partial(group_key_kernel, loop),
        [shape((anchors, width))],
        group_queries + group_logs + [key_rows, inverse],
        2 * loop * one_block,
    )
    middle = chips // 2
    near = [p for p in range(chips) if min(p, chips - p) < middle - 1]
    for batch in (near, [middle - 1, middle + 1], [middle]):
        counts = [len(query_pieces[place]) for place in batch]
        summed_k = call(
            functools.partial(grad_key_kernel, batch, counts, len(summed_k)),
            [shape((anchors, width))] * 2,
            where + flat(query_pieces, batch) + [messages] + list(summed_k),
            2 * len(batch) * one_block,
            smem=(0, 1),
        )
    (grad_keys,) = call(
        finish_kernel,
        [shape((anchors, width))],
        [keys, summed_k[0], swap(summed_k[1])],
        1e6,
    )
    return (loss.reshape(anchors), grad_queries, grad_keys)


def solution(mesh):
    in_specs = (
        P(("sky", "loop"), None),
        P(("sky", "loop"), None),
        P(("sky", "loop"), None),
        P(("sky", "loop"), None),
        P(("sky", "loop")),
    )
    out_specs = (P(("sky", "loop")), P(("sky", "loop"), None), P(("sky", "loop"), None))
    return jax.shard_map(shards, mesh=mesh, in_specs=in_specs, out_specs=out_specs, check_vma=False)
```

time: 131 us -> 113 us (0.86)
  blocking collectives: 23.8 us -> 0 us
  waiting for transfers between devices: 4.88 us -> 14 us
  Pallas kernels: 39.9 us -> 31.7 us
  local copies, waits for them, and re-layouts: 19 us -> 22.7 us
  starting transfers between devices: 38.7 us -> 41.5 us
  other arithmetic: 2.7 us -> 0.6 us
    all_gather x3 -> x0, blocking collectives: 23.8 us -> none  [the longest x1 10.8 us: shards(): group_queries = lax.all_gather(query_rows, 'loop', axis=0, tiled=True)]
    ppermute x28, waiting for transfers between devices: 4.34 us -> 13.9 us  [around(): return lax.ppermute(x, 'sky', pairs)]
    pallas_call x17 -> x18, Pallas kernels: 39.9 us -> 31.7 us  [call(): pl.pallas_call(kernel, out_shape=list(outs), in_specs=specs, out_specs=[p...]
    unnamed x86 -> x92, local copies, waits for them, and re-layouts: 15.5 us -> 22 us
    ppermute x0 -> x3, starting transfers between devices: none -> 4.3 us  [group(): return [x] + [lax.ppermute(x, 'loop', pairs) for pairs in shifts]]
    gather x2 -> x0, local copies, waits for them, and re-layouts: 2.15 us -> none  [the longest x1 1.55 us: shards(): messages = jnp.take(arrived, from_chip, axis=0)]
  transfers between devices with their start and end apart: 34 -> 37, of which waited for: 6 -> 10; matrix products, arithmetic and copies ran while one was open for 5% -> 1% of each run, Pallas kernels for 29% -> 27%
where the time goes in v2:
time: 113 us; the launch traced here: 112 us
  starting transfers between devices  41.5 us (37%)
  Pallas kernels  31.7 us (28%)
  local copies, waits for them, and re-layouts  22.7 us (20%)
  waiting for transfers between devices  14 us (12%)
    pallas_call x18, Pallas kernels, call(): pl.pallas_call(kernel, out_shape=list(outs), in_specs=specs, out_specs=[p...  31.7 us
    ppermute x28, starting transfers between devices, around(): return lax.ppermute(x, 'sky', pairs)  31.5 us
    unnamed x92, local copies, waits for them, and re-layouts  22 us
    ppermute x28, waiting for transfers between devices, around(): return lax.ppermute(x, 'sky', pairs)  13.9 us
    all_to_all x1, starting transfers between devices, shards(): lax.all_to_all(message, 'sky', split_axis=0, concat_axis=0, axis_index_gr...  5.01 us
    ppermute x3, starting transfers between devices, group(): return [x] + [lax.ppermute(x, 'loop', pairs) for pairs in shifts]  4.3 us
  transfers between devices with their start and end apart: 37, of which 10 were waited for; matrix products, arithmetic and copies ran while one was open for 1% of the time, Pallas kernels for 27%

profile of v2, /device:TPU:0, one launch (start us, length us, event | category | flops | bytes accessed | tf_op | source)
XLA Modules:
  0.0 111.6 jit_solution(18018889826991961487)
XLA Ops:
  1.9 3.0 %collective-permute-start.2 = (bf16[384,256]{1,0:T(8,128)(2,1)S(1)}, bf16[384,256]{1,0:T(8,128)(2,1)S(1)}, u32[]{:S(2)}, u32[]{:S(2)}) collective-permute-start(bf16[384,256]{1,0:T(8,128)(2,1)S(1)} %get-tuple-element.33), channel_id=1, source_target_pairs={{4,12},{6,14},{12,20},{14,22},{20,28},{22,30},{28,24},{30,26},{24,... | collective-permute-start | bytes 589832 | tf_op jit(solution)/shard_map/ppermute | solution.py:335
  7.3 1.9 %collective-permute-start.3 = (bf16[384,256]{1,0:T(8,128)(2,1)S(1)}, bf16[384,256]{1,0:T(8,128)(2,1)S(1)}, u32[]{:S(2)}, u32[]{:S(2)}) collective-permute-start(bf16[384,256]{1,0:T(8,128)(2,1)S(1)} %get-tuple-element.34), channel_id=1, source_target_pairs={{4,12},{6,14},{12,20},{14,22},{20,28},{22,30},{28,24},{30,26},{24,... | collective-permute-start | bytes 589832 | tf_op jit(solution)/shard_map/ppermute | solution.py:335
  9.9 1.8 %collective-permute-start.19 = (bf16[384,256]{1,0:T(8,128)(2,1)S(1)}, bf16[384,256]{1,0:T(8,128)(2,1)S(1)}, u32[]{:S(2)}, u32[]{:S(2)}) collective-permute-start(bf16[384,256]{1,0:T(8,128)(2,1)S(1)} %get-tuple-element.45), channel_id=1, source_target_pairs={{4,12},{6,14},{12,20},{14,22},{20,28},{22,30},{28,24},{30,26},{24,... | collective-permute-start | bytes 589832 | tf_op jit(solution)/shard_map/ppermute | solution.py:335
  11.6 3.3 %collective-permute-done.3.refs_1_.refs_2_ = bf16[384,256]{1,0:T(8,128)(2,1)S(1)} collective-permute-done((bf16[384,256]{1,0:T(8,128)(2,1)S(1)}, bf16[384,256]{1,0:T(8,128)(2,1)S(1)}, u32[]{:S(2)}, u32[]{:S(2)}) %collective-permute-start.3) | collective-permute-done | bytes 196640 | tf_op jit(solution)/shard_map/ppermute | solution.py:335
  15.0 2.0 %collective-permute-start.23 = (bf16[384,256]{1,0:T(8,128)(2,1)S(1)}, bf16[384,256]{1,0:T(8,128)(2,1)S(1)}, u32[]{:S(2)}, u32[]{:S(2)}) collective-permute-start(bf16[384,256]{1,0:T(8,128)(2,1)S(1)} %get-tuple-element.46), channel_id=1, source_target_pairs={{4,0},{6,2},{12,4},{14,6},{20,12},{22,14},{28,20},{30,22},{24,28},... | collective-permute-start | bytes 589832 | tf_op jit(solution)/shard_map/ppermute | solution.py:335
  19.1 1.6 %collective-permute-start.6 = (bf16[384,256]{1,0:T(8,128)(2,1)S(1)}, bf16[384,256]{1,0:T(8,128)(2,1)S(1)}, u32[]{:S(2)}, u32[]{:S(2)}) collective-permute-start(bf16[384,256]{1,0:T(8,128)(2,1)S(1)} %collective-permute-done.2.refs_0_.refs_1_), channel_id=1, source_target_pairs={{4,12},{6,14},{12,20},{14,22},{20,28},{22,30},{28,24},{30,26},{24,... | collective-permute-start | bytes 589832 | tf_op jit(solution)/shard_map/ppermute | solution.py:335
  21.1 2.2 %collective-permute-done.23.refs_8_ = bf16[384,256]{1,0:T(8,128)(2,1)S(1)} collective-permute-done((bf16[384,256]{1,0:T(8,128)(2,1)S(1)}, bf16[384,256]{1,0:T(8,128)(2,1)S(1)}, u32[]{:S(2)}, u32[]{:S(2)}) %collective-permute-start.23) | collective-permute-done | bytes 196640 | tf_op jit(solution)/shard_map/ppermute | solution.py:335
  23.3 1.6 %collective-permute-start.7 = (bf16[384,256]{1,0:T(8,128)(2,1)S(1)}, bf16[384,256]{1,0:T(8,128)(2,1)S(1)}, u32[]{:S(2)}, u32[]{:S(2)}) collective-permute-start(bf16[384,256]{1,0:T(8,128)(2,1)S(1)} %collective-permute-done.3.refs_1_.refs_2_), channel_id=1, source_target_pairs={{4,12},{6,14},{12,20},{14,22},{20,28},{22,30},{28,24},{30,26},{24,... | collective-permute-start | bytes 589832 | tf_op jit(solution)/shard_map/ppermute | solution.py:335
  25.3 1.6 %collective-permute-start.10 = (bf16[384,256]{1,0:T(8,128)(2,1)S(1)}, bf16[384,256]{1,0:T(8,128)(2,1)S(1)}, u32[]{:S(2)}, u32[]{:S(2)}) collective-permute-start(bf16[384,256]{1,0:T(8,128)(2,1)S(1)} %collective-permute-done.6.refs_0_.refs_3_), channel_id=1, source_target_pairs={{4,12},{6,14},{12,20},{14,22},{20,28},{22,30},{28,24},{30,26},{24,... | collective-permute-start | bytes 589832 | tf_op jit(solution)/shard_map/ppermute | solution.py:335
  29.3 1.9 %collective-permute-done.7.refs_1_.refs_4_ = bf16[384,256]{1,0:T(8,128)(2,1)S(1)} collective-permute-done((bf16[384,256]{1,0:T(8,128)(2,1)S(1)}, bf16[384,256]{1,0:T(8,128)(2,1)S(1)}, u32[]{:S(2)}, u32[]{:S(2)}) %collective-permute-start.7) | collective-permute-done | bytes 196640 | tf_op jit(solution)/shard_map/ppermute | solution.py:335
  31.1 1.6 %collective-permute-start.27 = (bf16[384,256]{1,0:T(8,128)(2,1)S(1)}, bf16[384,256]{1,0:T(8,128)(2,1)S(1)}, u32[]{:S(2)}, u32[]{:S(2)}) collective-permute-start(bf16[384,256]{1,0:T(8,128)(2,1)S(1)} %get-tuple-element.46), channel_id=1, source_target_pairs={{4,12},{6,14},{12,20},{14,22},{20,28},{22,30},{28,24},{30,26},{24,... | collective-permute-start | bytes 589832 | tf_op jit(solution)/shard_map/ppermute | solution.py:335
  32.7 1.6 %collective-permute-start.11 = (bf16[384,256]{1,0:T(8,128)(2,1)S(1)}, bf16[384,256]{1,0:T(8,128)(2,1)S(1)}, u32[]{:S(2)}, u32[]{:S(2)}) collective-permute-start(bf16[384,256]{1,0:T(8,128)(2,1)S(1)} %collective-permute-done.7.refs_1_.refs_4_), channel_id=1, source_target_pairs={{4,12},{6,14},{12,20},{14,22},{20,28},{22,30},{28,24},{30,26},{24,... | collective-permute-start | bytes 589832 | tf_op jit(solution)/shard_map/ppermute | solution.py:335
  41.5 2.3 %collective-permute-done.11.refs_1_.refs_6_ = bf16[384,256]{1,0:T(8,128)(2,1)S(1)} collective-permute-done((bf16[384,256]{1,0:T(8,128)(2,1)S(1)}, bf16[384,256]{1,0:T(8,128)(2,1)S(1)}, u32[]{:S(2)}, u32[]{:S(2)}) %collective-permute-start.11) | collective-permute-done | bytes 196640 | tf_op jit(solution)/shard_map/ppermute | solution.py:335
  43.8 1.6 %collective-permute-start.20 = (bf16[384,256]{1,0:T(8,128)(2,1)S(1)}, bf16[384,256]{1,0:T(8,128)(2,1)}, u32[]{:S(2)}, u32[]{:S(2)}) collective-permute-start(bf16[384,256]{1,0:T(8,128)(2,1)S(1)} %collective-permute-done.19.refs_1_), channel_id=1, source_target_pairs={{4,12},{6,14},{12,20},{14,22},{20,28},{22,30},{28,24},{30,26},{24,... | collective-permute-start | bytes 589832 | tf_op jit(solution)/shard_map/ppermute | solution.py:335
  45.9 2.1 %collective-permute-done.14.refs_0_.refs_7_ = bf16[384,256]{1,0:T(8,128)(2,1)S(1)} collective-permute-done((bf16[384,256]{1,0:T(8,128)(2,1)S(1)}, bf16[384,256]{1,0:T(8,128)(2,1)S(1)}, u32[]{:S(2)}, u32[]{:S(2)}) %collective-permute-start.14) | collective-permute-done | bytes 196640 | tf_op jit(solution)/shard_map/ppermute | solution.py:335
  48.0 1.6 %collective-permute-start.28 = (bf16[384,256]{1,0:T(8,128)(2,1)S(1)}, bf16[384,256]{1,0:T(8,128)(2,1)}, u32[]{:S(2)}, u32[]{:S(2)}) collective-permute-start(bf16[384,256]{1,0:T(8,128)(2,1)S(1)} %collective-permute-done.27.refs_2_), channel_id=1, source_target_pairs={{4,12},{6,14},{12,20},{14,22},{20,28},{22,30},{28,24},{30,26},{24,... | collective-permute-start | bytes 589832 | tf_op jit(solution)/shard_map/ppermute | solution.py:335
  59.0 5.0 %all-to-all-start = ((f32[8,4,768]{2,1,0:T(4,128)}), f32[8,4,768]{2,1,0:T(4,128)S(1)}, u32[]{:S(2)}, u32[]{:S(2)}) async-start(f32[8,4,768]{2,1,0:T(4,128)} %get-tuple-element.47), calls=%async_computation | async-start | bytes 196608 | tf_op jit(solution)/shard_map/all_to_all | solution.py:420
  79.3 7.5 %shard_map.96 = (f32[768,256]{1,0:T(8,128)S(1)}, f32[768,256]{1,0:T(8,128)}) custom-call(bf16[768,256]{1,0:T(8,128)(2,1)S(1)} %get-tuple-element.29.refs_0_.refs_15_.refs_4_, bf16[384,256]{1,0:T(8,128)(2,1)S(1)} %copy-done.15, bf16[384,256]{1,0:T(8,128)(2,1)S(1)} %copy-done.19, bf16[384,256]{1,0:T(8,128)(2,1)S(1)} %copy-done.25, ...), custom_call_target="tpu_custom_call" | custom-call | flops 6039797760 | bytes 6684672 | tf_op jit(solution)/shard_map/pallas_call | solution.py:45
  86.9 2.0 %collective-permute-start.29 = (bf16[384,256]{1,0:T(8,128)(2,1)}, bf16[384,256]{1,0:T(8,128)(2,1)}, u32[]{:S(2)}, u32[]{:S(2)}) collective-permute-start(bf16[384,256]{1,0:T(8,128)(2,1)} %collective-permute-done.28.refs_4_), channel_id=1, source_target_pairs={{4,12},{6,14},{12,20},{14,22},{20,28},{22,30},{28,24},{30,26},{24,... | collective-permute-start | bytes 589832 | tf_op jit(solution)/shard_map/ppermute | solution.py:335
  89.7 2.0 %collective-permute-start.22 = (bf16[384,256]{1,0:T(8,128)(2,1)}, bf16[384,256]{1,0:T(8,128)(2,1)}, u32[]{:S(2)}, u32[]{:S(2)}) collective-permute-start(bf16[384,256]{1,0:T(8,128)(2,1)} %collective-permute-done.21.refs_0_), channel_id=1, source_target_pairs={{4,12},{6,14},{12,20},{14,22},{20,28},{22,30},{28,24},{30,26},{24,... | collective-permute-start | bytes 589832 | tf_op jit(solution)/shard_map/ppermute | solution.py:335
  92.9 1.8 %shard_map.98.refs_10_ = f32[768,256]{1,0:T(8,128)S(1)} custom-call(bf16[768,256]{1,0:T(8,128)(2,1)S(1)} %get-tuple-element.30.refs_1_.refs_4_.refs_2_.refs_17_.refs_0_, bf16[768,256]{1,0:T(8,128)(2,1)S(1)} %copy-done.7, f32[1,768]{1,0:T(1,128)S(1)} %get-tuple-element.48.refs_2_, f32[1,768]{1,0:T(1,128)S(1)} %collective-permute-done.34.refs_3_, ...), custom_call_target="tpu_custom_call" | custom-call | flops 1207959552 | bytes 2039808 | tf_op jit(solution)/shard_map/pallas_call | solution.py:45
  97.7 4.5 %shard_map.99 = (f32[768,256]{1,0:T(8,128)S(1)}, f32[768,256]{1,0:T(8,128)S(1)}) custom-call(s32[1]{0:T(128)} %bitcast.me_ref, s32[16,16]{1,0:T(8,128)S(1)} %copy-done.3, bf16[768,256]{1,0:T(8,128)(2,1)S(1)} %get-tuple-element.30.refs_1_.refs_4_.refs_2_.refs_17_.refs_0_, bf16[384,256]{1,0:T(8,128)(2,1)S(1)} %collective-permute-done.19.refs_1_, ...), custom_call_target="tpu_custom_call" | custom-call | flops 3019898880 | bytes 4534272 | tf_op jit(solution)/shard_map/pallas_call | solution.py:45
  102.2 2.6 %shard_map.100 = (f32[768,256]{1,0:T(8,128)S(1)}, f32[768,256]{1,0:T(8,128)S(1)}) custom-call(s32[1]{0:T(128)} %bitcast.me_ref, s32[16,16]{1,0:T(8,128)S(1)} %copy-done.3, bf16[384,256]{1,0:T(8,128)(2,1)} %collective-permute-done.21.refs_0_, bf16[384,256]{1,0:T(8,128)(2,1)} %collective-permute-done.29.refs_1_, ...), custom_call_target="tpu_custom_call" | custom-call | flops 1207959552 | bytes 4141056 | tf_op jit(solution)/shard_map/pallas_call | solution.py:45
  104.9 2.7 %shard_map.101 = (f32[768,256]{1,0:T(8,128)S(1)}, f32[768,256]{1,0:T(8,128)}) custom-call(s32[1]{0:T(128)} %bitcast.me_ref, s32[16,16]{1,0:T(8,128)S(1)} %copy-done.3, bf16[384,256]{1,0:T(8,128)(2,1)} %collective-permute-done.22.refs_0_, bf16[384,256]{1,0:T(8,128)(2,1)} %collective-permute-done.26.refs_1_, ...), custom_call_target="tpu_custom_call" | custom-call | flops 603979776 | bytes 3747840 | tf_op jit(solution)/shard_map/pallas_call | solution.py:45
  (162 shorter events, 50.8 us)
Async XLA Ops:
  7.1 9.9 %collective-permute-start.4 = (bf16[384,256]{1,0:T(8,128)(2,1)S(1)}, bf16[384,256]{1,0:T(8,128)(2,1)S(1)}, u32[]{:S(2)}, u32[]{:S(2)}) collective-permute-start(bf16[384,256]{1,0:T(8,128)(2,1)S(1)} %get-tuple-element.33), channel_id=1, source_target_pairs={{4,0},{6,2},{12,4},{14,6},{20,12},{22,14},{28,20},{30,22},{24,28},... | collective-permute-start | bytes 589832 | tf_op jit(solution)/shard_map/ppermute | solution.py:335
  9.5 15.4 %collective-permute-start = (bf16[768,256]{1,0:T(8,128)(2,1)S(1)}, bf16[768,256]{1,0:T(8,128)(2,1)S(1)}, u32[]{:S(2)}, u32[]{:S(2)}) collective-permute-start(bf16[768,256]{1,0:T(8,128)(2,1)S(1)} %get-tuple-element.30.refs_1_.refs_4_.refs_2_.refs_17_.refs_0_), channel_id=1, source_target_pairs={{0,2},{2,0},{4,6},{6,4},{8,10},{10,8},{12,14},{14,12},{16,18},{18,... | collective-permute-start | bytes 1179656 | tf_op jit(solution)/shard_map/ppermute | solution.py:338
  9.9 10.8 %collective-permute-start.19 = (bf16[384,256]{1,0:T(8,128)(2,1)S(1)}, bf16[384,256]{1,0:T(8,128)(2,1)S(1)}, u32[]{:S(2)}, u32[]{:S(2)}) collective-permute-start(bf16[384,256]{1,0:T(8,128)(2,1)S(1)} %get-tuple-element.45), channel_id=1, source_target_pairs={{4,12},{6,14},{12,20},{14,22},{20,28},{22,30},{28,24},{30,26},{24,... | collective-permute-start | bytes 589832 | tf_op jit(solution)/shard_map/ppermute | solution.py:335
  17.0 17.3 %collective-permute-start.16 = (bf16[768,256]{1,0:T(8,128)(2,1)S(1)}, bf16[768,256]{1,0:T(8,128)(2,1)S(1)}, u32[]{:S(2)}, u32[]{:S(2)}) collective-permute-start(bf16[768,256]{1,0:T(8,128)(2,1)S(1)} %get-tuple-element.29.refs_0_.refs_15_.refs_4_), channel_id=1, source_target_pairs={{0,1},{1,0},{2,3},{3,2},{4,5},{5,4},{6,7},{7,6},{8,9},{9,8},{10,11... | collective-permute-start | bytes 1179656 | tf_op jit(solution)/shard_map/ppermute | solution.py:353
  25.3 10.0 %collective-permute-start.10 = (bf16[384,256]{1,0:T(8,128)(2,1)S(1)}, bf16[384,256]{1,0:T(8,128)(2,1)S(1)}, u32[]{:S(2)}, u32[]{:S(2)}) collective-permute-start(bf16[384,256]{1,0:T(8,128)(2,1)S(1)} %collective-permute-done.6.refs_0_.refs_3_), channel_id=1, source_target_pairs={{4,12},{6,14},{12,20},{14,22},{20,28},{22,30},{28,24},{30,26},{24,... | collective-permute-start | bytes 589832 | tf_op jit(solution)/shard_map/ppermute | solution.py:335
  27.7 10.8 %collective-permute-start.13 = (bf16[384,256]{1,0:T(8,128)(2,1)S(1)}, bf16[384,256]{1,0:T(8,128)(2,1)S(1)}, u32[]{:S(2)}, u32[]{:S(2)}) collective-permute-start(bf16[384,256]{1,0:T(8,128)(2,1)S(1)} %collective-permute-done.9.refs_3_.refs_12_), channel_id=1, source_target_pairs={{4,0},{6,2},{12,4},{14,6},{20,12},{22,14},{28,20},{30,22},{24,28},... | collective-permute-start | bytes 589832 | tf_op jit(solution)/shard_map/ppermute | solution.py:335
  32.7 11.1 %collective-permute-start.11 = (bf16[384,256]{1,0:T(8,128)(2,1)S(1)}, bf16[384,256]{1,0:T(8,128)(2,1)S(1)}, u32[]{:S(2)}, u32[]{:S(2)}) collective-permute-start(bf16[384,256]{1,0:T(8,128)(2,1)S(1)} %collective-permute-done.7.refs_1_.refs_4_), channel_id=1, source_target_pairs={{4,12},{6,14},{12,20},{14,22},{20,28},{22,30},{28,24},{30,26},{24,... | collective-permute-start | bytes 589832 | tf_op jit(solution)/shard_map/ppermute | solution.py:335
  34.3 11.1 %collective-permute-start.12 = (bf16[384,256]{1,0:T(8,128)(2,1)S(1)}, bf16[384,256]{1,0:T(8,128)(2,1)S(1)}, u32[]{:S(2)}, u32[]{:S(2)}) collective-permute-start(bf16[384,256]{1,0:T(8,128)(2,1)S(1)} %collective-permute-done.8.refs_2_.refs_11_), channel_id=1, source_target_pairs={{4,0},{6,2},{12,4},{14,6},{20,12},{22,14},{28,20},{30,22},{24,28},... | collective-permute-start | bytes 589832 | tf_op jit(solution)/shard_map/ppermute | solution.py:335
  35.4 12.6 %collective-permute-start.14 = (bf16[384,256]{1,0:T(8,128)(2,1)S(1)}, bf16[384,256]{1,0:T(8,128)(2,1)S(1)}, u32[]{:S(2)}, u32[]{:S(2)}) collective-permute-start(bf16[384,256]{1,0:T(8,128)(2,1)S(1)} %collective-permute-done.10.refs_0_.refs_5_), channel_id=1, source_target_pairs={{4,12},{6,14},{12,20},{14,22},{20,28},{22,30},{28,24},{30,26},{24,... | collective-permute-start | bytes 589832 | tf_op jit(solution)/shard_map/ppermute | solution.py:335
  38.4 12.6 %collective-permute-start.15 = (bf16[384,256]{1,0:T(8,128)(2,1)S(1)}, bf16[384,256]{1,0:T(8,128)(2,1)S(1)}, u32[]{:S(2)}, u32[]{:S(2)}) collective-permute-start(bf16[384,256]{1,0:T(8,128)(2,1)S(1)} %collective-permute-done.13.refs_3_.refs_10_), channel_id=1, source_target_pairs={{4,0},{6,2},{12,4},{14,6},{20,12},{22,14},{28,20},{30,22},{24,28},... | collective-permute-start | bytes 589832 | tf_op jit(solution)/shard_map/ppermute | solution.py:335
  40.9 11.1 %collective-permute-start.30 = (bf16[384,256]{1,0:T(8,128)(2,1)S(1)}, bf16[384,256]{1,0:T(8,128)(2,1)}, u32[]{:S(2)}, u32[]{:S(2)}) collective-permute-start(bf16[384,256]{1,0:T(8,128)(2,1)S(1)} %get-tuple-element.45), channel_id=1, source_target_pairs={{4,0},{6,2},{12,4},{14,6},{20,12},{22,14},{28,20},{30,22},{24,28},... | collective-permute-start | bytes 589832 | tf_op jit(solution)/shard_map/ppermute | solution.py:335
  43.8 9.8 %collective-permute-start.20 = (bf16[384,256]{1,0:T(8,128)(2,1)S(1)}, bf16[384,256]{1,0:T(8,128)(2,1)}, u32[]{:S(2)}, u32[]{:S(2)}) collective-permute-start(bf16[384,256]{1,0:T(8,128)(2,1)S(1)} %collective-permute-done.19.refs_1_), channel_id=1, source_target_pairs={{4,12},{6,14},{12,20},{14,22},{20,28},{22,30},{28,24},{30,26},{24,... | collective-permute-start | bytes 589832 | tf_op jit(solution)/shard_map/ppermute | solution.py:335
  48.0 16.0 %collective-permute-start.28 = (bf16[384,256]{1,0:T(8,128)(2,1)S(1)}, bf16[384,256]{1,0:T(8,128)(2,1)}, u32[]{:S(2)}, u32[]{:S(2)}) collective-permute-start(bf16[384,256]{1,0:T(8,128)(2,1)S(1)} %collective-permute-done.27.refs_2_), channel_id=1, source_target_pairs={{4,12},{6,14},{12,20},{14,22},{20,28},{22,30},{28,24},{30,26},{24,... | collective-permute-start | bytes 589832 | tf_op jit(solution)/shard_map/ppermute | solution.py:335
  52.1 36.8 %collective-permute-start.33 = (bf16[768,256]{1,0:T(8,128)(2,1)S(1)}, bf16[768,256]{1,0:T(8,128)(2,1)S(1)}, u32[]{:S(2)}, u32[]{:S(2)}) collective-permute-start(bf16[768,256]{1,0:T(8,128)(2,1)S(1)} %get-tuple-element.30.refs_1_.refs_4_.refs_2_.refs_17_.refs_0_), channel_id=1, source_target_pairs={{0,1},{1,0},{2,3},{3,2},{4,5},{5,4},{6,7},{7,6},{8,9},{9,8},{10,11... | collective-permute-start | bytes 1179656 | tf_op jit(solution)/shard_map/ppermute | solution.py:353
  53.6 33.3 %collective-permute-start.31 = (bf16[384,256]{1,0:T(8,128)(2,1)}, bf16[384,256]{1,0:T(8,128)(2,1)}, u32[]{:S(2)}, u32[]{:S(2)}) collective-permute-start(bf16[384,256]{1,0:T(8,128)(2,1)} %collective-permute-done.30.refs_7_), channel_id=1, source_target_pairs={{4,0},{6,2},{12,4},{14,6},{20,12},{22,14},{28,20},{30,22},{24,28},... | collective-permute-start | bytes 589832 | tf_op jit(solution)/shard_map/ppermute | solution.py:335
  54.1 35.6 %collective-permute-start.21 = (bf16[384,256]{1,0:T(8,128)(2,1)}, bf16[384,256]{1,0:T(8,128)(2,1)}, u32[]{:S(2)}, u32[]{:S(2)}) collective-permute-start(bf16[384,256]{1,0:T(8,128)(2,1)} %collective-permute-done.20.refs_3_), channel_id=1, source_target_pairs={{4,12},{6,14},{12,20},{14,22},{20,28},{22,30},{28,24},{30,26},{24,... | collective-permute-start | bytes 589832 | tf_op jit(solution)/shard_map/ppermute | solution.py:335
  55.7 36.0 %collective-permute-start.25 = (bf16[384,256]{1,0:T(8,128)(2,1)}, bf16[384,256]{1,0:T(8,128)(2,1)}, u32[]{:S(2)}, u32[]{:S(2)}) collective-permute-start(bf16[384,256]{1,0:T(8,128)(2,1)} %collective-permute-done.24.refs_6_), channel_id=1, source_target_pairs={{4,0},{6,2},{12,4},{14,6},{20,12},{22,14},{28,20},{30,22},{24,28},... | collective-permute-start | bytes 589832 | tf_op jit(solution)/shard_map/ppermute | solution.py:335
  59.0 36.6 %all-to-all-start = ((f32[8,4,768]{2,1,0:T(4,128)}), f32[8,4,768]{2,1,0:T(4,128)S(1)}, u32[]{:S(2)}, u32[]{:S(2)}) async-start(f32[8,4,768]{2,1,0:T(4,128)} %get-tuple-element.47), calls=%async_computation | async-start | bytes 196608 | tf_op jit(solution)/shard_map/all_to_all | solution.py:420
  64.0 27.9 %collective-permute-start.34 = (f32[1,768]{1,0:T(1,128)S(1)}, f32[1,768]{1,0:T(1,128)S(1)}, u32[]{:S(2)}, u32[]{:S(2)}) collective-permute-start(f32[1,768]{1,0:T(1,128)S(1)} %get-tuple-element.48.refs_2_), channel_id=1, source_target_pairs={{0,1},{1,0},{2,3},{3,2},{4,5},{5,4},{6,7},{7,6},{8,9},{9,8},{10,11... | collective-permute-start | bytes 9224 | tf_op jit(solution)/shard_map/ppermute | solution.py:353
  86.9 15.3 %collective-permute-start.29 = (bf16[384,256]{1,0:T(8,128)(2,1)}, bf16[384,256]{1,0:T(8,128)(2,1)}, u32[]{:S(2)}, u32[]{:S(2)}) collective-permute-start(bf16[384,256]{1,0:T(8,128)(2,1)} %collective-permute-done.28.refs_4_), channel_id=1, source_target_pairs={{4,12},{6,14},{12,20},{14,22},{20,28},{22,30},{28,24},{30,26},{24,... | collective-permute-start | bytes 589832 | tf_op jit(solution)/shard_map/ppermute | solution.py:335
  89.6 12.6 %collective-permute-start.32 = (bf16[384,256]{1,0:T(8,128)(2,1)}, bf16[384,256]{1,0:T(8,128)(2,1)}, u32[]{:S(2)}, u32[]{:S(2)}) collective-permute-start(bf16[384,256]{1,0:T(8,128)(2,1)} %collective-permute-done.31.refs_5_), channel_id=1, source_target_pairs={{4,0},{6,2},{12,4},{14,6},{20,12},{22,14},{28,20},{30,22},{24,28},... | collective-permute-start | bytes 589832 | tf_op jit(solution)/shard_map/ppermute | solution.py:335
  89.7 15.2 %collective-permute-start.22 = (bf16[384,256]{1,0:T(8,128)(2,1)}, bf16[384,256]{1,0:T(8,128)(2,1)}, u32[]{:S(2)}, u32[]{:S(2)}) collective-permute-start(bf16[384,256]{1,0:T(8,128)(2,1)} %collective-permute-done.21.refs_0_), channel_id=1, source_target_pairs={{4,12},{6,14},{12,20},{14,22},{20,28},{22,30},{28,24},{30,26},{24,... | collective-permute-start | bytes 589832 | tf_op jit(solution)/shard_map/ppermute | solution.py:335
  91.6 13.2 %collective-permute-start.26 = (bf16[384,256]{1,0:T(8,128)(2,1)}, bf16[384,256]{1,0:T(8,128)(2,1)}, u32[]{:S(2)}, u32[]{:S(2)}) collective-permute-start(bf16[384,256]{1,0:T(8,128)(2,1)} %collective-permute-done.25.refs_3_), channel_id=1, source_target_pairs={{4,0},{6,2},{12,4},{14,6},{20,12},{22,14},{28,20},{30,22},{24,28},... | collective-permute-start | bytes 589832 | tf_op jit(solution)/shard_map/ppermute | solution.py:335
  91.9 16.8 %collective-permute-start.18 = (f32[768,256]{1,0:T(8,128)}, f32[768,256]{1,0:T(8,128)S(1)}, u32[]{:S(2)}, u32[]{:S(2)}) collective-permute-start(f32[768,256]{1,0:T(8,128)} %get-tuple-element.44), channel_id=1, source_target_pairs={{0,2},{2,0},{4,6},{6,4},{8,10},{10,8},{12,14},{14,12},{16,18},{18,... | collective-permute-start | bytes 2359304 | tf_op jit(solution)/shard_map/ppermute | solution.py:338
  (59 other events, 298.4 us)

commit v3 on v2

v3 whole, which is shorter than its diff:
```python
import functools

import jax
import jax.numpy as jnp
import numpy as np
from jax import lax
from jax.experimental import pallas as pl
from jax.experimental.pallas import tpu as pltpu
from jax.sharding import PartitionSpec as P

SCALE = 10.0
EPS = 1e-06
F32 = jnp.float32
BF16 = jnp.bfloat16
COST = 1.0
SPARE_BYTES = 6 * 1024 * 1024


def chip_ring(chips):
    width = 2 if chips <= 8 else 4
    if chips % width or (chips // width) % 2:
        return list(range(chips))
    height = chips // width
    order = []
    for row in range(height):
        columns = range(1, width) if row % 2 == 0 else range(width - 1, 0, -1)
        order += [row * width + column for column in columns]
    order += [row * width for row in range(height - 1, -1, -1)]
    return order


def padded(x):
    dims = (1, 1) + tuple(x.shape)
    size = jnp.dtype(x.dtype).itemsize
    rows = 32 // size
    tile = -(-dims[-2] // rows) * rows * -(-dims[-1] // 128) * 128
    return int(np.prod(dims[:-2])) * tile * size


def call(kernel, outs, operands, flops, smem=()):
    moved = sum(padded(x) for x in list(operands) + list(outs))
    specs = [
        pl.BlockSpec(memory_space=pltpu.SMEM if i in smem else pltpu.VMEM)
        for i in range(len(operands))
    ]
    return pl.pallas_call(
        kernel,
        out_shape=list(outs),
        in_specs=specs,
        out_specs=[pl.BlockSpec(memory_space=pltpu.VMEM)] * len(outs),
        compiler_params=pltpu.CompilerParams(vmem_limit_bytes=moved + SPARE_BYTES),
        cost_estimate=pl.CostEstimate(flops=int(flops * COST), bytes_accessed=int(moved * COST), transcendentals=0),
    )(*operands)


def shape(dims, dtype=F32):
    return jax.ShapeDtypeStruct(dims, dtype)


def unit_of(rows):
    wide = rows.astype(F32)
    norms = jnp.sqrt(jnp.sum(wide * wide, axis=1, keepdims=True) + EPS)
    return wide / norms, norms


def back_unit(unit, norms, grad):
    return (grad - unit * jnp.sum(unit * grad, axis=1, keepdims=True)) / norms


def dot_t(a, b):
    return lax.dot_general(a, b, (((1,), (1,)), ((), ())), preferred_element_type=F32)


def dot(a, b):
    return jnp.dot(a, b, preferred_element_type=F32)


def row_ids(rows, columns, offset=0):
    return (lax.broadcasted_iota(jnp.int32, (rows, columns), 0) + offset).astype(F32)


def column_ids(rows, columns, offset=0):
    return (lax.broadcasted_iota(jnp.int32, (rows, columns), 1) + offset).astype(F32)


def unit_kernel(x_ref, unit_ref):
    unit_ref[...] = unit_of(x_ref[...])[0].astype(BF16)


def unit_both_kernel(x_ref, k_ref, unit_ref, both_ref):
    unit_kernel(x_ref, unit_ref)
    rows = x_ref.shape[0]
    both_ref[:rows, :] = k_ref[...]
    both_ref[rows:, :] = unit_ref[...]


def codes_kernel(
    me_ref, table_ref, owner_ref, row_ref, count_ref, codes_ref, inverse_ref, columns_ref
):
    slots = owner_ref.shape[0]
    places = codes_ref.shape[0] - 1
    count = count_ref[...]
    inverse = 1.0 / (1.0 + count.astype(F32))
    inverse_ref[...] = inverse
    codes_ref[places : places + 1, :] = inverse
    me = me_ref[0]
    for place in range(places):
        owner = table_ref[me, place]
        code = jnp.full(count.shape, -1, jnp.int32)
        for slot in range(slots):
            here = (owner_ref[slot : slot + 1, :] == owner) & (slot < count)
            code = jnp.where(here, row_ref[slot : slot + 1, :], code)
        codes_ref[place : place + 1, :] = code.astype(F32)
    columns_ref[...] = codes_ref[...].T


def group_forward_kernel(groups, k_ref, *refs):
    both = refs[: groups - 1]
    q_ref, total_ref, diag_ref = refs[groups - 1 :]
    anchors = q_ref.shape[0]
    step = 256
    for start in range(0, anchors, step):
        q = q_ref[start : start + step, :]
        total = jnp.zeros((1, step), F32)
        for index in range(groups):
            keys = both[index - 1][:anchors, :] if index else k_ref[...]
            scores = SCALE * dot_t(keys, q)
            total += jnp.sum(jnp.exp(scores), axis=0, keepdims=True)
            if index == 0:
                same = row_ids(anchors, step) == column_ids(anchors, step, start)
                diag = jnp.sum(jnp.where(same, scores, 0.0), axis=0, keepdims=True)
        total_ref[:, start : start + step] = total
        diag_ref[:, start : start + step] = diag


def turn_kernel(rows_ref, columns_ref):
    columns_ref[...] = rows_ref[...].T


def partner_kernel(places, *refs):
    blocks = refs[: len(places)]
    q_ref, s_ref, own_ref, sib_ref, keys_ref, logits_ref = refs[len(places) :]
    anchors = q_ref.shape[0]
    step = 256
    chips = own_ref.shape[1] // 2
    for side, (rows_ref, code_ref) in enumerate(((q_ref, own_ref), (s_ref, sib_ref))):
        for start in range(0, anchors, step):
            rows = slice(start, start + step)
            here = slice(side * anchors + start, side * anchors + start + step)
            q = rows_ref[rows, :].astype(F32)
            logits = []
            for slot, (place, block) in enumerate(zip(places, blocks)):
                at = side * chips + place
                code = code_ref[rows, at : at + 1]
                hot = jnp.where(code == column_ids(step, anchors), 1.0, 0.0).astype(BF16)
                named = dot(hot, block[...])
                keys_ref[slot, here, :] = named.astype(BF16)
                logits.append(SCALE * jnp.sum(named * q, axis=1, keepdims=True))
            logits_ref[here, :] = jnp.concatenate(logits, axis=1)


def totals_kernel(*refs):
    parts = refs[:-3]
    group_ref, logits_ref, payload_ref = refs[-3:]
    anchors = group_ref.shape[1]
    turned = jnp.concatenate([part[...] for part in parts], axis=1).T
    chips = turned.shape[0]
    logits_ref[...] = turned
    payload_ref[:chips, :] = turned[:, anchors:]
    payload_ref[chips : 2 * chips, :] = turned[:, :anchors]
    payload_ref[2 * chips :, :] = group_ref[...]


def weights_kernel(
    me_ref,
    table_ref,
    logits_ref,
    other_ref,
    own_ref,
    sib_ref,
    group_ref,
    diag_ref,
    loss_ref,
    log_ref,
    message_ref,
    columns_ref,
    sib_columns_ref,
):
    chips, anchors = logits_ref.shape[0], group_ref.shape[1]
    me = me_ref[0]

    def all_weights(near, far, near_codes, far_codes, group, inverse):
        total, chosen = group, jnp.zeros((1, anchors), F32)
        for logits, codes in ((near, near_codes), (far, far_codes)):
            live = codes >= 0
            total += jnp.sum(jnp.where(live, jnp.exp(logits), 0.0), axis=0, keepdims=True)
            chosen += jnp.sum(jnp.where(live, logits, 0.0), axis=0, keepdims=True)
        log_total = jnp.log(total)
        near, far = (
            jnp.where(codes >= 0, jnp.exp(logits - log_total) - inverse, 0.0)
            for logits, codes in ((near, near_codes), (far, far_codes))
        )
        return log_total, chosen, near, far

    inverse = own_ref[2 * chips :, :]
    near_code, far_code = own_ref[:chips, :], own_ref[chips : 2 * chips, :]
    sib_near_code, sib_far_code = sib_ref[chips : 2 * chips, :], sib_ref[:chips, :]
    log_total, chosen, near, far = all_weights(
        logits_ref[:, :anchors],
        other_ref[:chips, :],
        near_code,
        far_code,
        group_ref[...],
        inverse,
    )
    loss_ref[...] = log_total - inverse * (diag_ref[...] + chosen)
    log_ref[...] = log_total
    unused, unused, sib_near, sib_far = all_weights(
        logits_ref[:, anchors:],
        other_ref[chips : 2 * chips, :],
        sib_near_code,
        sib_far_code,
        other_ref[2 * chips :, :],
        sib_ref[2 * chips :, :],
    )
    filler = jnp.zeros((6, anchors), F32)
    columns_ref[...] = jnp.concatenate([near, log_total, inverse, filler], axis=0).T
    sib_columns_ref[...] = sib_near.T

    def row(x, slot):
        return x[slot : slot + 1, :]

    message_ref[...] = jnp.zeros_like(message_ref)
    for slot in (0, chips - 1):
        there = table_ref[me, 3 * chips + slot]
        rows = [row(near_code, slot), row(far_code, slot), row(near, slot), row(far, slot)]
        message_ref[there, :4, :] = jnp.concatenate(rows, axis=0)
    for slot in range(2, chips - 1, 2):
        there = table_ref[me, 3 * chips + slot]
        rows = []
        for codes, weights in ((far_code, far), (sib_far_code, sib_far)):
            rows += [row(codes, slot), row(codes, slot - 1)]
            rows += [row(weights, slot), row(weights, slot - 1)]
        message_ref[there] = jnp.concatenate(rows, axis=0)


def partner_sum(columns, order, named, rows):
    total = None
    for place, (ref, slot) in zip(order, named):
        weight = columns[:, place : place + 1].astype(BF16).astype(F32)
        term = weight * ref[slot, rows, :].astype(F32)
        total = term if total is None else total + term
    return total


def named_rows(batches, refs):
    named = [(ref, slot) for ref, places in zip(refs, batches) for slot in range(len(places))]
    return [place for places in batches for place in places], named


def grad_sibling_kernel(batches, *refs):
    order, named = named_rows(batches, refs)
    columns_ref, out_ref = refs[len(batches) :]
    anchors = out_ref.shape[0]
    step = 256
    for start in range(0, anchors, step):
        rows = slice(start, start + step)
        far = slice(anchors + start, anchors + start + step)
        out_ref[rows, :] = partner_sum(columns_ref[rows, :], order, named, far)


def grad_query_kernel(batches, groups, *refs):
    order, named = named_rows(batches, refs)
    rest = refs[len(batches) :]
    k_ref, rest = rest[0], rest[1:]
    both, rest = rest[: groups - 1], rest[groups - 1 :]
    q_ref, columns_ref, out_ref = rest
    anchors = q_ref.shape[0]
    chips = len(order)
    step = 256
    for start in range(0, anchors, step):
        rows = slice(start, start + step)
        columns = columns_ref[rows, :]
        total = partner_sum(columns, order, named, rows)
        q = q_ref[rows, :]
        log_total = columns[:, chips : chips + 1]
        inverse = columns[:, chips + 1 : chips + 2]
        for index in range(groups):
            keys = both[index - 1][:anchors, :] if index else k_ref[...]
            scores = SCALE * dot_t(q, keys)
            weights = jnp.exp(scores - log_total)
            if index == 0:
                same = row_ids(step, anchors, start) == column_ids(step, anchors)
                weights -= jnp.where(same, inverse, 0.0)
            total += dot(weights.astype(BF16), keys)
        out_ref[rows, :] = total


def finish_kernel(x_ref, own_ref, other_ref, out_ref):
    unit, norms = unit_of(x_ref[...])
    out_ref[...] = back_unit(unit, norms, SCALE * (own_ref[...] + other_ref[...]))


def group_key_kernel(groups, *refs):
    q_ref, both, logs = refs[0], refs[1:groups], refs[groups : 2 * groups]
    k_ref, inv_ref, out_ref = refs[2 * groups :]
    anchors, width = k_ref.shape
    step = 256
    for start in range(0, anchors, step):
        rows = slice(start, start + step)
        total = jnp.zeros((step, width), F32)
        for index in range(groups):
            q = both[index - 1][anchors:, :] if index else q_ref[...]
            scores = SCALE * dot_t(k_ref[rows, :], q)
            weights = jnp.exp(scores - logs[index][...])
            if index == 0:
                same = row_ids(step, anchors, start) == column_ids(step, anchors)
                weights -= jnp.where(same, inv_ref[...], 0.0)
            total += dot(weights.astype(BF16), q)
        out_ref[rows, :] = total


def grad_key_kernel(places, carried, me_ref, table_ref, *refs):
    blocks, rest = refs[: len(places)], refs[len(places) :]
    message_ref = rest[0]
    so_far = rest[1 : 1 + carried]
    outs = rest[1 + carried :]
    anchors, width = outs[0].shape
    chips = message_ref.shape[0]
    step = 256
    source = [table_ref[me_ref[0], 2 * chips + place] for place in places]
    first = [4 if place % 2 == 0 and place else 0 for place in places]
    for side, out in enumerate(outs):
        for start in range(0, anchors, step):
            rows = slice(start, start + step)
            total = so_far[side][rows, :] if side < carried else jnp.zeros((step, width), F32)
            for at, base, block in zip(source, first, blocks):
                code = message_ref[at, base + side : base + side + 1, :]
                weight = message_ref[at, base + 2 + side : base + 3 + side, :]
                spread = jnp.where(row_ids(step, anchors, start) == code, weight, 0.0)
                total += dot(spread.astype(BF16), block[...])
            out[rows, :] = total


def shards(queries, keys, partner_owner, partner_row, partner_count):
    anchors, width = queries.shape
    sky = lax.axis_size("sky")
    loop = lax.axis_size("loop")
    chips = sky // 2
    middle = chips // 2
    bits = chips.bit_length() - 1
    order = chip_ring(chips)
    position = {chip: place for place, chip in enumerate(order)}

    def handled(device):
        chip, core = divmod(device, 2)
        way = 1 if core else -1
        along = [order[(position[chip] + way * step) % chips] for step in range(middle + 1)]
        owners = [device]
        for step in range(1, middle):
            owners += [2 * along[step] + core, 2 * along[step] + 1 - core]
        return owners + [2 * along[middle] + core]

    table = np.zeros((sky, 4 * chips), np.int32)
    for device in range(sky):
        near, far = handled(device), handled(device ^ 1)
        for slot in range(chips):
            relative = near[slot] // 2 ^ device // 2
            table[device, slot] = near[slot]
            table[device, chips + slot] = far[slot]
            table[device, 2 * chips + slot] = sum(
                (relative >> bit & 1) << (bits - 1 - bit) for bit in range(bits)
            )
            table[device, 3 * chips + slot] = far[slot] // 2 ^ device // 2
    siblings = [(i, i ^ 1) for i in range(sky)]
    onward = []
    for place, chip in enumerate(order):
        onward.append((chip * 2, order[(place + 1) % chips] * 2))
        onward.append((chip * 2 + 1, order[place - 1] * 2 + 1))

    def swap(x):
        return lax.ppermute(x, "sky", siblings)

    def exchange(message):
        held = message[None]
        stages = []
        step = chips // 2
        while step:
            pairs = [(i, i ^ (2 * step)) for i in range(sky)]
            got = lax.ppermute(held[:, step:], "sky", pairs)
            stages.append(got)
            held = jnp.concatenate([held[:, :step], got], axis=0)
            step //= 2
        return stages, held.reshape(message.shape)

    def after(x, *others):
        return lax.optimization_barrier((x,) + others)[0] if others else x

    class Ring:
        def __init__(self, own, sibling):
            self.front = [own, sibling]
            self.blocks = [own]

        def hop(self, which, *pins):
            self.front[which] = lax.ppermute(after(self.front[which], *pins), "sky", onward)
            self.blocks.append(self.front[which])

    def group(x):
        shifts = [[(i, (i + s) % loop) for i in range(loop)] for s in range(1, loop)]
        return [lax.ppermute(x, "loop", pairs) for pairs in shifts]

    me = lax.axis_index("sky").reshape(1).astype(jnp.int32)
    where = [me, jnp.asarray(table)]
    block = shape((anchors, width), BF16)
    one_block = 2 * anchors * anchors * width
    (key_rows,) = call(unit_kernel, [block], [keys], 5 * keys.size)
    key_ring = Ring(key_rows, swap(key_rows))
    key_ring.hop(0)
    query_rows, both = call(
        unit_both_kernel,
        [block, shape((2 * anchors, width), BF16)],
        [queries, key_rows],
        5 * queries.size,
    )
    key_ring.hop(1)
    sib_queries = swap(query_rows)
    query_ring = Ring(query_rows, sib_queries)
    others = group(both)
    codes, inverse, code_columns = call(
        codes_kernel,
        [shape((sky + 1, anchors)), shape((1, anchors)), shape((anchors, sky + 1))],
        where + [partner_owner.T, partner_row.T, partner_count.reshape(1, anchors)],
        1e6,
        smem=(0, 1),
    )
    sib_codes = swap(codes)
    (sib_code_columns,) = call(turn_kernel, [shape((anchors, sky + 1))], [sib_codes], 1e6)

    def partners_of(batch, *pins):
        return call(
            functools.partial(partner_kernel, batch),
            [shape((len(batch), 2 * anchors, width), BF16), shape((2 * anchors, len(batch)))],
            [key_ring.blocks[place] for place in batch]
            + [after(query_rows, *pins), sib_queries, code_columns, sib_code_columns],
            2 * len(batch) * one_block,
        )

    batches = [[0]] + [[2 * s - 1, 2 * s] for s in range(1, middle)] + [[chips - 1]]
    parts = []
    group_total = diag = None
    pins = ()
    for step in range(2, middle + 1):
        incoming = key_ring.front[0]
        key_ring.hop(0, *pins)
        if step == 2:
            parts.append(partners_of(batches[0]))
            pins = (parts[-1][1],)
        elif group_total is None:
            group_total, diag = call(
                functools.partial(group_forward_kernel, loop),
                [shape((1, anchors))] * 2,
                [key_rows] + others + [after(query_rows, *pins)],
                loop * one_block,
            )
            pins = (group_total,)
        if step < middle:
            key_ring.hop(1, *pins)
            parts.append(partners_of(batches[step - 1], *pins))
            pins = (parts[-1][1],)
    query_ring.hop(0, incoming)
    parts.append(partners_of(batches[middle - 1], *pins))
    query_ring.hop(1, parts[-1][1])
    parts.append(partners_of(batches[middle], parts[-1][1]))
    logits, payload = call(
        totals_kernel,
        [shape((chips, 2 * anchors)), shape((2 * chips + 1, anchors))],
        [part[1] for part in parts] + [group_total],
        1e6,
    )
    query_ring.hop(0, logits)
    other = swap(payload)
    loss, log_total, message, columns, sib_columns = call(
        weights_kernel,
        [
            shape((1, anchors)),
            shape((1, anchors)),
            shape((chips, 8, anchors)),
            shape((anchors, chips + 8)),
            shape((anchors, chips)),
        ],
        where + [logits, other, codes, sib_codes, group_total, diag],
        1e6,
        smem=(0, 1),
    )
    stages, messages = exchange(message)
    all_logs = [log_total] + group(log_total)
    query_ring.hop(1, log_total)
    for step in range(3, middle):
        if step < middle - 1:
            query_ring.hop(0)
            query_ring.hop(1)
    (sib_summed_q,) = call(
        functools.partial(grad_sibling_kernel, batches),
        [shape((anchors, width))],
        [part[0] for part in parts] + [sib_columns],
        1e6,
    )
    query_ring.hop(0, sib_summed_q)
    (summed_q,) = call(
        functools.partial(grad_query_kernel, batches, loop),
        [shape((anchors, width))],
        [part[0] for part in parts]
        + [key_rows]
        + others
        + [after(query_rows, stages[0], sib_summed_q), columns],
        2 * loop * one_block,
    )
    query_ring.hop(1, summed_q)
    (group_k,) = call(
        functools.partial(group_key_kernel, loop),
        [shape((anchors, width))],
        [query_rows] + others + all_logs + [after(key_rows, stages[1], summed_q), inverse],
        2 * loop * one_block,
    )
    query_ring.hop(0, group_k)
    (grad_queries,) = call(
        finish_kernel,
        [shape((anchors, width))],
        [queries, summed_q, swap(sib_summed_q)],
        1e6,
    )
    summed_k = [group_k]
    for batch in (range(chips - 3), [chips - 3, chips - 2], [chips - 1]):
        summed_k = call(
            functools.partial(grad_key_kernel, list(batch), len(summed_k)),
            [shape((anchors, width))] * 2,
            where + [query_ring.blocks[p] for p in batch] + [messages] + list(summed_k),
            2 * len(batch) * one_block,
            smem=(0, 1),
        )
    (grad_keys,) = call(
        finish_kernel,
        [shape((anchors, width))],
        [keys, summed_k[0], swap(summed_k[1])],
        1e6,
    )
    return (loss.reshape(anchors), grad_queries, grad_keys)


def solution(mesh):
    in_specs = (
        P(("sky", "loop"), None),
        P(("sky", "loop"), None),
        P(("sky", "loop"), None),
        P(("sky", "loop"), None),
        P(("sky", "loop")),
    )
    out_specs = (P(("sky", "loop")), P(("sky", "loop"), None), P(("sky", "loop"), None))
    return jax.shard_map(shards, mesh=mesh, in_specs=in_specs, out_specs=out_specs, check_vma=False)
```

time: 113 us -> 88.4 us (0.78)
  local copies, waits for them, and re-layouts: 22.7 us -> 2.95 us
  starting transfers between devices: 41.5 us -> 33 us
  waiting for transfers between devices: 14 us -> 16.8 us
  Pallas kernels: 31.7 us -> 33.6 us
    unnamed x92 -> x24, local copies, waits for them, and re-layouts: 22 us -> 2.92 us
    all_to_all x1 -> x0, starting transfers between devices: 5.01 us -> none  [shards(): lax.all_to_all(message, 'sky', split_axis=0, concat_axis=0, axis_index_gr...]
    ppermute x31 -> x19, starting transfers between devices: 35.8 us -> 32 us  [the longest x14 23.8 us: hop(): lax.ppermute(after(self.front[which], *pins), 'sky', onward)]
    pallas_call x18 -> x20, Pallas kernels: 31.7 us -> 33.6 us  [call(): pl.pallas_call(kernel, out_shape=list(outs), in_specs=specs, out_specs=[p...]
    ppermute x5 -> x6, waiting for transfers between devices: 0.16 us -> 1.91 us  [swap(): return lax.ppermute(x, 'sky', siblings)]
    ppermute x31 -> x19, waiting for transfers between devices: 13.9 us -> 14.9 us  [the longest x3 8 us: exchange(): got = lax.ppermute(held[:, step:], 'sky', pairs)]
  transfers between devices with their start and end apart: 37 -> 25, of which waited for: 10 -> 10; matrix products, arithmetic and copies ran while one was open for 1% -> 1% of each run, Pallas kernels for 27% -> 35%
where the time goes in v3:
time: 88.4 us; the launch traced here: 88 us
  Pallas kernels  33.6 us (38%)
  starting transfers between devices  33 us (37%)
  waiting for transfers between devices  16.8 us (19%)
  local copies, waits for them, and re-layouts  2.95 us (3%)
  between operations  0.96 us (1%)
    pallas_call x20, Pallas kernels, call(): pl.pallas_call(kernel, out_shape=list(outs), in_specs=specs, out_specs=[p...  33.6 us
    ppermute x14, starting transfers between devices, hop(): lax.ppermute(after(self.front[which], *pins), 'sky', onward)  23.8 us
    ppermute x3, waiting for transfers between devices, exchange(): got = lax.ppermute(held[:, step:], 'sky', pairs)  8 us
    ppermute x3, starting transfers between devices, exchange(): got = lax.ppermute(held[:, step:], 'sky', pairs)  5.18 us
    ppermute x14, waiting for transfers between devices, hop(): lax.ppermute(after(self.front[which], *pins), 'sky', onward)  3.93 us
    ppermute x2, starting transfers between devices, group(): return [lax.ppermute(x, 'loop', pairs) for pairs in shifts]  2.97 us
    ppermute x2, waiting for transfers between devices, group(): return [lax.ppermute(x, 'loop', pairs) for pairs in shifts]  2.95 us
    unnamed x24, local copies, waits for them, and re-layouts  2.92 us
  transfers between devices with their start and end apart: 25, of which 10 were waited for; matrix products, arithmetic and copies ran while one was open for 1% of the time, Pallas kernels for 35%

profile of v3, /device:TPU:0, one launch (start us, length us, event | category | flops | bytes accessed | tf_op | source)
XLA Modules:
  0.0 88.0 jit_solution(4165689182665529754)
XLA Ops:
  2.4 2.6 %collective-permute-start.2 = (bf16[768,256]{1,0:T(8,128)(2,1)S(1)}, bf16[768,256]{1,0:T(8,128)(2,1)}, u32[]{:S(2)}, u32[]{:S(2)}) collective-permute-start(bf16[768,256]{1,0:T(8,128)(2,1)S(1)} %shard_map.85.k_ref.refs_0_.refs_5_.refs_4_), channel_id=1, source_target_pairs={{4,12},{6,2},{12,20},{14,6},{20,28},{22,14},{28,24},{30,22},{24,16... | collective-permute-start | bytes 1179656 | tf_op jit(solution)/shard_map/ppermute | solution.py:405
  10.9 2.0 %collective-permute-start.5 = (bf16[768,256]{1,0:T(8,128)(2,1)}, bf16[768,256]{1,0:T(8,128)(2,1)}, u32[]{:S(2)}, u32[]{:S(2)}) collective-permute-start(bf16[768,256]{1,0:T(8,128)(2,1)} %collective-permute-done.2.refs_0_), channel_id=1, source_target_pairs={{4,12},{6,2},{12,20},{14,6},{20,28},{22,14},{28,24},{30,22},{24,16... | collective-permute-start | bytes 1179656 | tf_op jit(solution)/shard_map/ppermute | solution.py:405
  15.3 1.9 %shard_map.89 = (bf16[1,1536,256]{2,1,0:T(8,128)(2,1)S(1)}, f32[1536,1]{1,0:T(8,128)S(1)}) custom-call(bf16[768,256]{1,0:T(8,128)(2,1)S(1)} %shard_map.85.k_ref.refs_0_.refs_5_.refs_4_, bf16[768,256]{1,0:T(8,128)(2,1)S(1)} %get-tuple-element.83.refs_1_.refs_2_.refs_7_.refs_0_, bf16[768,256]{1,0:T(8,128)(2,1)} %collective-permute-done.refs_2_.refs_3_, ...), custom_call_target="tpu_custom_call" | custom-call | flops 603979776 | bytes 3538944 | tf_op jit(solution)/shard_map/pallas_call | solution.py:46
  18.8 2.8 %shard_map.90 = (bf16[2,1536,256]{2,1,0:T(8,128)(2,1)S(1)}, f32[1536,2]{1,0:T(8,128)S(1)}) custom-call(bf16[768,256]{1,0:T(8,128)(2,1)} %collective-permute-done.2.refs_0_, bf16[768,256]{1,0:T(8,128)(2,1)} %collective-permute-done.4.refs_1_, bf16[768,256]{1,0:T(8,128)(2,1)S(1)} %get-tuple-element.83.refs_1_.refs_2_.refs_7_.refs_0_, ...), custom_call_target="tpu_custom_call" | custom-call | flops 1207959552 | bytes 4718592 | tf_op jit(solution)/shard_map/pallas_call | solution.py:46
  21.7 1.6 %collective-permute-start.8 = (bf16[768,256]{1,0:T(8,128)(2,1)}, bf16[768,256]{1,0:T(8,128)(2,1)S(1)}, u32[]{:S(2)}, u32[]{:S(2)}) collective-permute-start(bf16[768,256]{1,0:T(8,128)(2,1)} %collective-permute-done.5.refs_0_), channel_id=1, source_target_pairs={{4,12},{6,2},{12,20},{14,6},{20,28},{22,14},{28,24},{30,22},{24,16... | collective-permute-start | bytes 1179656 | tf_op jit(solution)/shard_map/ppermute | solution.py:405
  23.3 3.0 %collective-permute-done.7.refs_0_.refs_6_.refs_1_ = bf16[1536,256]{1,0:T(8,128)(2,1)S(1)} collective-permute-done((bf16[1536,256]{1,0:T(8,128)(2,1)S(1)}, bf16[1536,256]{1,0:T(8,128)(2,1)S(1)}, u32[]{:S(2)}, u32[]{:S(2)}) %collective-permute-start.7) | collective-permute-done | bytes 786464 | tf_op jit(solution)/shard_map/ppermute | solution.py:410
  27.4 1.6 %collective-permute-start.9 = (bf16[768,256]{1,0:T(8,128)(2,1)S(1)}, bf16[768,256]{1,0:T(8,128)(2,1)S(1)}, u32[]{:S(2)}, u32[]{:S(2)}) collective-permute-start(bf16[768,256]{1,0:T(8,128)(2,1)S(1)} %collective-permute-done.6.refs_1_), channel_id=1, source_target_pairs={{4,12},{6,2},{12,20},{14,6},{20,28},{22,14},{28,24},{30,22},{24,16... | collective-permute-start | bytes 1179656 | tf_op jit(solution)/shard_map/ppermute | solution.py:405
  29.0 2.7 %shard_map.92 = (bf16[2,1536,256]{2,1,0:T(8,128)(2,1)S(1)}, f32[1536,2]{1,0:T(8,128)S(1)}) custom-call(bf16[768,256]{1,0:T(8,128)(2,1)} %collective-permute-done.5.refs_0_, bf16[768,256]{1,0:T(8,128)(2,1)S(1)} %collective-permute-done.6.refs_1_, bf16[768,256]{1,0:T(8,128)(2,1)S(1)} %get-tuple-element.83.refs_1_.refs_2_.refs_7_.refs_0_, ...), custom_call_target="tpu_custom_call" | custom-call | flops 1207959552 | bytes 4718592 | tf_op jit(solution)/shard_map/pallas_call | solution.py:46
  35.2 2.6 %shard_map.93 = (bf16[2,1536,256]{2,1,0:T(8,128)(2,1)S(1)}, f32[1536,2]{1,0:T(8,128)S(1)}) custom-call(bf16[768,256]{1,0:T(8,128)(2,1)S(1)} %collective-permute-done.8.refs_0_, bf16[768,256]{1,0:T(8,128)(2,1)S(1)} %collective-permute-done.9.refs_1_, bf16[768,256]{1,0:T(8,128)(2,1)S(1)} %get-tuple-element.83.refs_1_.refs_2_.refs_7_.refs_0_, ...), custom_call_target="tpu_custom_call" | custom-call | flops 1207959552 | bytes 4718592 | tf_op jit(solution)/shard_map/pallas_call | solution.py:46
  37.8 1.8 %collective-permute-done.10.refs_0_ = bf16[768,256]{1,0:T(8,128)(2,1)S(1)} collective-permute-done((bf16[768,256]{1,0:T(8,128)(2,1)S(1)}, bf16[768,256]{1,0:T(8,128)(2,1)S(1)}, u32[]{:S(2)}, u32[]{:S(2)}) %collective-permute-start.10) | collective-permute-done | bytes 393248 | tf_op jit(solution)/shard_map/ppermute | solution.py:405
  39.6 1.9 %shard_map.94 = (bf16[1,1536,256]{2,1,0:T(8,128)(2,1)S(1)}, f32[1536,1]{1,0:T(8,128)S(1)}) custom-call(bf16[768,256]{1,0:T(8,128)(2,1)S(1)} %collective-permute-done.10.refs_0_, bf16[768,256]{1,0:T(8,128)(2,1)S(1)} %get-tuple-element.83.refs_1_.refs_2_.refs_7_.refs_0_, bf16[768,256]{1,0:T(8,128)(2,1)} %collective-permute-done.refs_2_.refs_3_, ...), custom_call_target="tpu_custom_call" | custom-call | flops 603979776 | bytes 3538944 | tf_op jit(solution)/shard_map/pallas_call | solution.py:46
  45.3 1.9 %collective-permute-start.12 = (f32[1,4,8,768]{3,2,0,1:T(8,128)S(1)}, f32[1,4,8,768]{3,2,0,1:T(8,128)S(1)}, u32[]{:S(2)}, u32[]{:S(2)}) collective-permute-start(f32[1,4,8,768]{3,2,0,1:T(8,128)S(1)} %get-tuple-element.102), channel_id=1, source_target_pairs={{0,16},{2,18},{4,20},{6,22},{8,24},{10,26},{12,28},{14,30},{16,0},... | collective-permute-start | bytes 294920 | tf_op jit(solution)/shard_map/ppermute | solution.py:390
  47.2 1.8 %collective-permute-start.15 = (bf16[768,256]{1,0:T(8,128)(2,1)S(1)}, bf16[768,256]{1,0:T(8,128)(2,1)S(1)}, u32[]{:S(2)}, u32[]{:S(2)}) collective-permute-start(bf16[768,256]{1,0:T(8,128)(2,1)S(1)} %collective-permute-done.14.refs_1_), channel_id=1, source_target_pairs={{4,12},{6,2},{12,20},{14,6},{20,28},{22,14},{28,24},{30,22},{24,16... | collective-permute-start | bytes 1179656 | tf_op jit(solution)/shard_map/ppermute | solution.py:405
  51.3 4.3 %collective-permute-done.12 = f32[1,4,8,768]{3,2,0,1:T(8,128)S(1)} collective-permute-done((f32[1,4,8,768]{3,2,0,1:T(8,128)S(1)}, f32[1,4,8,768]{3,2,0,1:T(8,128)S(1)}, u32[]{:S(2)}, u32[]{:S(2)}) %collective-permute-start.12) | collective-permute-done | bytes 98336 | tf_op jit(solution)/shard_map/ppermute | solution.py:390
  55.7 2.3 %shard_map.98.own_ref = f32[768,256]{1,0:T(8,128)S(1)} custom-call(bf16[1,1536,256]{2,1,0:T(8,128)(2,1)S(1)} %get-tuple-element.74.refs_0_, bf16[2,1536,256]{2,1,0:T(8,128)(2,1)S(1)} %get-tuple-element.75.refs_1_, bf16[2,1536,256]{2,1,0:T(8,128)(2,1)S(1)} %get-tuple-element.76.refs_2_, bf16[2,1536,256]{2,1,0:T(8,128)(2,1)S(1)} %get-tuple-element.77.refs_3_, ...), custom_call_target="tpu_custom_call" | custom-call | flops 1207959552 | bytes 9043968 | tf_op jit(solution)/shard_map/pallas_call | solution.py:46
  60.4 3.2 %collective-permute-start.20 = (f32[4,1,8,768]{3,2,0,1:T(8,128)S(1)}, f32[4,1,8,768]{3,2,0,1:T(8,128)S(1)}, u32[]{:S(2)}, u32[]{:S(2)}) collective-permute-start(f32[4,1,8,768]{3,2,0,1:T(8,128)S(1)} %get-tuple-element.100), channel_id=1, source_target_pairs={{0,4},{2,6},{4,0},{6,2},{8,12},{10,14},{12,8},{14,10},{16,20},{18,... | collective-permute-start | bytes 294920 | tf_op jit(solution)/shard_map/ppermute | solution.py:390
  63.7 1.8 %shard_map.100.refs_6_ = f32[768,256]{1,0:T(8,128)S(1)} custom-call(bf16[768,256]{1,0:T(8,128)(2,1)S(1)} %copy-done.7, bf16[1536,256]{1,0:T(8,128)(2,1)S(1)} %collective-permute-done.7.refs_0_.refs_6_.refs_1_, f32[1,768]{1,0:T(1,128)S(1)} %get-tuple-element.86.refs_2_, f32[1,768]{1,0:T(1,128)S(1)} %collective-permute-done.17.refs_3_, ...), custom_call_target="tpu_custom_call" | custom-call | flops 1207959552 | bytes 2433024 | tf_op jit(solution)/shard_map/pallas_call | solution.py:46
  65.9 2.4 %collective-permute-start.23 = (bf16[768,256]{1,0:T(8,128)(2,1)S(1)}, bf16[768,256]{1,0:T(8,128)(2,1)S(1)}, u32[]{:S(2)}, u32[]{:S(2)}) collective-permute-start(bf16[768,256]{1,0:T(8,128)(2,1)S(1)} %collective-permute-done.22.refs_4_), channel_id=1, source_target_pairs={{4,12},{6,2},{12,20},{14,6},{20,28},{22,14},{28,24},{30,22},{24,16... | collective-permute-start | bytes 1179656 | tf_op jit(solution)/shard_map/ppermute | solution.py:405
  68.2 2.8 %collective-permute-done.20 = f32[4,1,8,768]{3,2,0,1:T(8,128)S(1)} collective-permute-done((f32[4,1,8,768]{3,2,0,1:T(8,128)S(1)}, f32[4,1,8,768]{3,2,0,1:T(8,128)S(1)}, u32[]{:S(2)}, u32[]{:S(2)}) %collective-permute-start.20) | collective-permute-done | bytes 98336 | tf_op jit(solution)/shard_map/ppermute | solution.py:390
  71.1 2.5 %collective-permute-start.19 = (bf16[768,256]{1,0:T(8,128)(2,1)S(1)}, bf16[768,256]{1,0:T(8,128)(2,1)S(1)}, u32[]{:S(2)}, u32[]{:S(2)}) collective-permute-start(bf16[768,256]{1,0:T(8,128)(2,1)S(1)} %collective-permute-done.16.refs_0_), channel_id=1, source_target_pairs={{4,12},{6,2},{12,20},{14,6},{20,28},{22,14},{28,24},{30,22},{24,16... | collective-permute-start | bytes 1179656 | tf_op jit(solution)/shard_map/ppermute | solution.py:405
  73.6 3.9 %shard_map.101 = (f32[768,256]{1,0:T(8,128)S(1)}, f32[768,256]{1,0:T(8,128)S(1)}) custom-call(s32[1]{0:T(128)} %bitcast.me_ref, s32[16,32]{1,0:T(8,128)S(1)} %copy-done.8, bf16[768,256]{1,0:T(8,128)(2,1)S(1)} %copy-done.7, bf16[768,256]{1,0:T(8,128)(2,1)S(1)} %collective-permute-done.14.refs_1_, bf16[768,256]{1,0:T(8,128)(2,1)S(1)} %collective-permute-done.21.refs_2_, ...), custom_call_target="tpu_custom_call" | custom-call | flops 3019898880 | bytes 4534272 | tf_op jit(solution)/shard_map/pallas_call | solution.py:46
  77.5 2.1 %shard_map.102 = (f32[768,256]{1,0:T(8,128)S(1)}, f32[768,256]{1,0:T(8,128)S(1)}) custom-call(s32[1]{0:T(128)} %bitcast.me_ref, s32[16,32]{1,0:T(8,128)S(1)} %copy-done.8, bf16[768,256]{1,0:T(8,128)(2,1)S(1)} %collective-permute-done.16.refs_0_, bf16[768,256]{1,0:T(8,128)(2,1)S(1)} %collective-permute-done.23.refs_1_, ...), custom_call_target="tpu_custom_call" | custom-call | flops 1207959552 | bytes 4141056 | tf_op jit(solution)/shard_map/pallas_call | solution.py:46
  79.6 2.4 %shard_map.103 = (f32[768,256]{1,0:T(8,128)S(1)}, f32[768,256]{1,0:T(8,128)}) custom-call(s32[1]{0:T(128)} %bitcast.me_ref, s32[16,32]{1,0:T(8,128)S(1)} %copy-done.8, bf16[768,256]{1,0:T(8,128)(2,1)S(1)} %collective-permute-done.19.refs_0_, f32[8,8,768]{2,1,0:T(8,128)S(1)} %maximum_bitcast_fusion.refs_5_.refs_2_.refs_1_, ...), custom_call_target="tpu_custom_call" | custom-call | flops 603979776 | bytes 3747840 | tf_op jit(solution)/shard_map/pallas_call | solution.py:46
  85.5 2.5 %shard_map.104 = f32[768,256]{1,0:T(8,128)} custom-call(bf16[768,256]{1,0:T(8,128)(2,1)S(1)} %copy-done.3, f32[768,256]{1,0:T(8,128)S(1)} %copy-done.5, f32[768,256]{1,0:T(8,128)} %collective-permute-done.24.other_ref), custom_call_target="tpu_custom_call" | custom-call | flops 1000000 | bytes 2752512 | tf_op jit(solution)/shard_map/pallas_call | solution.py:46
  (77 shorter events, 28.8 us)
Async XLA Ops:
  1.9 6.1 %collective-permute-start.3 = (bf16[768,256]{1,0:T(8,128)(2,1)S(1)}, bf16[768,256]{1,0:T(8,128)(2,1)}, u32[]{:S(2)}, u32[]{:S(2)}) collective-permute-start(bf16[768,256]{1,0:T(8,128)(2,1)S(1)} %shard_map.85.k_ref.refs_0_.refs_5_.refs_4_), channel_id=1, source_target_pairs={{0,2},{2,0},{4,6},{6,4},{8,10},{10,8},{12,14},{14,12},{16,18},{18,... | collective-permute-start | bytes 1179656 | tf_op jit(solution)/shard_map/ppermute | solution.py:382
  2.4 8.5 %collective-permute-start.2 = (bf16[768,256]{1,0:T(8,128)(2,1)S(1)}, bf16[768,256]{1,0:T(8,128)(2,1)}, u32[]{:S(2)}, u32[]{:S(2)}) collective-permute-start(bf16[768,256]{1,0:T(8,128)(2,1)S(1)} %shard_map.85.k_ref.refs_0_.refs_5_.refs_4_), channel_id=1, source_target_pairs={{4,12},{6,2},{12,20},{14,6},{20,28},{22,14},{28,24},{30,22},{24,16... | collective-permute-start | bytes 1179656 | tf_op jit(solution)/shard_map/ppermute | solution.py:405
  6.3 9.0 %collective-permute-start = (bf16[768,256]{1,0:T(8,128)(2,1)S(1)}, bf16[768,256]{1,0:T(8,128)(2,1)}, u32[]{:S(2)}, u32[]{:S(2)}) collective-permute-start(bf16[768,256]{1,0:T(8,128)(2,1)S(1)} %get-tuple-element.83.refs_1_.refs_2_.refs_7_.refs_0_), channel_id=1, source_target_pairs={{0,2},{2,0},{4,6},{6,4},{8,10},{10,8},{12,14},{14,12},{16,18},{18,... | collective-permute-start | bytes 1179656 | tf_op jit(solution)/shard_map/ppermute | solution.py:382
  6.5 19.7 %collective-permute-start.7 = (bf16[1536,256]{1,0:T(8,128)(2,1)S(1)}, bf16[1536,256]{1,0:T(8,128)(2,1)S(1)}, u32[]{:S(2)}, u32[]{:S(2)}) collective-permute-start(bf16[1536,256]{1,0:T(8,128)(2,1)S(1)} %get-tuple-element.58), channel_id=1, source_target_pairs={{0,1},{1,0},{2,3},{3,2},{4,5},{5,4},{6,7},{7,6},{8,9},{9,8},{10,11... | collective-permute-start | bytes 2359304 | tf_op jit(solution)/shard_map/ppermute | solution.py:410
  8.0 9.2 %collective-permute-start.4 = (bf16[768,256]{1,0:T(8,128)(2,1)}, bf16[768,256]{1,0:T(8,128)(2,1)}, u32[]{:S(2)}, u32[]{:S(2)}) collective-permute-start(bf16[768,256]{1,0:T(8,128)(2,1)} %collective-permute-done.3), channel_id=1, source_target_pairs={{4,12},{6,2},{12,20},{14,6},{20,28},{22,14},{28,24},{30,22},{24,16... | collective-permute-start | bytes 1179656 | tf_op jit(solution)/shard_map/ppermute | solution.py:405
  10.9 10.8 %collective-permute-start.5 = (bf16[768,256]{1,0:T(8,128)(2,1)}, bf16[768,256]{1,0:T(8,128)(2,1)}, u32[]{:S(2)}, u32[]{:S(2)}) collective-permute-start(bf16[768,256]{1,0:T(8,128)(2,1)} %collective-permute-done.2.refs_0_), channel_id=1, source_target_pairs={{4,12},{6,2},{12,20},{14,6},{20,28},{22,14},{28,24},{30,22},{24,16... | collective-permute-start | bytes 1179656 | tf_op jit(solution)/shard_map/ppermute | solution.py:405
  17.2 10.2 %collective-permute-start.6 = (bf16[768,256]{1,0:T(8,128)(2,1)}, bf16[768,256]{1,0:T(8,128)(2,1)S(1)}, u32[]{:S(2)}, u32[]{:S(2)}) collective-permute-start(bf16[768,256]{1,0:T(8,128)(2,1)} %collective-permute-done.4.refs_1_), channel_id=1, source_target_pairs={{4,12},{6,2},{12,20},{14,6},{20,28},{22,14},{28,24},{30,22},{24,16... | collective-permute-start | bytes 1179656 | tf_op jit(solution)/shard_map/ppermute | solution.py:405
  21.7 10.1 %collective-permute-start.8 = (bf16[768,256]{1,0:T(8,128)(2,1)}, bf16[768,256]{1,0:T(8,128)(2,1)S(1)}, u32[]{:S(2)}, u32[]{:S(2)}) collective-permute-start(bf16[768,256]{1,0:T(8,128)(2,1)} %collective-permute-done.5.refs_0_), channel_id=1, source_target_pairs={{4,12},{6,2},{12,20},{14,6},{20,28},{22,14},{28,24},{30,22},{24,16... | collective-permute-start | bytes 1179656 | tf_op jit(solution)/shard_map/ppermute | solution.py:405
  27.4 7.8 %collective-permute-start.9 = (bf16[768,256]{1,0:T(8,128)(2,1)S(1)}, bf16[768,256]{1,0:T(8,128)(2,1)S(1)}, u32[]{:S(2)}, u32[]{:S(2)}) collective-permute-start(bf16[768,256]{1,0:T(8,128)(2,1)S(1)} %collective-permute-done.6.refs_1_), channel_id=1, source_target_pairs={{4,12},{6,2},{12,20},{14,6},{20,28},{22,14},{28,24},{30,22},{24,16... | collective-permute-start | bytes 1179656 | tf_op jit(solution)/shard_map/ppermute | solution.py:405
  31.8 7.8 %collective-permute-start.10 = (bf16[768,256]{1,0:T(8,128)(2,1)S(1)}, bf16[768,256]{1,0:T(8,128)(2,1)S(1)}, u32[]{:S(2)}, u32[]{:S(2)}) collective-permute-start(bf16[768,256]{1,0:T(8,128)(2,1)S(1)} %collective-permute-done.8.refs_0_), channel_id=1, source_target_pairs={{4,12},{6,2},{12,20},{14,6},{20,28},{22,14},{28,24},{30,22},{24,16... | collective-permute-start | bytes 1179656 | tf_op jit(solution)/shard_map/ppermute | solution.py:405
  33.4 13.8 %collective-permute-start.14 = (bf16[768,256]{1,0:T(8,128)(2,1)S(1)}, bf16[768,256]{1,0:T(8,128)(2,1)S(1)}, u32[]{:S(2)}, u32[]{:S(2)}) collective-permute-start(bf16[768,256]{1,0:T(8,128)(2,1)S(1)} %get-tuple-element.83.refs_1_.refs_2_.refs_7_.refs_0_), channel_id=1, source_target_pairs={{4,12},{6,2},{12,20},{14,6},{20,28},{22,14},{28,24},{30,22},{24,16... | collective-permute-start | bytes 1179656 | tf_op jit(solution)/shard_map/ppermute | solution.py:405
  42.6 1.7 %collective-permute-start.11 = (f32[17,768]{1,0:T(8,128)S(1)}, f32[17,768]{1,0:T(8,128)S(1)}, u32[]{:S(2)}, u32[]{:S(2)}) collective-permute-start(f32[17,768]{1,0:T(8,128)S(1)} %get-tuple-element.71), channel_id=1, source_target_pairs={{0,2},{2,0},{4,6},{6,4},{8,10},{10,8},{12,14},{14,12},{16,18},{18,... | collective-permute-start | bytes 156680 | tf_op jit(solution)/shard_map/ppermute | solution.py:382
  42.6 15.4 %collective-permute-start.21 = (bf16[768,256]{1,0:T(8,128)(2,1)}, bf16[768,256]{1,0:T(8,128)(2,1)S(1)}, u32[]{:S(2)}, u32[]{:S(2)}) collective-permute-start(bf16[768,256]{1,0:T(8,128)(2,1)} %collective-permute-done.refs_2_.refs_3_), channel_id=1, source_target_pairs={{4,12},{6,2},{12,20},{14,6},{20,28},{22,14},{28,24},{30,22},{24,16... | collective-permute-start | bytes 1179656 | tf_op jit(solution)/shard_map/ppermute | solution.py:405
  45.3 10.3 %collective-permute-start.12 = (f32[1,4,8,768]{3,2,0,1:T(8,128)S(1)}, f32[1,4,8,768]{3,2,0,1:T(8,128)S(1)}, u32[]{:S(2)}, u32[]{:S(2)}) collective-permute-start(f32[1,4,8,768]{3,2,0,1:T(8,128)S(1)} %get-tuple-element.102), channel_id=1, source_target_pairs={{0,16},{2,18},{4,20},{6,22},{8,24},{10,26},{12,28},{14,30},{16,0},... | collective-permute-start | bytes 294920 | tf_op jit(solution)/shard_map/ppermute | solution.py:390
  47.2 13.2 %collective-permute-start.15 = (bf16[768,256]{1,0:T(8,128)(2,1)S(1)}, bf16[768,256]{1,0:T(8,128)(2,1)S(1)}, u32[]{:S(2)}, u32[]{:S(2)}) collective-permute-start(bf16[768,256]{1,0:T(8,128)(2,1)S(1)} %collective-permute-done.14.refs_1_), channel_id=1, source_target_pairs={{4,12},{6,2},{12,20},{14,6},{20,28},{22,14},{28,24},{30,22},{24,16... | collective-permute-start | bytes 1179656 | tf_op jit(solution)/shard_map/ppermute | solution.py:405
  49.0 14.7 %collective-permute-start.17 = (f32[1,768]{1,0:T(1,128)S(1)}, f32[1,768]{1,0:T(1,128)S(1)}, u32[]{:S(2)}, u32[]{:S(2)}) collective-permute-start(f32[1,768]{1,0:T(1,128)S(1)} %get-tuple-element.86.refs_2_), channel_id=1, source_target_pairs={{0,1},{1,0},{2,3},{3,2},{4,5},{5,4},{6,7},{7,6},{8,9},{9,8},{10,11... | collective-permute-start | bytes 9224 | tf_op jit(solution)/shard_map/ppermute | solution.py:410
  51.2 32.2 %collective-permute-start.13 = (f32[768,256]{1,0:T(8,128)S(1)}, f32[768,256]{1,0:T(8,128)S(1)}, u32[]{:S(2)}, u32[]{:S(2)}) collective-permute-start(f32[768,256]{1,0:T(8,128)S(1)} %shard_map.97), channel_id=1, source_target_pairs={{0,2},{2,0},{4,6},{6,4},{8,10},{10,8},{12,14},{14,12},{16,18},{18,... | collective-permute-start | bytes 2359304 | tf_op jit(solution)/shard_map/ppermute | solution.py:382
  55.6 4.7 %collective-permute-start.18 = (f32[2,2,8,768]{3,2,0,1:T(8,128)S(1)}, f32[2,2,8,768]{3,2,0,1:T(8,128)S(1)}, u32[]{:S(2)}, u32[]{:S(2)}) collective-permute-start(f32[2,2,8,768]{3,2,0,1:T(8,128)S(1)} %fusion.1), channel_id=1, source_target_pairs={{0,8},{2,10},{4,12},{6,14},{8,0},{10,2},{12,4},{14,6},{16,24},{18,... | collective-permute-start | bytes 294920 | tf_op jit(solution)/shard_map/ppermute | solution.py:390
  58.1 7.8 %collective-permute-start.22 = (bf16[768,256]{1,0:T(8,128)(2,1)S(1)}, bf16[768,256]{1,0:T(8,128)(2,1)S(1)}, u32[]{:S(2)}, u32[]{:S(2)}) collective-permute-start(bf16[768,256]{1,0:T(8,128)(2,1)S(1)} %collective-permute-done.21.refs_2_), channel_id=1, source_target_pairs={{4,12},{6,2},{12,20},{14,6},{20,28},{22,14},{28,24},{30,22},{24,16... | collective-permute-start | bytes 1179656 | tf_op jit(solution)/shard_map/ppermute | solution.py:405
  60.4 10.7 %collective-permute-start.16 = (bf16[768,256]{1,0:T(8,128)(2,1)S(1)}, bf16[768,256]{1,0:T(8,128)(2,1)S(1)}, u32[]{:S(2)}, u32[]{:S(2)}) collective-permute-start(bf16[768,256]{1,0:T(8,128)(2,1)S(1)} %collective-permute-done.15.refs_3_), channel_id=1, source_target_pairs={{4,12},{6,2},{12,20},{14,6},{20,28},{22,14},{28,24},{30,22},{24,16... | collective-permute-start | bytes 1179656 | tf_op jit(solution)/shard_map/ppermute | solution.py:405
  60.4 10.6 %collective-permute-start.20 = (f32[4,1,8,768]{3,2,0,1:T(8,128)S(1)}, f32[4,1,8,768]{3,2,0,1:T(8,128)S(1)}, u32[]{:S(2)}, u32[]{:S(2)}) collective-permute-start(f32[4,1,8,768]{3,2,0,1:T(8,128)S(1)} %get-tuple-element.100), channel_id=1, source_target_pairs={{0,4},{2,6},{4,0},{6,2},{8,12},{10,14},{12,8},{14,10},{16,20},{18,... | collective-permute-start | bytes 294920 | tf_op jit(solution)/shard_map/ppermute | solution.py:390
  65.9 11.6 %collective-permute-start.23 = (bf16[768,256]{1,0:T(8,128)(2,1)S(1)}, bf16[768,256]{1,0:T(8,128)(2,1)S(1)}, u32[]{:S(2)}, u32[]{:S(2)}) collective-permute-start(bf16[768,256]{1,0:T(8,128)(2,1)S(1)} %collective-permute-done.22.refs_4_), channel_id=1, source_target_pairs={{4,12},{6,2},{12,20},{14,6},{20,28},{22,14},{28,24},{30,22},{24,16... | collective-permute-start | bytes 1179656 | tf_op jit(solution)/shard_map/ppermute | solution.py:405
  71.1 8.5 %collective-permute-start.19 = (bf16[768,256]{1,0:T(8,128)(2,1)S(1)}, bf16[768,256]{1,0:T(8,128)(2,1)S(1)}, u32[]{:S(2)}, u32[]{:S(2)}) collective-permute-start(bf16[768,256]{1,0:T(8,128)(2,1)S(1)} %collective-permute-done.16.refs_0_), channel_id=1, source_target_pairs={{4,12},{6,2},{12,20},{14,6},{20,28},{22,14},{28,24},{30,22},{24,16... | collective-permute-start | bytes 1179656 | tf_op jit(solution)/shard_map/ppermute | solution.py:405
  82.8 2.6 %collective-permute-start.24 = (f32[768,256]{1,0:T(8,128)}, f32[768,256]{1,0:T(8,128)}, u32[]{:S(2)}, u32[]{:S(2)}) collective-permute-start(f32[768,256]{1,0:T(8,128)} %get-tuple-element.98), channel_id=1, source_target_pairs={{0,2},{2,0},{4,6},{6,4},{8,10},{10,8},{12,14},{14,12},{16,18},{18,... | collective-permute-start | bytes 2359304 | tf_op jit(solution)/shard_map/ppermute | solution.py:382
  (13 other events, 96.4 us)

commit v4 on v3

--- a/solution.py
+++ b/solution.py
@@ -172,8 +172,6 @@
 
 
 def weights_kernel(
-    me_ref,
-    table_ref,
     logits_ref,
     other_ref,
     own_ref,
@@ -182,12 +180,12 @@
     diag_ref,
     loss_ref,
     log_ref,
+    home_ref,
     message_ref,
     columns_ref,
     sib_columns_ref,
 ):
     chips, anchors = logits_ref.shape[0], group_ref.shape[1]
-    me = me_ref[0]
 
     def all_weights(near, far, near_codes, far_codes, group, inverse):
         total, chosen = group, jnp.zeros((1, anchors), F32)
@@ -230,18 +228,19 @@
     def row(x, slot):
         return x[slot : slot + 1, :]
 
-    message_ref[...] = jnp.zeros_like(message_ref)
-    for slot in (0, chips - 1):
-        there = table_ref[me, 3 * chips + slot]
-        rows = [row(near_code, slot), row(far_code, slot), row(near, slot), row(far, slot)]
-        message_ref[there, :4, :] = jnp.concatenate(rows, axis=0)
+    def both_sides(slot):
+        return [row(near_code, slot), row(far_code, slot), row(near, slot), row(far, slot)]
+
+    home_ref[:4, :] = jnp.concatenate(both_sides(0), axis=0)
+    home_ref[4:, :] = jnp.zeros((4, anchors), F32)
     for slot in range(2, chips - 1, 2):
-        there = table_ref[me, 3 * chips + slot]
         rows = []
         for codes, weights in ((far_code, far), (sib_far_code, sib_far)):
             rows += [row(codes, slot), row(codes, slot - 1)]
             rows += [row(weights, slot), row(weights, slot - 1)]
-        message_ref[there] = jnp.concatenate(rows, axis=0)
+        message_ref[slot // 2 - 1] = jnp.concatenate(rows, axis=0)
+    last = both_sides(chips - 1) + [jnp.zeros((4, anchors), F32)]
+    message_ref[chips // 2 - 1] = jnp.concatenate(last, axis=0)
 
 
 def partner_sum(columns, order, named, rows):
@@ -320,23 +319,18 @@
         out_ref[rows, :] = total
 
 
-def grad_key_kernel(places, carried, me_ref, table_ref, *refs):
-    blocks, rest = refs[: len(places)], refs[len(places) :]
-    message_ref = rest[0]
-    so_far = rest[1 : 1 + carried]
-    outs = rest[1 + carried :]
+def grad_key_kernel(sources, blocks, carried, *refs):
+    queries, messages = refs[:blocks], refs[blocks : -2 - carried]
+    so_far, outs = refs[len(refs) - 2 - carried : len(refs) - 2], refs[-2:]
     anchors, width = outs[0].shape
-    chips = message_ref.shape[0]
     step = 256
-    source = [table_ref[me_ref[0], 2 * chips + place] for place in places]
-    first = [4 if place % 2 == 0 and place else 0 for place in places]
     for side, out in enumerate(outs):
         for start in range(0, anchors, step):
             rows = slice(start, start + step)
             total = so_far[side][rows, :] if side < carried else jnp.zeros((step, width), F32)
-            for at, base, block in zip(source, first, blocks):
-                code = message_ref[at, base + side : base + side + 1, :]
-                weight = message_ref[at, base + 2 + side : base + 3 + side, :]
+            for (at, base), block in zip(sources, queries):
+                code = messages[at][base + side : base + side + 1, :]
+                weight = messages[at][base + 2 + side : base + 3 + side, :]
                 spread = jnp.where(row_ids(step, anchors, start) == code, weight, 0.0)
                 total += dot(spread.astype(BF16), block[...])
             out[rows, :] = total
@@ -348,7 +342,6 @@
     loop = lax.axis_size("loop")
     chips = sky // 2
     middle = chips // 2
-    bits = chips.bit_length() - 1
     order = chip_ring(chips)
     position = {chip: place for place, chip in enumerate(order)}
 
@@ -361,17 +354,7 @@
             owners += [2 * along[step] + core, 2 * along[step] + 1 - core]
         return owners + [2 * along[middle] + core]
 
-    table = np.zeros((sky, 4 * chips), np.int32)
-    for device in range(sky):
-        near, far = handled(device), handled(device ^ 1)
-        for slot in range(chips):
-            relative = near[slot] // 2 ^ device // 2
-            table[device, slot] = near[slot]
-            table[device, chips + slot] = far[slot]
-            table[device, 2 * chips + slot] = sum(
-                (relative >> bit & 1) << (bits - 1 - bit) for bit in range(bits)
-            )
-            table[device, 3 * chips + slot] = far[slot] // 2 ^ device // 2
+    table = np.array([handled(device) + handled(device ^ 1) for device in range(sky)], np.int32)
     siblings = [(i, i ^ 1) for i in range(sky)]
     onward = []
     for place, chip in enumerate(order):
@@ -380,18 +363,6 @@
 
     def swap(x):
         return lax.ppermute(x, "sky", siblings)
-
-    def exchange(message):
-        held = message[None]
-        stages = []
-        step = chips // 2
-        while step:
-            pairs = [(i, i ^ (2 * step)) for i in range(sky)]
-            got = lax.ppermute(held[:, step:], "sky", pairs)
-            stages.append(got)
-            held = jnp.concatenate([held[:, :step], got], axis=0)
-            step //= 2
-        return stages, held.reshape(message.shape)
 
     def after(x, *others):
         return lax.optimization_barrier((x,) + others)[0] if others else x
@@ -447,7 +418,6 @@
 
     batches = [[0]] + [[2 * s - 1, 2 * s] for s in range(1, middle)] + [[chips - 1]]
     parts = []
-    group_total = diag = None
     pins = ()
     for step in range(2, middle + 1):
         incoming = key_ring.front[0]
@@ -455,14 +425,6 @@
         if step == 2:
             parts.append(partners_of(batches[0]))
             pins = (parts[-1][1],)
-        elif group_total is None:
-            group_total, diag = call(
-                functools.partial(group_forward_kernel, loop),
-                [shape((1, anchors))] * 2,
-                [key_rows] + others + [after(query_rows, *pins)],
-                loop * one_block,
-            )
-            pins = (group_total,)
         if step < middle:
             key_ring.hop(1, *pins)
             parts.append(partners_of(batches[step - 1], *pins))
@@ -470,74 +432,94 @@
     query_ring.hop(0, incoming)
     parts.append(partners_of(batches[middle - 1], *pins))
     query_ring.hop(1, parts[-1][1])
-    parts.append(partners_of(batches[middle], parts[-1][1]))
+    group_total, diag = call(
+        functools.partial(group_forward_kernel, loop),
+        [shape((1, anchors))] * 2,
+        [key_rows] + others + [after(query_rows, parts[-1][1])],
+        loop * one_block,
+    )
+    parts.append(partners_of(batches[middle], group_total))
     logits, payload = call(
         totals_kernel,
         [shape((chips, 2 * anchors)), shape((2 * chips + 1, anchors))],
         [part[1] for part in parts] + [group_total],
         1e6,
     )
-    query_ring.hop(0, logits)
     other = swap(payload)
-    loss, log_total, message, columns, sib_columns = call(
+    loss, log_total, home, message, columns, sib_columns = call(
         weights_kernel,
         [
             shape((1, anchors)),
             shape((1, anchors)),
-            shape((chips, 8, anchors)),
+            shape((8, anchors)),
+            shape((middle, 8, anchors)),
             shape((anchors, chips + 8)),
             shape((anchors, chips)),
         ],
-        where + [logits, other, codes, sib_codes, group_total, diag],
+        [logits, other, codes, sib_codes, group_total, diag],
         1e6,
-        smem=(0, 1),
-    )
-    stages, messages = exchange(message)
+    )
+    arrived = []
+    for step in range(middle):
+        message = lax.ppermute(message, "sky", onward)
+        arrived.append(message[0])
+        message = message[1:]
+
+    def grad_keys_of(steps, sums, *pins):
+        blocks, sources, messages = [], [], []
+        for step in steps:
+            slots = [0] if step == 0 else [chips - 1] if step == middle else [2 * step - 1, 2 * step]
+            for half, slot in enumerate(slots):
+                blocks.append(query_ring.blocks[slot])
+                sources.append((len(messages), 4 * half))
+            messages.append(arrived[step - 1] if step else home)
+        return call(
+            functools.partial(grad_key_kernel, sources, len(blocks), len(sums)),
+            [shape((anchors, width))] * 2,
+            blocks + messages + [after(sums[0], *pins)] + list(sums[1:]),
+            2 * len(blocks) * one_block,
+        )
+
+    query_ring.hop(0, log_total)
     all_logs = [log_total] + group(log_total)
-    query_ring.hop(1, log_total)
-    for step in range(3, middle):
-        if step < middle - 1:
-            query_ring.hop(0)
-            query_ring.hop(1)
     (sib_summed_q,) = call(
         functools.partial(grad_sibling_kernel, batches),
         [shape((anchors, width))],
         [part[0] for part in parts] + [sib_columns],
         1e6,
     )
-    query_ring.hop(0, sib_summed_q)
+    query_ring.hop(1, sib_summed_q)
+    for step in range(3, middle):
+        if step < middle - 1:
+            query_ring.hop(0)
+            query_ring.hop(1)
     (summed_q,) = call(
         functools.partial(grad_query_kernel, batches, loop),
         [shape((anchors, width))],
         [part[0] for part in parts]
         + [key_rows]
         + others
-        + [after(query_rows, stages[0], sib_summed_q), columns],
+        + [after(query_rows, sib_summed_q), columns],
         2 * loop * one_block,
     )
-    query_ring.hop(1, summed_q)
+    query_ring.hop(0, summed_q)
     (group_k,) = call(
         functools.partial(group_key_kernel, loop),
         [shape((anchors, width))],
-        [query_rows] + others + all_logs + [after(key_rows, stages[1], summed_q), inverse],
+        [query_rows] + others + all_logs + [after(key_rows, summed_q), inverse],
         2 * loop * one_block,
     )
-    query_ring.hop(0, group_k)
+    query_ring.hop(1, group_k)
+    summed_k = grad_keys_of([0, 1], [group_k])
+    query_ring.hop(0, summed_k[0])
     (grad_queries,) = call(
         finish_kernel,
         [shape((anchors, width))],
-        [queries, summed_q, swap(sib_summed_q)],
+        [queries, after(summed_q, summed_k[0]), swap(sib_summed_q)],
         1e6,
     )
-    summed_k = [group_k]
-    for batch in (range(chips - 3), [chips - 3, chips - 2], [chips - 1]):
-        summed_k = call(
-            functools.partial(grad_key_kernel, list(batch), len(summed_k)),
-            [shape((anchors, width))] * 2,
-            where + [query_ring.blocks[p] for p in batch] + [messages] + list(summed_k),
-            2 * len(batch) * one_block,
-            smem=(0, 1),
-        )
+    for step in range(2, middle + 1):
+        summed_k = grad_keys_of([step], summed_k)
     (grad_keys,) = call(
         finish_kernel,
         [shape((anchors, width))],

time: 88.4 us -> 81.1 us (0.917)
  Pallas kernels: 33.6 us -> 26.6 us
  starting transfers between devices: 33 us -> 31.9 us
  waiting for transfers between devices: 16.8 us -> 17.8 us
    pallas_call x20 -> x21, Pallas kernels: 33.6 us -> 26.6 us  [call(): pl.pallas_call(kernel, out_shape=list(outs), in_specs=specs, out_specs=[p...]
    ppermute x14, waiting for transfers between devices: 3.93 us -> 10.3 us  [hop(): lax.ppermute(after(self.front[which], *pins), 'sky', onward)]
    ppermute x3 -> x4, waiting for transfers between devices: 8 us -> 4.36 us  [shards(): message = lax.ppermute(message, 'sky', onward)]
    ppermute x2, waiting for transfers between devices: 2.95 us -> 0.01 us  [group(): return [lax.ppermute(x, 'loop', pairs) for pairs in shifts]]
    ppermute x6, waiting for transfers between devices: 1.91 us -> 3.16 us  [swap(): return lax.ppermute(x, 'sky', siblings)]
    ppermute x3 -> x4, starting transfers between devices: 5.18 us -> 5.34 us  [shards(): message = lax.ppermute(message, 'sky', onward)]
    unnamed x24 -> x20, local copies, waits for them, and re-layouts: 2.92 us -> 2.91 us
  transfers between devices with their start and end apart: 25 -> 26, of which waited for: 10 -> 12; matrix products, arithmetic and copies ran while one was open for 1% -> 1% of each run, Pallas kernels for 35% -> 30%
where the time goes in v4:
time: 81.1 us; the launch traced here: 80.8 us
  starting transfers between devices  31.9 us (39%)
  Pallas kernels  26.6 us (33%)
  waiting for transfers between devices  17.8 us (22%)
  local copies, waits for them, and re-layouts  2.94 us (4%)
  between operations  0.89 us (1%)
    pallas_call x21, Pallas kernels, call(): pl.pallas_call(kernel, out_shape=list(outs), in_specs=specs, out_specs=[p...  26.6 us
    ppermute x14, starting transfers between devices, hop(): lax.ppermute(after(self.front[which], *pins), 'sky', onward)  23.3 us
    ppermute x14, waiting for transfers between devices, hop(): lax.ppermute(after(self.front[which], *pins), 'sky', onward)  10.3 us
    ppermute x4, starting transfers between devices, shards(): message = lax.ppermute(message, 'sky', onward)  5.34 us
    ppermute x4, waiting for transfers between devices, shards(): message = lax.ppermute(message, 'sky', onward)  4.36 us
    ppermute x6, waiting for transfers between devices, swap(): return lax.ppermute(x, 'sky', siblings)  3.16 us
    unnamed x20, local copies, waits for them, and re-layouts  2.91 us
    ppermute x2, starting transfers between devices, group(): return [lax.ppermute(x, 'loop', pairs) for pairs in shifts]  2.1 us
  transfers between devices with their start and end apart: 26, of which 12 were waited for; matrix products, arithmetic and copies ran while one was open for 1% of the time, Pallas kernels for 30%

profile of v4, /device:TPU:0, one launch (start us, length us, event | category | flops | bytes accessed | tf_op | source)
XLA Modules:
  0.0 80.8 jit_solution(13747837181023473273)
XLA Ops:
  2.4 2.6 %collective-permute-start.2 = (bf16[768,256]{1,0:T(8,128)(2,1)S(1)}, bf16[768,256]{1,0:T(8,128)(2,1)S(1)}, u32[]{:S(2)}, u32[]{:S(2)}) collective-permute-start(bf16[768,256]{1,0:T(8,128)(2,1)S(1)} %shard_map.85.k_ref.refs_0_.refs_5_.refs_4_), channel_id=1, source_target_pairs={{4,12},{6,2},{12,20},{14,6},{20,28},{22,14},{28,24},{30,22},{24,16... | collective-permute-start | bytes 1179656 | tf_op jit(solution)/shard_map/ppermute | solution.py:376
  8.0 2.8 %collective-permute-done.2.refs_0_ = bf16[768,256]{1,0:T(8,128)(2,1)S(1)} collective-permute-done((bf16[768,256]{1,0:T(8,128)(2,1)S(1)}, bf16[768,256]{1,0:T(8,128)(2,1)S(1)}, u32[]{:S(2)}, u32[]{:S(2)}) %collective-permute-start.2) | collective-permute-done | bytes 393248 | tf_op jit(solution)/shard_map/ppermute | solution.py:376
  10.8 2.0 %collective-permute-start.5 = (bf16[768,256]{1,0:T(8,128)(2,1)S(1)}, bf16[768,256]{1,0:T(8,128)(2,1)S(1)}, u32[]{:S(2)}, u32[]{:S(2)}) collective-permute-start(bf16[768,256]{1,0:T(8,128)(2,1)S(1)} %collective-permute-done.2.refs_0_), channel_id=1, source_target_pairs={{4,12},{6,2},{12,20},{14,6},{20,28},{22,14},{28,24},{30,22},{24,16... | collective-permute-start | bytes 1179656 | tf_op jit(solution)/shard_map/ppermute | solution.py:376
  16.1 1.6 %collective-permute-start.6 = (bf16[768,256]{1,0:T(8,128)(2,1)}, bf16[768,256]{1,0:T(8,128)(2,1)S(1)}, u32[]{:S(2)}, u32[]{:S(2)}) collective-permute-start(bf16[768,256]{1,0:T(8,128)(2,1)} %collective-permute-done.4.refs_1_), channel_id=1, source_target_pairs={{4,12},{6,2},{12,20},{14,6},{20,28},{22,14},{28,24},{30,22},{24,16... | collective-permute-start | bytes 1179656 | tf_op jit(solution)/shard_map/ppermute | solution.py:376
  19.2 2.6 %shard_map.90 = (bf16[2,1536,256]{2,1,0:T(8,128)(2,1)S(1)}, f32[1536,2]{1,0:T(8,128)S(1)}) custom-call(bf16[768,256]{1,0:T(8,128)(2,1)S(1)} %collective-permute-done.2.refs_0_, bf16[768,256]{1,0:T(8,128)(2,1)} %collective-permute-done.4.refs_1_, bf16[768,256]{1,0:T(8,128)(2,1)S(1)} %get-tuple-element.86.refs_1_.refs_2_.refs_7_.refs_0_, ...), custom_call_target="tpu_custom_call" | custom-call | flops 1207959552 | bytes 4718592 | tf_op jit(solution)/shard_map/pallas_call | solution.py:46
  21.9 1.6 %collective-permute-start.7 = (bf16[768,256]{1,0:T(8,128)(2,1)S(1)}, bf16[768,256]{1,0:T(8,128)(2,1)S(1)}, u32[]{:S(2)}, u32[]{:S(2)}) collective-permute-start(bf16[768,256]{1,0:T(8,128)(2,1)S(1)} %collective-permute-done.5.refs_0_), channel_id=1, source_target_pairs={{4,12},{6,2},{12,20},{14,6},{20,28},{22,14},{28,24},{30,22},{24,16... | collective-permute-start | bytes 1179656 | tf_op jit(solution)/shard_map/ppermute | solution.py:376
  24.2 1.6 %collective-permute-start.8 = (bf16[768,256]{1,0:T(8,128)(2,1)S(1)}, bf16[768,256]{1,0:T(8,128)(2,1)S(1)}, u32[]{:S(2)}, u32[]{:S(2)}) collective-permute-start(bf16[768,256]{1,0:T(8,128)(2,1)S(1)} %collective-permute-done.6.refs_1_), channel_id=1, source_target_pairs={{4,12},{6,2},{12,20},{14,6},{20,28},{22,14},{28,24},{30,22},{24,16... | collective-permute-start | bytes 1179656 | tf_op jit(solution)/shard_map/ppermute | solution.py:376
  25.7 1.6 %shard_map.91 = (bf16[2,1536,256]{2,1,0:T(8,128)(2,1)S(1)}, f32[1536,2]{1,0:T(8,128)S(1)}) custom-call(bf16[768,256]{1,0:T(8,128)(2,1)S(1)} %collective-permute-done.5.refs_0_, bf16[768,256]{1,0:T(8,128)(2,1)S(1)} %collective-permute-done.6.refs_1_, bf16[768,256]{1,0:T(8,128)(2,1)S(1)} %get-tuple-element.86.refs_1_.refs_2_.refs_7_.refs_0_, ...), custom_call_target="tpu_custom_call" | custom-call | flops 1207959552 | bytes 4718592 | tf_op jit(solution)/shard_map/pallas_call | solution.py:46
  27.4 2.4 %collective-permute-done.7.refs_0_ = bf16[768,256]{1,0:T(8,128)(2,1)S(1)} collective-permute-done((bf16[768,256]{1,0:T(8,128)(2,1)S(1)}, bf16[768,256]{1,0:T(8,128)(2,1)S(1)}, u32[]{:S(2)}, u32[]{:S(2)}) %collective-permute-start.7) | collective-permute-done | bytes 393248 | tf_op jit(solution)/shard_map/ppermute | solution.py:376
  29.7 1.6 %collective-permute-start.9 = (bf16[768,256]{1,0:T(8,128)(2,1)S(1)}, bf16[768,256]{1,0:T(8,128)(2,1)S(1)}, u32[]{:S(2)}, u32[]{:S(2)}) collective-permute-start(bf16[768,256]{1,0:T(8,128)(2,1)S(1)} %collective-permute-done.7.refs_0_), channel_id=1, source_target_pairs={{4,12},{6,2},{12,20},{14,6},{20,28},{22,14},{28,24},{30,22},{24,16... | collective-permute-start | bytes 1179656 | tf_op jit(solution)/shard_map/ppermute | solution.py:376
  31.3 1.6 %collective-permute-start.12 = (bf16[768,256]{1,0:T(8,128)(2,1)S(1)}, bf16[768,256]{1,0:T(8,128)(2,1)S(1)}, u32[]{:S(2)}, u32[]{:S(2)}) collective-permute-start(bf16[768,256]{1,0:T(8,128)(2,1)S(1)} %get-tuple-element.86.refs_1_.refs_2_.refs_7_.refs_0_), channel_id=1, source_target_pairs={{4,12},{6,2},{12,20},{14,6},{20,28},{22,14},{28,24},{30,22},{24,16... | collective-permute-start | bytes 1179656 | tf_op jit(solution)/shard_map/ppermute | solution.py:376
  33.9 1.6 %shard_map.92 = (bf16[2,1536,256]{2,1,0:T(8,128)(2,1)S(1)}, f32[1536,2]{1,0:T(8,128)S(1)}) custom-call(bf16[768,256]{1,0:T(8,128)(2,1)S(1)} %collective-permute-done.7.refs_0_, bf16[768,256]{1,0:T(8,128)(2,1)S(1)} %collective-permute-done.8.refs_1_, bf16[768,256]{1,0:T(8,128)(2,1)S(1)} %get-tuple-element.86.refs_1_.refs_2_.refs_7_.refs_0_, ...), custom_call_target="tpu_custom_call" | custom-call | flops 1207959552 | bytes 4718592 | tf_op jit(solution)/shard_map/pallas_call | solution.py:46
  35.5 1.6 %collective-permute-start.13 = (bf16[768,256]{1,0:T(8,128)(2,1)S(1)}, bf16[768,256]{1,0:T(8,128)(2,1)S(1)}, u32[]{:S(2)}, u32[]{:S(2)}) collective-permute-start(bf16[768,256]{1,0:T(8,128)(2,1)S(1)} %collective-permute-done.refs_2_.refs_3_), channel_id=1, source_target_pairs={{4,12},{6,2},{12,20},{14,6},{20,28},{22,14},{28,24},{30,22},{24,16... | collective-permute-start | bytes 1179656 | tf_op jit(solution)/shard_map/ppermute | solution.py:376
  46.4 2.2 %shard_map.98.own_ref = f32[768,256]{1,0:T(8,128)S(1)} custom-call(bf16[1,1536,256]{2,1,0:T(8,128)(2,1)S(1)} %get-tuple-element.78.refs_0_, bf16[2,1536,256]{2,1,0:T(8,128)(2,1)S(1)} %get-tuple-element.79.refs_1_, bf16[2,1536,256]{2,1,0:T(8,128)(2,1)S(1)} %get-tuple-element.80.refs_2_, bf16[2,1536,256]{2,1,0:T(8,128)(2,1)S(1)} %get-tuple-element.81.refs_3_, ...), custom_call_target="tpu_custom_call" | custom-call | flops 1207959552 | bytes 9043968 | tf_op jit(solution)/shard_map/pallas_call | solution.py:46
  48.6 1.7 %shard_map.99.refs_5_ = f32[768,256]{1,0:T(8,128)S(1)} custom-call(bf16[768,256]{1,0:T(8,128)(2,1)S(1)} %get-tuple-element.86.refs_1_.refs_2_.refs_7_.refs_0_, bf16[1536,256]{1,0:T(8,128)(2,1)S(1)} %collective-permute-done.10.refs_0_.refs_6_.refs_1_, f32[1,768]{1,0:T(1,128)S(1)} %get-tuple-element.90.refs_2_, f32[1,768]{1,0:T(1,128)S(1)} %collective-permute-done.15.refs_3_, ...), custom_call_target="tpu_custom_call" | custom-call | flops 1207959552 | bytes 2433024 | tf_op jit(solution)/shard_map/pallas_call | solution.py:46
  51.9 1.6 %collective-permute-start.23 = (bf16[768,256]{1,0:T(8,128)(2,1)S(1)}, bf16[768,256]{1,0:T(8,128)(2,1)S(1)}, u32[]{:S(2)}, u32[]{:S(2)}) collective-permute-start(bf16[768,256]{1,0:T(8,128)(2,1)S(1)} %collective-permute-done.13.refs_2_), channel_id=1, source_target_pairs={{4,12},{6,2},{12,20},{14,6},{20,28},{22,14},{28,24},{30,22},{24,16... | collective-permute-start | bytes 1179656 | tf_op jit(solution)/shard_map/ppermute | solution.py:376
  56.3 1.6 %collective-permute-start.18 = (bf16[768,256]{1,0:T(8,128)(2,1)S(1)}, bf16[768,256]{1,0:T(8,128)(2,1)S(1)}, u32[]{:S(2)}, u32[]{:S(2)}) collective-permute-start(bf16[768,256]{1,0:T(8,128)(2,1)S(1)} %collective-permute-done.17.refs_0_), channel_id=1, source_target_pairs={{4,12},{6,2},{12,20},{14,6},{20,28},{22,14},{28,24},{30,22},{24,16... | collective-permute-start | bytes 1179656 | tf_op jit(solution)/shard_map/ppermute | solution.py:376
  57.9 1.8 %collective-permute-done.23.refs_1_ = bf16[768,256]{1,0:T(8,128)(2,1)S(1)} collective-permute-done((bf16[768,256]{1,0:T(8,128)(2,1)S(1)}, bf16[768,256]{1,0:T(8,128)(2,1)S(1)}, u32[]{:S(2)}, u32[]{:S(2)}) %collective-permute-start.23) | collective-permute-done | bytes 393248 | tf_op jit(solution)/shard_map/ppermute | solution.py:376
  59.7 1.6 %collective-permute-start.24 = (bf16[768,256]{1,0:T(8,128)(2,1)S(1)}, bf16[768,256]{1,0:T(8,128)(2,1)S(1)}, u32[]{:S(2)}, u32[]{:S(2)}) collective-permute-start(bf16[768,256]{1,0:T(8,128)(2,1)S(1)} %collective-permute-done.23.refs_1_), channel_id=1, source_target_pairs={{4,12},{6,2},{12,20},{14,6},{20,28},{22,14},{28,24},{30,22},{24,16... | collective-permute-start | bytes 1179656 | tf_op jit(solution)/shard_map/ppermute | solution.py:376
  61.3 2.0 %shard_map.100 = (f32[768,256]{1,0:T(8,128)S(1)}, f32[768,256]{1,0:T(8,128)S(1)}) custom-call(bf16[768,256]{1,0:T(8,128)(2,1)S(1)} %get-tuple-element.86.refs_1_.refs_2_.refs_7_.refs_0_, bf16[768,256]{1,0:T(8,128)(2,1)S(1)} %collective-permute-done.12.refs_1_, bf16[768,256]{1,0:T(8,128)(2,1)S(1)} %collective-permute-done.13.refs_2_, ...), custom_call_target="tpu_custom_call" | custom-call | flops 1811939328 | bytes 3588096 | tf_op jit(solution)/shard_map/pallas_call | solution.py:46
  64.4 1.6 %collective-permute-start.19 = (bf16[768,256]{1,0:T(8,128)(2,1)S(1)}, bf16[768,256]{1,0:T(8,128)(2,1)S(1)}, u32[]{:S(2)}, u32[]{:S(2)}) collective-permute-start(bf16[768,256]{1,0:T(8,128)(2,1)S(1)} %collective-permute-done.18.refs_0_), channel_id=1, source_target_pairs={{4,12},{6,2},{12,20},{14,6},{20,28},{22,14},{28,24},{30,22},{24,16... | collective-permute-start | bytes 1179656 | tf_op jit(solution)/shard_map/ppermute | solution.py:376
  70.0 3.1 %collective-permute-done.22 = f32[1,8,768]{2,1,0:T(8,128)S(1)} collective-permute-done((f32[1,8,768]{2,1,0:T(8,128)S(1)}, f32[1,8,768]{2,1,0:T(8,128)S(1)}, u32[]{:S(2)}, u32[]{:S(2)}) %collective-permute-start.22) | collective-permute-done | bytes 24608 | tf_op jit(solution)/shard_map/ppermute | solution.py:464
  73.1 1.7 %shard_map.104 = (f32[768,256]{1,0:T(8,128)S(1)}, f32[768,256]{1,0:T(8,128)}) custom-call(bf16[768,256]{1,0:T(8,128)(2,1)S(1)} %collective-permute-done.19.refs_0_, f32[8,768]{1,0:T(8,128)S(1)} %bitcast.12, f32[768,256]{1,0:T(8,128)S(1)} %get-tuple-element.103.refs_2_, f32[768,256]{1,0:T(8,128)S(1)} %get-tuple-element.104.refs_3_), custom_call_target="tpu_custom_call" | custom-call | flops 603979776 | bytes 3563520 | tf_op jit(solution)/shard_map/pallas_call | solution.py:46
  78.3 2.5 %shard_map.105 = f32[768,256]{1,0:T(8,128)} custom-call(bf16[768,256]{1,0:T(8,128)(2,1)S(1)} %copy-done.3, f32[768,256]{1,0:T(8,128)S(1)} %copy-done.5, f32[768,256]{1,0:T(8,128)} %collective-permute-done.25.other_ref), custom_call_target="tpu_custom_call" | custom-call | flops 1000000 | bytes 2752512 | tf_op jit(solution)/shard_map/pallas_call | solution.py:46
  (76 shorter events, 33.5 us)
Async XLA Ops:
  1.9 4.6 %collective-permute-start.3 = (bf16[768,256]{1,0:T(8,128)(2,1)S(1)}, bf16[768,256]{1,0:T(8,128)(2,1)}, u32[]{:S(2)}, u32[]{:S(2)}) collective-permute-start(bf16[768,256]{1,0:T(8,128)(2,1)S(1)} %shard_map.85.k_ref.refs_0_.refs_5_.refs_4_), channel_id=1, source_target_pairs={{0,2},{2,0},{4,6},{6,4},{8,10},{10,8},{12,14},{14,12},{16,18},{18,... | collective-permute-start | bytes 1179656 | tf_op jit(solution)/shard_map/ppermute | solution.py:365
  2.4 8.4 %collective-permute-start.2 = (bf16[768,256]{1,0:T(8,128)(2,1)S(1)}, bf16[768,256]{1,0:T(8,128)(2,1)S(1)}, u32[]{:S(2)}, u32[]{:S(2)}) collective-permute-start(bf16[768,256]{1,0:T(8,128)(2,1)S(1)} %shard_map.85.k_ref.refs_0_.refs_5_.refs_4_), channel_id=1, source_target_pairs={{4,12},{6,2},{12,20},{14,6},{20,28},{22,14},{28,24},{30,22},{24,16... | collective-permute-start | bytes 1179656 | tf_op jit(solution)/shard_map/ppermute | solution.py:376
  6.2 8.9 %collective-permute-start = (bf16[768,256]{1,0:T(8,128)(2,1)S(1)}, bf16[768,256]{1,0:T(8,128)(2,1)S(1)}, u32[]{:S(2)}, u32[]{:S(2)}) collective-permute-start(bf16[768,256]{1,0:T(8,128)(2,1)S(1)} %get-tuple-element.86.refs_1_.refs_2_.refs_7_.refs_0_), channel_id=1, source_target_pairs={{0,2},{2,0},{4,6},{6,4},{8,10},{10,8},{12,14},{14,12},{16,18},{18,... | collective-permute-start | bytes 1179656 | tf_op jit(solution)/shard_map/ppermute | solution.py:365
  6.5 9.6 %collective-permute-start.4 = (bf16[768,256]{1,0:T(8,128)(2,1)}, bf16[768,256]{1,0:T(8,128)(2,1)}, u32[]{:S(2)}, u32[]{:S(2)}) collective-permute-start(bf16[768,256]{1,0:T(8,128)(2,1)} %collective-permute-done.3), channel_id=1, source_target_pairs={{4,12},{6,2},{12,20},{14,6},{20,28},{22,14},{28,24},{30,22},{24,16... | collective-permute-start | bytes 1179656 | tf_op jit(solution)/shard_map/ppermute | solution.py:376
  10.8 11.1 %collective-permute-start.5 = (bf16[768,256]{1,0:T(8,128)(2,1)S(1)}, bf16[768,256]{1,0:T(8,128)(2,1)S(1)}, u32[]{:S(2)}, u32[]{:S(2)}) collective-permute-start(bf16[768,256]{1,0:T(8,128)(2,1)S(1)} %collective-permute-done.2.refs_0_), channel_id=1, source_target_pairs={{4,12},{6,2},{12,20},{14,6},{20,28},{22,14},{28,24},{30,22},{24,16... | collective-permute-start | bytes 1179656 | tf_op jit(solution)/shard_map/ppermute | solution.py:376
  16.1 8.0 %collective-permute-start.6 = (bf16[768,256]{1,0:T(8,128)(2,1)}, bf16[768,256]{1,0:T(8,128)(2,1)S(1)}, u32[]{:S(2)}, u32[]{:S(2)}) collective-permute-start(bf16[768,256]{1,0:T(8,128)(2,1)} %collective-permute-done.4.refs_1_), channel_id=1, source_target_pairs={{4,12},{6,2},{12,20},{14,6},{20,28},{22,14},{28,24},{30,22},{24,16... | collective-permute-start | bytes 1179656 | tf_op jit(solution)/shard_map/ppermute | solution.py:376
  17.7 19.4 %collective-permute-start.10 = (bf16[1536,256]{1,0:T(8,128)(2,1)S(1)}, bf16[1536,256]{1,0:T(8,128)(2,1)S(1)}, u32[]{:S(2)}, u32[]{:S(2)}) collective-permute-start(bf16[1536,256]{1,0:T(8,128)(2,1)S(1)} %get-tuple-element.69), channel_id=1, source_target_pairs={{0,1},{1,0},{2,3},{3,2},{4,5},{5,4},{6,7},{7,6},{8,9},{9,8},{10,11... | collective-permute-start | bytes 2359304 | tf_op jit(solution)/shard_map/ppermute | solution.py:381
  21.9 7.8 %collective-permute-start.7 = (bf16[768,256]{1,0:T(8,128)(2,1)S(1)}, bf16[768,256]{1,0:T(8,128)(2,1)S(1)}, u32[]{:S(2)}, u32[]{:S(2)}) collective-permute-start(bf16[768,256]{1,0:T(8,128)(2,1)S(1)} %collective-permute-done.5.refs_0_), channel_id=1, source_target_pairs={{4,12},{6,2},{12,20},{14,6},{20,28},{22,14},{28,24},{30,22},{24,16... | collective-permute-start | bytes 1179656 | tf_op jit(solution)/shard_map/ppermute | solution.py:376
  24.2 9.8 %collective-permute-start.8 = (bf16[768,256]{1,0:T(8,128)(2,1)S(1)}, bf16[768,256]{1,0:T(8,128)(2,1)S(1)}, u32[]{:S(2)}, u32[]{:S(2)}) collective-permute-start(bf16[768,256]{1,0:T(8,128)(2,1)S(1)} %collective-permute-done.6.refs_1_), channel_id=1, source_target_pairs={{4,12},{6,2},{12,20},{14,6},{20,28},{22,14},{28,24},{30,22},{24,16... | collective-permute-start | bytes 1179656 | tf_op jit(solution)/shard_map/ppermute | solution.py:376
  29.7 8.6 %collective-permute-start.9 = (bf16[768,256]{1,0:T(8,128)(2,1)S(1)}, bf16[768,256]{1,0:T(8,128)(2,1)S(1)}, u32[]{:S(2)}, u32[]{:S(2)}) collective-permute-start(bf16[768,256]{1,0:T(8,128)(2,1)S(1)} %collective-permute-done.7.refs_0_), channel_id=1, source_target_pairs={{4,12},{6,2},{12,20},{14,6},{20,28},{22,14},{28,24},{30,22},{24,16... | collective-permute-start | bytes 1179656 | tf_op jit(solution)/shard_map/ppermute | solution.py:376
  31.3 12.2 %collective-permute-start.12 = (bf16[768,256]{1,0:T(8,128)(2,1)S(1)}, bf16[768,256]{1,0:T(8,128)(2,1)S(1)}, u32[]{:S(2)}, u32[]{:S(2)}) collective-permute-start(bf16[768,256]{1,0:T(8,128)(2,1)S(1)} %get-tuple-element.86.refs_1_.refs_2_.refs_7_.refs_0_), channel_id=1, source_target_pairs={{4,12},{6,2},{12,20},{14,6},{20,28},{22,14},{28,24},{30,22},{24,16... | collective-permute-start | bytes 1179656 | tf_op jit(solution)/shard_map/ppermute | solution.py:376
  35.5 16.4 %collective-permute-start.13 = (bf16[768,256]{1,0:T(8,128)(2,1)S(1)}, bf16[768,256]{1,0:T(8,128)(2,1)S(1)}, u32[]{:S(2)}, u32[]{:S(2)}) collective-permute-start(bf16[768,256]{1,0:T(8,128)(2,1)S(1)} %collective-permute-done.refs_2_.refs_3_), channel_id=1, source_target_pairs={{4,12},{6,2},{12,20},{14,6},{20,28},{22,14},{28,24},{30,22},{24,16... | collective-permute-start | bytes 1179656 | tf_op jit(solution)/shard_map/ppermute | solution.py:376
  42.7 33.6 %collective-permute-start.16 = (f32[768,256]{1,0:T(8,128)S(1)}, f32[768,256]{1,0:T(8,128)S(1)}, u32[]{:S(2)}, u32[]{:S(2)}) collective-permute-start(f32[768,256]{1,0:T(8,128)S(1)} %shard_map.97), channel_id=1, source_target_pairs={{0,2},{2,0},{4,6},{6,4},{8,10},{10,8},{12,14},{14,12},{16,18},{18,... | collective-permute-start | bytes 2359304 | tf_op jit(solution)/shard_map/ppermute | solution.py:365
  42.9 5.7 %collective-permute-start.15 = (f32[1,768]{1,0:T(1,128)S(1)}, f32[1,768]{1,0:T(1,128)S(1)}, u32[]{:S(2)}, u32[]{:S(2)}) collective-permute-start(f32[1,768]{1,0:T(1,128)S(1)} %get-tuple-element.90.refs_2_), channel_id=1, source_target_pairs={{0,1},{1,0},{2,3},{3,2},{4,5},{5,4},{6,7},{7,6},{8,9},{9,8},{10,11... | collective-permute-start | bytes 9224 | tf_op jit(solution)/shard_map/ppermute | solution.py:381
  43.5 6.9 %collective-permute-start.14 = (f32[4,8,768]{2,1,0:T(8,128)S(1)}, f32[4,8,768]{2,1,0:T(8,128)S(1)}, u32[]{:S(2)}, u32[]{:S(2)}) collective-permute-start(f32[4,8,768]{2,1,0:T(8,128)S(1)} %get-tuple-element.89), channel_id=1, source_target_pairs={{4,12},{6,2},{12,20},{14,6},{20,28},{22,14},{28,24},{30,22},{24,16... | collective-permute-start | bytes 294920 | tf_op jit(solution)/shard_map/ppermute | solution.py:464
  45.0 11.2 %collective-permute-start.17 = (bf16[768,256]{1,0:T(8,128)(2,1)S(1)}, bf16[768,256]{1,0:T(8,128)(2,1)S(1)}, u32[]{:S(2)}, u32[]{:S(2)}) collective-permute-start(bf16[768,256]{1,0:T(8,128)(2,1)S(1)} %collective-permute-done.12.refs_1_), channel_id=1, source_target_pairs={{4,12},{6,2},{12,20},{14,6},{20,28},{22,14},{28,24},{30,22},{24,16... | collective-permute-start | bytes 1179656 | tf_op jit(solution)/shard_map/ppermute | solution.py:376
  50.4 4.4 %collective-permute-start.20 = (f32[3,8,768]{2,1,0:T(8,128)S(1)}, f32[3,8,768]{2,1,0:T(8,128)S(1)}, u32[]{:S(2)}, u32[]{:S(2)}) collective-permute-start(f32[3,8,768]{2,1,0:T(8,128)S(1)} %slice.25), channel_id=1, source_target_pairs={{4,12},{6,2},{12,20},{14,6},{20,28},{22,14},{28,24},{30,22},{24,16... | collective-permute-start | bytes 221192 | tf_op jit(solution)/shard_map/ppermute | solution.py:464
  51.9 7.8 %collective-permute-start.23 = (bf16[768,256]{1,0:T(8,128)(2,1)S(1)}, bf16[768,256]{1,0:T(8,128)(2,1)S(1)}, u32[]{:S(2)}, u32[]{:S(2)}) collective-permute-start(bf16[768,256]{1,0:T(8,128)(2,1)S(1)} %collective-permute-done.13.refs_2_), channel_id=1, source_target_pairs={{4,12},{6,2},{12,20},{14,6},{20,28},{22,14},{28,24},{30,22},{24,16... | collective-permute-start | bytes 1179656 | tf_op jit(solution)/shard_map/ppermute | solution.py:376
  54.8 11.2 %collective-permute-start.21 = (f32[2,8,768]{2,1,0:T(8,128)S(1)}, f32[2,8,768]{2,1,0:T(8,128)S(1)}, u32[]{:S(2)}, u32[]{:S(2)}) collective-permute-start(f32[2,8,768]{2,1,0:T(8,128)S(1)} %slice.26), channel_id=1, source_target_pairs={{4,12},{6,2},{12,20},{14,6},{20,28},{22,14},{28,24},{30,22},{24,16... | collective-permute-start | bytes 147464 | tf_op jit(solution)/shard_map/ppermute | solution.py:464
  56.3 8.2 %collective-permute-start.18 = (bf16[768,256]{1,0:T(8,128)(2,1)S(1)}, bf16[768,256]{1,0:T(8,128)(2,1)S(1)}, u32[]{:S(2)}, u32[]{:S(2)}) collective-permute-start(bf16[768,256]{1,0:T(8,128)(2,1)S(1)} %collective-permute-done.17.refs_0_), channel_id=1, source_target_pairs={{4,12},{6,2},{12,20},{14,6},{20,28},{22,14},{28,24},{30,22},{24,16... | collective-permute-start | bytes 1179656 | tf_op jit(solution)/shard_map/ppermute | solution.py:376
  59.7 9.0 %collective-permute-start.24 = (bf16[768,256]{1,0:T(8,128)(2,1)S(1)}, bf16[768,256]{1,0:T(8,128)(2,1)S(1)}, u32[]{:S(2)}, u32[]{:S(2)}) collective-permute-start(bf16[768,256]{1,0:T(8,128)(2,1)S(1)} %collective-permute-done.23.refs_1_), channel_id=1, source_target_pairs={{4,12},{6,2},{12,20},{14,6},{20,28},{22,14},{28,24},{30,22},{24,16... | collective-permute-start | bytes 1179656 | tf_op jit(solution)/shard_map/ppermute | solution.py:376
  64.4 8.7 %collective-permute-start.19 = (bf16[768,256]{1,0:T(8,128)(2,1)S(1)}, bf16[768,256]{1,0:T(8,128)(2,1)S(1)}, u32[]{:S(2)}, u32[]{:S(2)}) collective-permute-start(bf16[768,256]{1,0:T(8,128)(2,1)S(1)} %collective-permute-done.18.refs_0_), channel_id=1, source_target_pairs={{4,12},{6,2},{12,20},{14,6},{20,28},{22,14},{28,24},{30,22},{24,16... | collective-permute-start | bytes 1179656 | tf_op jit(solution)/shard_map/ppermute | solution.py:376
  66.0 7.1 %collective-permute-start.22 = (f32[1,8,768]{2,1,0:T(8,128)S(1)}, f32[1,8,768]{2,1,0:T(8,128)S(1)}, u32[]{:S(2)}, u32[]{:S(2)}) collective-permute-start(f32[1,8,768]{2,1,0:T(8,128)S(1)} %get-tuple-element.108), channel_id=1, source_target_pairs={{4,12},{6,2},{12,20},{14,6},{20,28},{22,14},{28,24},{30,22},{24,16... | collective-permute-start | bytes 73736 | tf_op jit(solution)/shard_map/ppermute | solution.py:464
  75.7 2.6 %collective-permute-start.25 = (f32[768,256]{1,0:T(8,128)}, f32[768,256]{1,0:T(8,128)}, u32[]{:S(2)}, u32[]{:S(2)}) collective-permute-start(f32[768,256]{1,0:T(8,128)} %get-tuple-element.106), channel_id=1, source_target_pairs={{0,2},{2,0},{4,6},{6,4},{8,10},{10,8},{12,14},{14,12},{16,18},{18,... | collective-permute-start | bytes 2359304 | tf_op jit(solution)/shard_map/ppermute | solution.py:365
  (12 other events, 61.1 us)

commit v5 on v4

--- a/solution.py
+++ b/solution.py
@@ -12,7 +12,8 @@
 EPS = 1e-06
 F32 = jnp.float32
 BF16 = jnp.bfloat16
-COST = 1.0
+CODE_BASE = 32.0
+HEAVY = 3e9
 SPARE_BYTES = 6 * 1024 * 1024
 
 
@@ -49,12 +50,16 @@
         in_specs=specs,
         out_specs=[pl.BlockSpec(memory_space=pltpu.VMEM)] * len(outs),
         compiler_params=pltpu.CompilerParams(vmem_limit_bytes=moved + SPARE_BYTES),
-        cost_estimate=pl.CostEstimate(flops=int(flops * COST), bytes_accessed=int(moved * COST), transcendentals=0),
+        cost_estimate=pl.CostEstimate(flops=int(flops), bytes_accessed=moved, transcendentals=0),
     )(*operands)
 
 
 def shape(dims, dtype=F32):
     return jax.ShapeDtypeStruct(dims, dtype)
+
+
+def message_rows(middle):
+    return -(-(12 * (middle - 1) + 6) // 16) * 16
 
 
 def unit_of(rows):
@@ -87,23 +92,16 @@
     unit_ref[...] = unit_of(x_ref[...])[0].astype(BF16)
 
 
-def unit_both_kernel(x_ref, k_ref, unit_ref, both_ref):
-    unit_kernel(x_ref, unit_ref)
-    rows = x_ref.shape[0]
-    both_ref[:rows, :] = k_ref[...]
-    both_ref[rows:, :] = unit_ref[...]
-
-
 def codes_kernel(
-    me_ref, table_ref, owner_ref, row_ref, count_ref, codes_ref, inverse_ref, columns_ref
+    table_ref, owner_ref, row_ref, count_ref, codes_ref, inverse_ref, columns_ref
 ):
     slots = owner_ref.shape[0]
     places = codes_ref.shape[0] - 1
-    count = count_ref[...]
+    count = count_ref[...].reshape(1, count_ref.shape[0])
     inverse = 1.0 / (1.0 + count.astype(F32))
     inverse_ref[...] = inverse
     codes_ref[places : places + 1, :] = inverse
-    me = me_ref[0]
+    me = lax.axis_index("sky")
     for place in range(places):
         owner = table_ref[me, place]
         code = jnp.full(count.shape, -1, jnp.int32)
@@ -115,7 +113,7 @@
 
 
 def group_forward_kernel(groups, k_ref, *refs):
-    both = refs[: groups - 1]
+    others = refs[: groups - 1]
     q_ref, total_ref, diag_ref = refs[groups - 1 :]
     anchors = q_ref.shape[0]
     step = 256
@@ -123,7 +121,7 @@
         q = q_ref[start : start + step, :]
         total = jnp.zeros((1, step), F32)
         for index in range(groups):
-            keys = both[index - 1][:anchors, :] if index else k_ref[...]
+            keys = others[index - 1][...] if index else k_ref[...]
             scores = SCALE * dot_t(keys, q)
             total += jnp.sum(jnp.exp(scores), axis=0, keepdims=True)
             if index == 0:
@@ -231,16 +229,31 @@
     def both_sides(slot):
         return [row(near_code, slot), row(far_code, slot), row(near, slot), row(far, slot)]
 
-    home_ref[:4, :] = jnp.concatenate(both_sides(0), axis=0)
-    home_ref[4:, :] = jnp.zeros((4, anchors), F32)
+    home_ref[...] = jnp.concatenate(both_sides(0), axis=0)
+    def coded(codes, weights):
+        high = [jnp.floor(code / CODE_BASE) for code in codes]
+        return high + [code - CODE_BASE * h for code, h in zip(codes, high)] + weights
+
+    rows = []
     for slot in range(2, chips - 1, 2):
-        rows = []
         for codes, weights in ((far_code, far), (sib_far_code, sib_far)):
-            rows += [row(codes, slot), row(codes, slot - 1)]
-            rows += [row(weights, slot), row(weights, slot - 1)]
-        message_ref[slot // 2 - 1] = jnp.concatenate(rows, axis=0)
-    last = both_sides(chips - 1) + [jnp.zeros((4, anchors), F32)]
-    message_ref[chips // 2 - 1] = jnp.concatenate(last, axis=0)
+            pair = (slot, slot - 1)
+            rows += coded([row(codes, at) for at in pair], [row(weights, at) for at in pair])
+    codes = [row(near_code, chips - 1), row(sib_near_code, chips - 1)]
+    rows += coded(codes, [row(near, chips - 1), row(sib_near, chips - 1)])
+    number = message_rows(chips // 2)
+    rows.append(jnp.zeros((number - len(rows), anchors), F32))
+    block = jnp.concatenate(rows, axis=0).astype(BF16)
+    width = message_ref.shape[1]
+    for index in range(anchors // width):
+        part = block[:, index * width : (index + 1) * width]
+        message_ref[index * number : (index + 1) * number, :] = part
+
+
+def carrier_kernel(block_ref, message_ref, out_ref):
+    rows = block_ref.shape[0]
+    out_ref[:rows, :] = block_ref[...]
+    out_ref[rows:, :] = message_ref[...]
 
 
 def partner_sum(columns, order, named, rows):
@@ -272,7 +285,7 @@
     order, named = named_rows(batches, refs)
     rest = refs[len(batches) :]
     k_ref, rest = rest[0], rest[1:]
-    both, rest = rest[: groups - 1], rest[groups - 1 :]
+    others, rest = rest[: groups - 1], rest[groups - 1 :]
     q_ref, columns_ref, out_ref = rest
     anchors = q_ref.shape[0]
     chips = len(order)
@@ -285,7 +298,7 @@
         log_total = columns[:, chips : chips + 1]
         inverse = columns[:, chips + 1 : chips + 2]
         for index in range(groups):
-            keys = both[index - 1][:anchors, :] if index else k_ref[...]
+            keys = others[index - 1][...] if index else k_ref[...]
             scores = SCALE * dot_t(q, keys)
             weights = jnp.exp(scores - log_total)
             if index == 0:
@@ -295,13 +308,14 @@
         out_ref[rows, :] = total
 
 
-def finish_kernel(x_ref, own_ref, other_ref, out_ref):
+def grad_query_finish_kernel(x_ref, own_ref, other_ref, row_ref, out_ref, loss_ref):
     unit, norms = unit_of(x_ref[...])
     out_ref[...] = back_unit(unit, norms, SCALE * (own_ref[...] + other_ref[...]))
+    loss_ref[...] = row_ref[...].reshape(loss_ref.shape[0])
 
 
 def group_key_kernel(groups, *refs):
-    q_ref, both, logs = refs[0], refs[1:groups], refs[groups : 2 * groups]
+    q_ref, others, logs = refs[0], refs[1:groups], refs[groups : 2 * groups]
     k_ref, inv_ref, out_ref = refs[2 * groups :]
     anchors, width = k_ref.shape
     step = 256
@@ -309,7 +323,7 @@
         rows = slice(start, start + step)
         total = jnp.zeros((step, width), F32)
         for index in range(groups):
-            q = both[index - 1][anchors:, :] if index else q_ref[...]
+            q = others[index - 1][...] if index else q_ref[...]
             scores = SCALE * dot_t(k_ref[rows, :], q)
             weights = jnp.exp(scores - logs[index][...])
             if index == 0:
@@ -319,20 +333,62 @@
         out_ref[rows, :] = total
 
 
-def grad_key_kernel(sources, blocks, carried, *refs):
+def grad_key_finish_kernel(
+    number,
+    first,
+    x_ref,
+    group_ref,
+    own_ref,
+    other_ref,
+    near_ref,
+    far_ref,
+    message_ref,
+    out_ref,
+):
+    anchors, width = out_ref.shape
+    step = 256
+    told = read_message(message_ref, 0, number, first, anchors)
+    for start in range(0, anchors, step):
+        rows = slice(start, start + step)
+        total = group_ref[rows, :] + own_ref[rows, :] + other_ref[rows, :]
+        for side, block in enumerate((near_ref, far_ref)):
+            code = told[side : side + 1, :]
+            weight = told[2 + side : 3 + side, :]
+            spread = jnp.where(row_ids(step, anchors, start) == code, weight, 0.0)
+            total += dot(spread.astype(BF16), block[:anchors, :])
+        unit, norms = unit_of(x_ref[rows, :])
+        out_ref[rows, :] = back_unit(unit, norms, SCALE * total)
+
+
+def read_message(ref, begin, number, first, anchors):
+    parts = []
+    for index in range(anchors // ref.shape[1]):
+        start = begin + index * number
+        part = ref[start : start + number, :].astype(F32)[first : first + 6, :]
+        parts.append(jnp.concatenate([CODE_BASE * part[:2, :] + part[2:4, :], part[4:6, :]], axis=0))
+    return jnp.concatenate(parts, axis=1)
+
+
+def grad_key_kernel(sources, blocks, carried, number, *refs):
     queries, messages = refs[:blocks], refs[blocks : -2 - carried]
     so_far, outs = refs[len(refs) - 2 - carried : len(refs) - 2], refs[-2:]
     anchors, width = outs[0].shape
     step = 256
+    told = [
+        read_message(messages[at], anchors, number, 12 * distance - 12 + 6 * half, anchors)
+        if distance
+        else messages[at][...]
+        for at, distance, half in sources
+    ]
     for side, out in enumerate(outs):
         for start in range(0, anchors, step):
             rows = slice(start, start + step)
             total = so_far[side][rows, :] if side < carried else jnp.zeros((step, width), F32)
-            for (at, base), block in zip(sources, queries):
-                code = messages[at][base + side : base + side + 1, :]
-                weight = messages[at][base + 2 + side : base + 3 + side, :]
+            for message, block in zip(told, queries):
+                code = message[side : side + 1, :]
+                weight = message[2 + side : 3 + side, :]
                 spread = jnp.where(row_ids(step, anchors, start) == code, weight, 0.0)
-                total += dot(spread.astype(BF16), block[...])
+                total += dot(spread.astype(BF16), block[:anchors, :])
             out[rows, :] = total
 
 
@@ -380,32 +436,25 @@
         shifts = [[(i, (i + s) % loop) for i in range(loop)] for s in range(1, loop)]
         return [lax.ppermute(x, "loop", pairs) for pairs in shifts]
 
-    me = lax.axis_index("sky").reshape(1).astype(jnp.int32)
-    where = [me, jnp.asarray(table)]
     block = shape((anchors, width), BF16)
     one_block = 2 * anchors * anchors * width
     (key_rows,) = call(unit_kernel, [block], [keys], 5 * keys.size)
     key_ring = Ring(key_rows, swap(key_rows))
     key_ring.hop(0)
-    query_rows, both = call(
-        unit_both_kernel,
-        [block, shape((2 * anchors, width), BF16)],
-        [queries, key_rows],
-        5 * queries.size,
-    )
-    key_ring.hop(1)
-    sib_queries = swap(query_rows)
-    query_ring = Ring(query_rows, sib_queries)
-    others = group(both)
+    (query_rows,) = call(unit_kernel, [block], [queries], 5 * queries.size)
     codes, inverse, code_columns = call(
         codes_kernel,
         [shape((sky + 1, anchors)), shape((1, anchors)), shape((anchors, sky + 1))],
-        where + [partner_owner.T, partner_row.T, partner_count.reshape(1, anchors)],
+        [jnp.asarray(table), partner_owner.T, partner_row.T, partner_count],
         1e6,
-        smem=(0, 1),
-    )
+        smem=(0,),
+    )
+    key_ring.hop(1, codes)
+    sib_queries = swap(query_rows)
+    query_ring = Ring(query_rows, sib_queries)
     sib_codes = swap(codes)
     (sib_code_columns,) = call(turn_kernel, [shape((anchors, sky + 1))], [sib_codes], 1e6)
+    group_keys = group(key_rows)
 
     def partners_of(batch, *pins):
         return call(
@@ -417,28 +466,27 @@
         )
 
     batches = [[0]] + [[2 * s - 1, 2 * s] for s in range(1, middle)] + [[chips - 1]]
-    parts = []
-    pins = ()
-    for step in range(2, middle + 1):
-        incoming = key_ring.front[0]
-        key_ring.hop(0, *pins)
-        if step == 2:
-            parts.append(partners_of(batches[0]))
-            pins = (parts[-1][1],)
+    ring = key_ring.blocks
+    key_ring.hop(0)
+    parts = [partners_of(batches[0], ring[1])]
+    key_ring.hop(1, parts[-1][1])
+    parts.append(partners_of(batches[1], parts[-1][1]))
+    group_queries = group(after(query_rows, parts[-1][1]))
+    for step in range(3, middle + 1):
+        key_ring.hop(0, parts[-1][1])
         if step < middle:
-            key_ring.hop(1, *pins)
-            parts.append(partners_of(batches[step - 1], *pins))
-            pins = (parts[-1][1],)
-    query_ring.hop(0, incoming)
-    parts.append(partners_of(batches[middle - 1], *pins))
-    query_ring.hop(1, parts[-1][1])
+            parts.append(partners_of(batches[step - 1], parts[-1][1], ring[2 * step - 2]))
+            key_ring.hop(1, parts[-1][1])
     group_total, diag = call(
         functools.partial(group_forward_kernel, loop),
         [shape((1, anchors))] * 2,
-        [key_rows] + others + [after(query_rows, parts[-1][1])],
+        [key_rows] + group_keys + [after(query_rows, parts[-1][1], ring[chips - 3])],
         loop * one_block,
     )
-    parts.append(partners_of(batches[middle], group_total))
+    query_ring.hop(0, group_total)
+    parts.append(partners_of(batches[middle - 1], group_total))
+    query_ring.hop(1, parts[-1][1])
+    parts.append(partners_of(batches[middle], parts[-1][1]))
     logits, payload = call(
         totals_kernel,
         [shape((chips, 2 * anchors)), shape((2 * chips + 1, anchors))],
@@ -446,47 +494,48 @@
         1e6,
     )
     other = swap(payload)
+    ring = query_ring.blocks
+    each = message_rows(middle)
+    rows = each * (anchors // width)
     loss, log_total, home, message, columns, sib_columns = call(
         weights_kernel,
         [
             shape((1, anchors)),
             shape((1, anchors)),
-            shape((8, anchors)),
-            shape((middle, 8, anchors)),
+            shape((4, anchors)),
+            shape((rows, width), BF16),
             shape((anchors, chips + 8)),
             shape((anchors, chips)),
         ],
         [logits, other, codes, sib_codes, group_total, diag],
         1e6,
     )
-    arrived = []
-    for step in range(middle):
-        message = lax.ppermute(message, "sky", onward)
-        arrived.append(message[0])
-        message = message[1:]
+    (query_ring.front[0],) = call(
+        carrier_kernel, [shape((anchors + rows, width), BF16)], [after(ring[1]), message], 1e6
+    )
+    query_ring.hop(0)
 
     def grad_keys_of(steps, sums, *pins):
         blocks, sources, messages = [], [], []
         for step in steps:
-            slots = [0] if step == 0 else [chips - 1] if step == middle else [2 * step - 1, 2 * step]
-            for half, slot in enumerate(slots):
-                blocks.append(query_ring.blocks[slot])
-                sources.append((len(messages), 4 * half))
-            messages.append(arrived[step - 1] if step else home)
+            for half, slot in enumerate([2 * step - 1, 2 * step] if step else [0]):
+                blocks.append(ring[slot])
+                sources.append((len(messages), step, half))
+            messages.append(ring[min(2 * step + 1, chips - 1)] if step else home)
+        blocks[0] = after(blocks[0], *pins)
         return call(
-            functools.partial(grad_key_kernel, sources, len(blocks), len(sums)),
+            functools.partial(grad_key_kernel, sources, len(blocks), len(sums), each),
             [shape((anchors, width))] * 2,
-            blocks + messages + [after(sums[0], *pins)] + list(sums[1:]),
+            blocks + messages + list(sums),
             2 * len(blocks) * one_block,
         )
 
-    query_ring.hop(0, log_total)
     all_logs = [log_total] + group(log_total)
     (sib_summed_q,) = call(
         functools.partial(grad_sibling_kernel, batches),
         [shape((anchors, width))],
-        [part[0] for part in parts] + [sib_columns],
-        1e6,
+        [part[0] for part in parts] + [after(sib_columns, ring[2])],
+        HEAVY,
     )
     query_ring.hop(1, sib_summed_q)
     for step in range(3, middle):
@@ -498,35 +547,42 @@
         [shape((anchors, width))],
         [part[0] for part in parts]
         + [key_rows]
-        + others
+        + group_keys
         + [after(query_rows, sib_summed_q), columns],
         2 * loop * one_block,
     )
     query_ring.hop(0, summed_q)
+    summed_k = grad_keys_of([0, 1], [], summed_q)
+    query_ring.hop(1)
     (group_k,) = call(
         functools.partial(group_key_kernel, loop),
         [shape((anchors, width))],
-        [query_rows] + others + all_logs + [after(key_rows, summed_q), inverse],
+        [query_rows] + group_queries + all_logs + [after(key_rows, summed_k[0]), inverse],
         2 * loop * one_block,
     )
-    query_ring.hop(1, group_k)
-    summed_k = grad_keys_of([0, 1], [group_k])
-    query_ring.hop(0, summed_k[0])
-    (grad_queries,) = call(
-        finish_kernel,
+    query_ring.hop(0)
+    for step in range(2, middle - 1):
+        summed_k = grad_keys_of([step], summed_k, group_k)
+    (grad_queries, loss) = call(
+        grad_query_finish_kernel,
+        [shape((anchors, width)), shape((anchors,))],
+        [queries, after(summed_q, summed_k[0]), swap(sib_summed_q), loss],
+        1e6,
+    )
+    first = 12 * (middle - 1)
+    skip = first // 16 * 16
+    opposite = ring[-1][anchors:].reshape(anchors // width, each, width)[:, skip:]
+    opposite = lax.ppermute(opposite.reshape(-1, width), "sky", onward)
+    facing = swap(ring[-1])
+    summed_k = grad_keys_of([middle - 1], summed_k, grad_queries, opposite)
+    (grad_keys,) = call(
+        functools.partial(grad_key_finish_kernel, each - skip, first - skip),
         [shape((anchors, width))],
-        [queries, after(summed_q, summed_k[0]), swap(sib_summed_q)],
-        1e6,
-    )
-    for step in range(2, middle + 1):
-        summed_k = grad_keys_of([step], summed_k)
-    (grad_keys,) = call(
-        finish_kernel,
-        [shape((anchors, width))],
-        [keys, summed_k[0], swap(summed_k[1])],
-        1e6,
-    )
-    return (loss.reshape(anchors), grad_queries, grad_keys)
+        [keys, group_k, summed_k[0], swap(summed_k[1]), ring[-1], facing]
+        + [opposite],
+        2 * one_block,
+    )
+    return (loss, grad_queries, grad_keys)
 
 
 def solution(mesh):

time: 81.1 us -> 80 us (0.986)
  waiting for transfers between devices: 17.8 us -> 21 us
  Pallas kernels: 26.6 us -> 23.5 us
  local copies, waits for them, and re-layouts: 2.94 us -> 2.02 us
    ppermute x14, waiting for transfers between devices: 10.3 us -> 16 us  [hop(): lax.ppermute(after(self.front[which], *pins), 'sky', onward)]
    ppermute x4 -> x1, waiting for transfers between devices: 4.36 us -> 0.01 us  [shards(): opposite = lax.ppermute(opposite.reshape(-1, width), 'sky', onward)]
    ppermute x4 -> x1, starting transfers between devices: 5.34 us -> 1.63 us  [shards(): opposite = lax.ppermute(opposite.reshape(-1, width), 'sky', onward)]
    pallas_call x21, Pallas kernels: 26.6 us -> 23.5 us  [call(): pl.pallas_call(kernel, out_shape=list(outs), in_specs=specs, out_specs=[p...]
    ppermute x2 -> x3, starting transfers between devices: 2.1 us -> 4.47 us  [group(): return [lax.ppermute(x, 'loop', pairs) for pairs in shifts]]
    ppermute x6 -> x7, waiting for transfers between devices: 3.16 us -> 4.97 us  [swap(): return lax.ppermute(x, 'sky', siblings)]
    ppermute x14, starting transfers between devices: 23.3 us -> 24.9 us  [hop(): lax.ppermute(after(self.front[which], *pins), 'sky', onward)]
    unnamed x20 -> x16, local copies, waits for them, and re-layouts: 2.91 us -> 2.01 us
  transfers between devices with their start and end apart: 26 -> 25, of which waited for: 12 -> 14; matrix products, arithmetic and copies ran while one was open for 1% -> 0% of each run, Pallas kernels for 30% -> 25%
where the time goes in v5:
time: 80 us; the launch traced here: 79.8 us
  starting transfers between devices  32.4 us (40%)
  Pallas kernels  23.5 us (29%)
  waiting for transfers between devices  21 us (26%)
  local copies, waits for them, and re-layouts  2.02 us (3%)
  between operations  0.88 us (1%)
    ppermute x14, starting transfers between devices, hop(): lax.ppermute(after(self.front[which], *pins), 'sky', onward)  24.9 us
    pallas_call x21, Pallas kernels, call(): pl.pallas_call(kernel, out_shape=list(outs), in_specs=specs, out_specs=[p...  23.5 us
    ppermute x14, waiting for transfers between devices, hop(): lax.ppermute(after(self.front[which], *pins), 'sky', onward)  16 us
    ppermute x7, waiting for transfers between devices, swap(): return lax.ppermute(x, 'sky', siblings)  4.97 us
    ppermute x3, starting transfers between devices, group(): return [lax.ppermute(x, 'loop', pairs) for pairs in shifts]  4.47 us
    unnamed x16, local copies, waits for them, and re-layouts  2.01 us
    ppermute x1, starting transfers between devices, shards(): opposite = lax.ppermute(opposite.reshape(-1, width), 'sky', onward)  1.63 us
  transfers between devices with their start and end apart: 25, of which 14 were waited for; matrix products, arithmetic and copies ran while one was open for 0% of the time, Pallas kernels for 25%

profile of v5, /device:TPU:0, one launch (start us, length us, event | category | flops | bytes accessed | tf_op | source)
XLA Modules:
  0.0 79.8 jit_solution(15153363462030393749)
XLA Ops:
  2.4 2.6 %collective-permute-start = (bf16[768,256]{1,0:T(8,128)(2,1)S(1)}, bf16[768,256]{1,0:T(8,128)(2,1)S(1)}, u32[]{:S(2)}, u32[]{:S(2)}) collective-permute-start(bf16[768,256]{1,0:T(8,128)(2,1)S(1)} %shard_map.85.refs_0_.k_ref.refs_5_.refs_4_), channel_id=1, source_target_pairs={{4,12},{6,2},{12,20},{14,6},{20,28},{22,14},{28,24},{30,22},{24,16... | collective-permute-start | bytes 1179656 | tf_op jit(solution)/shard_map/ppermute | solution.py:432
  10.8 2.0 %collective-permute-start.5 = (bf16[768,256]{1,0:T(8,128)(2,1)S(1)}, bf16[768,256]{1,0:T(8,128)(2,1)S(1)}, u32[]{:S(2)}, u32[]{:S(2)}) collective-permute-start(bf16[768,256]{1,0:T(8,128)(2,1)S(1)} %collective-permute-done.refs_0_), channel_id=1, source_target_pairs={{4,12},{6,2},{12,20},{14,6},{20,28},{22,14},{28,24},{30,22},{24,16... | collective-permute-start | bytes 1179656 | tf_op jit(solution)/shard_map/ppermute | solution.py:432
  15.3 1.7 %collective-permute-start.6 = (bf16[768,256]{1,0:T(8,128)(2,1)S(1)}, bf16[768,256]{1,0:T(8,128)(2,1)S(1)}, u32[]{:S(2)}, u32[]{:S(2)}) collective-permute-start(bf16[768,256]{1,0:T(8,128)(2,1)S(1)} %collective-permute-done.4.refs_1_), channel_id=1, source_target_pairs={{4,12},{6,2},{12,20},{14,6},{20,28},{22,14},{28,24},{30,22},{24,16... | collective-permute-start | bytes 1179656 | tf_op jit(solution)/shard_map/ppermute | solution.py:432
  18.5 1.6 %shard_map.90 = (bf16[2,1536,256]{2,1,0:T(8,128)(2,1)S(1)}, f32[1536,2]{1,0:T(8,128)S(1)}) custom-call(bf16[768,256]{1,0:T(8,128)(2,1)S(1)} %collective-permute-done.refs_0_, bf16[768,256]{1,0:T(8,128)(2,1)S(1)} %collective-permute-done.4.refs_1_, bf16[768,256]{1,0:T(8,128)(2,1)S(1)} %shard_map.86.refs_1_.refs_2_.refs_7_.refs_0_, ...), custom_call_target="tpu_custom_call" | custom-call | flops 1207959552 | bytes 4718592 | tf_op jit(solution)/shard_map/pallas_call | solution.py:47
  20.1 1.6 %collective-permute-start.7 = (bf16[768,256]{1,0:T(8,128)(2,1)S(1)}, bf16[768,256]{1,0:T(8,128)(2,1)S(1)}, u32[]{:S(2)}, u32[]{:S(2)}) collective-permute-start(bf16[768,256]{1,0:T(8,128)(2,1)S(1)} %collective-permute-done.5.refs_0_), channel_id=1, source_target_pairs={{4,12},{6,2},{12,20},{14,6},{20,28},{22,14},{28,24},{30,22},{24,16... | collective-permute-start | bytes 1179656 | tf_op jit(solution)/shard_map/ppermute | solution.py:432
  21.7 2.0 %collective-permute-done.6.refs_1_ = bf16[768,256]{1,0:T(8,128)(2,1)S(1)} collective-permute-done((bf16[768,256]{1,0:T(8,128)(2,1)S(1)}, bf16[768,256]{1,0:T(8,128)(2,1)S(1)}, u32[]{:S(2)}, u32[]{:S(2)}) %collective-permute-start.6) | collective-permute-done | bytes 393248 | tf_op jit(solution)/shard_map/ppermute | solution.py:432
  23.7 1.6 %shard_map.91 = (bf16[2,1536,256]{2,1,0:T(8,128)(2,1)S(1)}, f32[1536,2]{1,0:T(8,128)S(1)}) custom-call(bf16[768,256]{1,0:T(8,128)(2,1)S(1)} %collective-permute-done.5.refs_0_, bf16[768,256]{1,0:T(8,128)(2,1)S(1)} %collective-permute-done.6.refs_1_, bf16[768,256]{1,0:T(8,128)(2,1)S(1)} %shard_map.86.refs_1_.refs_2_.refs_7_.refs_0_, ...), custom_call_target="tpu_custom_call" | custom-call | flops 1207959552 | bytes 4718592 | tf_op jit(solution)/shard_map/pallas_call | solution.py:47
  25.3 1.8 %collective-permute-start.8 = (bf16[768,256]{1,0:T(8,128)(2,1)S(1)}, bf16[768,256]{1,0:T(8,128)(2,1)S(1)}, u32[]{:S(2)}, u32[]{:S(2)}) collective-permute-start(bf16[768,256]{1,0:T(8,128)(2,1)S(1)} %collective-permute-done.6.refs_1_), channel_id=1, source_target_pairs={{4,12},{6,2},{12,20},{14,6},{20,28},{22,14},{28,24},{30,22},{24,16... | collective-permute-start | bytes 1179656 | tf_op jit(solution)/shard_map/ppermute | solution.py:432
  27.9 1.7 %collective-permute-start.10 = (bf16[768,256]{1,0:T(8,128)(2,1)S(1)}, bf16[768,256]{1,0:T(8,128)(2,1)S(1)}, u32[]{:S(2)}, u32[]{:S(2)}) collective-permute-start(bf16[768,256]{1,0:T(8,128)(2,1)S(1)} %collective-permute-done.7.refs_0_), channel_id=1, source_target_pairs={{4,12},{6,2},{12,20},{14,6},{20,28},{22,14},{28,24},{30,22},{24,16... | collective-permute-start | bytes 1179656 | tf_op jit(solution)/shard_map/ppermute | solution.py:432
  30.8 1.6 %collective-permute-start.13 = (bf16[768,256]{1,0:T(8,128)(2,1)S(1)}, bf16[768,256]{1,0:T(8,128)(2,1)S(1)}, u32[]{:S(2)}, u32[]{:S(2)}) collective-permute-start(bf16[768,256]{1,0:T(8,128)(2,1)S(1)} %shard_map.86.refs_1_.refs_2_.refs_7_.refs_0_), channel_id=1, source_target_pairs={{4,12},{6,2},{12,20},{14,6},{20,28},{22,14},{28,24},{30,22},{24,16... | collective-permute-start | bytes 1179656 | tf_op jit(solution)/shard_map/ppermute | solution.py:432
  34.7 1.8 %collective-permute-start.12 = (bf16[768,256]{1,0:T(8,128)(2,1)S(1)}, bf16[768,256]{1,0:T(8,128)(2,1)S(1)}, u32[]{:S(2)}, u32[]{:S(2)}) collective-permute-start(bf16[768,256]{1,0:T(8,128)(2,1)S(1)} %collective-permute-done.1.refs_2_.refs_3_), channel_id=1, source_target_pairs={{4,12},{6,2},{12,20},{14,6},{20,28},{22,14},{28,24},{30,22},{24,16... | collective-permute-start | bytes 1179656 | tf_op jit(solution)/shard_map/ppermute | solution.py:432
  41.6 2.0 %collective-permute-start.14 = (bf16[912,256]{1,0:T(8,128)(2,1)S(1)}, bf16[912,256]{1,0:T(8,128)(2,1)S(1)}, u32[]{:S(2)}, u32[]{:S(2)}) collective-permute-start(bf16[912,256]{1,0:T(8,128)(2,1)S(1)} %shard_map.99), channel_id=1, source_target_pairs={{4,12},{6,2},{12,20},{14,6},{20,28},{22,14},{28,24},{30,22},{24,16... | collective-permute-start | bytes 1400840 | tf_op jit(solution)/shard_map/ppermute | solution.py:432
  43.6 2.2 %collective-permute-done.12.refs_2_ = bf16[768,256]{1,0:T(8,128)(2,1)S(1)} collective-permute-done((bf16[768,256]{1,0:T(8,128)(2,1)S(1)}, bf16[768,256]{1,0:T(8,128)(2,1)S(1)}, u32[]{:S(2)}, u32[]{:S(2)}) %collective-permute-start.12) | collective-permute-done | bytes 393248 | tf_op jit(solution)/shard_map/ppermute | solution.py:432
  46.6 2.3 %shard_map.98.own_ref = f32[768,256]{1,0:T(8,128)S(1)} custom-call(bf16[1,1536,256]{2,1,0:T(8,128)(2,1)S(1)} %get-tuple-element.59.refs_0_, bf16[2,1536,256]{2,1,0:T(8,128)(2,1)S(1)} %get-tuple-element.63.refs_1_, bf16[2,1536,256]{2,1,0:T(8,128)(2,1)S(1)} %get-tuple-element.67.refs_2_, bf16[2,1536,256]{2,1,0:T(8,128)(2,1)S(1)} %get-tuple-element.74.refs_3_, ...), custom_call_target="tpu_custom_call" | custom-call | flops 1207959552 | bytes 8650752 | tf_op jit(solution)/shard_map/pallas_call | solution.py:47
  48.8 2.0 %collective-permute-done.14.refs_4_.refs_0_ = bf16[912,256]{1,0:T(8,128)(2,1)S(1)} collective-permute-done((bf16[912,256]{1,0:T(8,128)(2,1)S(1)}, bf16[912,256]{1,0:T(8,128)(2,1)S(1)}, u32[]{:S(2)}, u32[]{:S(2)}) %collective-permute-start.14) | collective-permute-done | bytes 466976 | tf_op jit(solution)/shard_map/ppermute | solution.py:432
  50.8 1.7 %collective-permute-start.18 = (bf16[912,256]{1,0:T(8,128)(2,1)S(1)}, bf16[912,256]{1,0:T(8,128)(2,1)S(1)}, u32[]{:S(2)}, u32[]{:S(2)}) collective-permute-start(bf16[912,256]{1,0:T(8,128)(2,1)S(1)} %collective-permute-done.14.refs_4_.refs_0_), channel_id=1, source_target_pairs={{4,12},{6,2},{12,20},{14,6},{20,28},{22,14},{28,24},{30,22},{24,16... | collective-permute-start | bytes 1400840 | tf_op jit(solution)/shard_map/ppermute | solution.py:432
  55.6 3.8 %collective-permute-done.18.refs_2_.refs_0_ = bf16[912,256]{1,0:T(8,128)(2,1)S(1)} collective-permute-done((bf16[912,256]{1,0:T(8,128)(2,1)S(1)}, bf16[912,256]{1,0:T(8,128)(2,1)S(1)}, u32[]{:S(2)}, u32[]{:S(2)}) %collective-permute-start.18) | collective-permute-done | bytes 466976 | tf_op jit(solution)/shard_map/ppermute | solution.py:432
  59.3 1.7 %collective-permute-start.20 = (bf16[912,256]{1,0:T(8,128)(2,1)S(1)}, bf16[912,256]{1,0:T(8,128)(2,1)S(1)}, u32[]{:S(2)}, u32[]{:S(2)}) collective-permute-start(bf16[912,256]{1,0:T(8,128)(2,1)S(1)} %collective-permute-done.18.refs_2_.refs_0_), channel_id=1, source_target_pairs={{4,12},{6,2},{12,20},{14,6},{20,28},{22,14},{28,24},{30,22},{24,16... | collective-permute-start | bytes 1400840 | tf_op jit(solution)/shard_map/ppermute | solution.py:432
  63.6 1.7 %collective-permute-start.22 = (bf16[768,256]{1,0:T(8,128)(2,1)S(1)}, bf16[768,256]{1,0:T(8,128)(2,1)S(1)}, u32[]{:S(2)}, u32[]{:S(2)}) collective-permute-start(bf16[768,256]{1,0:T(8,128)(2,1)S(1)} %collective-permute-done.17.refs_1_), channel_id=1, source_target_pairs={{4,12},{6,2},{12,20},{14,6},{20,28},{22,14},{28,24},{30,22},{24,16... | collective-permute-start | bytes 1179656 | tf_op jit(solution)/shard_map/ppermute | solution.py:432
  65.3 2.0 %shard_map.100 = (f32[768,256]{1,0:T(8,128)S(1)}, f32[768,256]{1,0:T(8,128)S(1)}) custom-call(bf16[768,256]{1,0:T(8,128)(2,1)S(1)} %shard_map.86.refs_1_.refs_2_.refs_7_.refs_0_, bf16[768,256]{1,0:T(8,128)(2,1)S(1)} %collective-permute-done.13.block_ref.refs_1_, bf16[768,256]{1,0:T(8,128)(2,1)S(1)} %collective-permute-done.12.refs_2_, ...), custom_call_target="tpu_custom_call" | custom-call | flops 1811939328 | bytes 3244032 | tf_op jit(solution)/shard_map/pallas_call | solution.py:47
  67.3 1.7 %shard_map.101.group_ref = f32[768,256]{1,0:T(8,128)S(1)} custom-call(bf16[768,256]{1,0:T(8,128)(2,1)S(1)} %shard_map.86.refs_1_.refs_2_.refs_7_.refs_0_, bf16[768,256]{1,0:T(8,128)(2,1)S(1)} %collective-permute-done.15.refs_1_, f32[1,768]{1,0:T(1,128)S(1)} %get-tuple-element.90.refs_2_, f32[1,768]{1,0:T(1,128)S(1)} %collective-permute-done.16.refs_3_, ...), custom_call_target="tpu_custom_call" | custom-call | flops 1207959552 | bytes 2039808 | tf_op jit(solution)/shard_map/pallas_call | solution.py:47
  69.1 1.6 %collective-permute-start.21 = (bf16[48,256]{1,0:T(8,128)(2,1)S(1)}, bf16[48,256]{1,0:T(8,128)(2,1)S(1)}, u32[]{:S(2)}, u32[]{:S(2)}) collective-permute-start(bf16[48,256]{1,0:T(8,128)(2,1)S(1)} %bitcast.7), channel_id=1, source_target_pairs={{4,12},{6,2},{12,20},{14,6},{20,28},{22,14},{28,24},{30,22},{24,16... | collective-permute-start | bytes 73736 | tf_op jit(solution)/shard_map/ppermute | solution.py:575
  75.5 2.4 %collective-permute-done.24.far_ref = bf16[912,256]{1,0:T(8,128)(2,1)S(1)} collective-permute-done((bf16[912,256]{1,0:T(8,128)(2,1)S(1)}, bf16[912,256]{1,0:T(8,128)(2,1)S(1)}, u32[]{:S(2)}, u32[]{:S(2)}) %collective-permute-start.24) | collective-permute-done | bytes 466976 | tf_op jit(solution)/shard_map/ppermute | solution.py:421
  77.9 1.9 %shard_map.105 = f32[768,256]{1,0:T(8,128)} custom-call(bf16[768,256]{1,0:T(8,128)(2,1)S(1)} %copy-done.1, f32[768,256]{1,0:T(8,128)S(1)} %shard_map.101.group_ref, f32[768,256]{1,0:T(8,128)S(1)} %get-tuple-element.107.own_ref, f32[768,256]{1,0:T(8,128)S(1)} %collective-permute-done.23.other_ref, ...), custom_call_target="tpu_custom_call" | custom-call | flops 603979776 | bytes 4497408 | tf_op jit(solution)/shard_map/pallas_call | solution.py:47
  (65 shorter events, 32.0 us)
Async XLA Ops:
  1.9 5.5 %collective-permute-start.3 = (bf16[768,256]{1,0:T(8,128)(2,1)S(1)}, bf16[768,256]{1,0:T(8,128)(2,1)S(1)}, u32[]{:S(2)}, u32[]{:S(2)}) collective-permute-start(bf16[768,256]{1,0:T(8,128)(2,1)S(1)} %shard_map.85.refs_0_.k_ref.refs_5_.refs_4_), channel_id=1, source_target_pairs={{0,2},{2,0},{4,6},{6,4},{8,10},{10,8},{12,14},{14,12},{16,18},{18,... | collective-permute-start | bytes 1179656 | tf_op jit(solution)/shard_map/ppermute | solution.py:421
  2.4 8.4 %collective-permute-start = (bf16[768,256]{1,0:T(8,128)(2,1)S(1)}, bf16[768,256]{1,0:T(8,128)(2,1)S(1)}, u32[]{:S(2)}, u32[]{:S(2)}) collective-permute-start(bf16[768,256]{1,0:T(8,128)(2,1)S(1)} %shard_map.85.refs_0_.k_ref.refs_5_.refs_4_), channel_id=1, source_target_pairs={{4,12},{6,2},{12,20},{14,6},{20,28},{22,14},{28,24},{30,22},{24,16... | collective-permute-start | bytes 1179656 | tf_op jit(solution)/shard_map/ppermute | solution.py:432
  6.2 6.5 %collective-permute-start.1 = (bf16[768,256]{1,0:T(8,128)(2,1)S(1)}, bf16[768,256]{1,0:T(8,128)(2,1)S(1)}, u32[]{:S(2)}, u32[]{:S(2)}) collective-permute-start(bf16[768,256]{1,0:T(8,128)(2,1)S(1)} %shard_map.86.refs_1_.refs_2_.refs_7_.refs_0_), channel_id=1, source_target_pairs={{0,2},{2,0},{4,6},{6,4},{8,10},{10,8},{12,14},{14,12},{16,18},{18,... | collective-permute-start | bytes 1179656 | tf_op jit(solution)/shard_map/ppermute | solution.py:421
  7.4 7.8 %collective-permute-start.4 = (bf16[768,256]{1,0:T(8,128)(2,1)S(1)}, bf16[768,256]{1,0:T(8,128)(2,1)S(1)}, u32[]{:S(2)}, u32[]{:S(2)}) collective-permute-start(bf16[768,256]{1,0:T(8,128)(2,1)S(1)} %collective-permute-done.3), channel_id=1, source_target_pairs={{4,12},{6,2},{12,20},{14,6},{20,28},{22,14},{28,24},{30,22},{24,16... | collective-permute-start | bytes 1179656 | tf_op jit(solution)/shard_map/ppermute | solution.py:432
  10.8 9.3 %collective-permute-start.5 = (bf16[768,256]{1,0:T(8,128)(2,1)S(1)}, bf16[768,256]{1,0:T(8,128)(2,1)S(1)}, u32[]{:S(2)}, u32[]{:S(2)}) collective-permute-start(bf16[768,256]{1,0:T(8,128)(2,1)S(1)} %collective-permute-done.refs_0_), channel_id=1, source_target_pairs={{4,12},{6,2},{12,20},{14,6},{20,28},{22,14},{28,24},{30,22},{24,16... | collective-permute-start | bytes 1179656 | tf_op jit(solution)/shard_map/ppermute | solution.py:432
  15.3 8.4 %collective-permute-start.6 = (bf16[768,256]{1,0:T(8,128)(2,1)S(1)}, bf16[768,256]{1,0:T(8,128)(2,1)S(1)}, u32[]{:S(2)}, u32[]{:S(2)}) collective-permute-start(bf16[768,256]{1,0:T(8,128)(2,1)S(1)} %collective-permute-done.4.refs_1_), channel_id=1, source_target_pairs={{4,12},{6,2},{12,20},{14,6},{20,28},{22,14},{28,24},{30,22},{24,16... | collective-permute-start | bytes 1179656 | tf_op jit(solution)/shard_map/ppermute | solution.py:432
  17.0 12.6 %collective-permute-start.9 = (bf16[768,256]{1,0:T(8,128)(2,1)S(1)}, bf16[768,256]{1,0:T(8,128)(2,1)S(1)}, u32[]{:S(2)}, u32[]{:S(2)}) collective-permute-start(bf16[768,256]{1,0:T(8,128)(2,1)S(1)} %shard_map.85.refs_0_.k_ref.refs_5_.refs_4_), channel_id=1, source_target_pairs={{0,1},{1,0},{2,3},{3,2},{4,5},{5,4},{6,7},{7,6},{8,9},{9,8},{10,11... | collective-permute-start | bytes 1179656 | tf_op jit(solution)/shard_map/ppermute | solution.py:437
  20.1 7.8 %collective-permute-start.7 = (bf16[768,256]{1,0:T(8,128)(2,1)S(1)}, bf16[768,256]{1,0:T(8,128)(2,1)S(1)}, u32[]{:S(2)}, u32[]{:S(2)}) collective-permute-start(bf16[768,256]{1,0:T(8,128)(2,1)S(1)} %collective-permute-done.5.refs_0_), channel_id=1, source_target_pairs={{4,12},{6,2},{12,20},{14,6},{20,28},{22,14},{28,24},{30,22},{24,16... | collective-permute-start | bytes 1179656 | tf_op jit(solution)/shard_map/ppermute | solution.py:432
  25.3 7.8 %collective-permute-start.8 = (bf16[768,256]{1,0:T(8,128)(2,1)S(1)}, bf16[768,256]{1,0:T(8,128)(2,1)S(1)}, u32[]{:S(2)}, u32[]{:S(2)}) collective-permute-start(bf16[768,256]{1,0:T(8,128)(2,1)S(1)} %collective-permute-done.6.refs_1_), channel_id=1, source_target_pairs={{4,12},{6,2},{12,20},{14,6},{20,28},{22,14},{28,24},{30,22},{24,16... | collective-permute-start | bytes 1179656 | tf_op jit(solution)/shard_map/ppermute | solution.py:432
  27.9 9.4 %collective-permute-start.10 = (bf16[768,256]{1,0:T(8,128)(2,1)S(1)}, bf16[768,256]{1,0:T(8,128)(2,1)S(1)}, u32[]{:S(2)}, u32[]{:S(2)}) collective-permute-start(bf16[768,256]{1,0:T(8,128)(2,1)S(1)} %collective-permute-done.7.refs_0_), channel_id=1, source_target_pairs={{4,12},{6,2},{12,20},{14,6},{20,28},{22,14},{28,24},{30,22},{24,16... | collective-permute-start | bytes 1179656 | tf_op jit(solution)/shard_map/ppermute | solution.py:432
  30.8 10.8 %collective-permute-start.13 = (bf16[768,256]{1,0:T(8,128)(2,1)S(1)}, bf16[768,256]{1,0:T(8,128)(2,1)S(1)}, u32[]{:S(2)}, u32[]{:S(2)}) collective-permute-start(bf16[768,256]{1,0:T(8,128)(2,1)S(1)} %shard_map.86.refs_1_.refs_2_.refs_7_.refs_0_), channel_id=1, source_target_pairs={{4,12},{6,2},{12,20},{14,6},{20,28},{22,14},{28,24},{30,22},{24,16... | collective-permute-start | bytes 1179656 | tf_op jit(solution)/shard_map/ppermute | solution.py:432
  34.7 11.0 %collective-permute-start.12 = (bf16[768,256]{1,0:T(8,128)(2,1)S(1)}, bf16[768,256]{1,0:T(8,128)(2,1)S(1)}, u32[]{:S(2)}, u32[]{:S(2)}) collective-permute-start(bf16[768,256]{1,0:T(8,128)(2,1)S(1)} %collective-permute-done.1.refs_2_.refs_3_), channel_id=1, source_target_pairs={{4,12},{6,2},{12,20},{14,6},{20,28},{22,14},{28,24},{30,22},{24,16... | collective-permute-start | bytes 1179656 | tf_op jit(solution)/shard_map/ppermute | solution.py:432
  39.3 1.3 %collective-permute-start.11 = (f32[17,768]{1,0:T(8,128)S(1)}, f32[17,768]{1,0:T(8,128)S(1)}, u32[]{:S(2)}, u32[]{:S(2)}) collective-permute-start(f32[17,768]{1,0:T(8,128)S(1)} %get-tuple-element.81), channel_id=1, source_target_pairs={{0,2},{2,0},{4,6},{6,4},{8,10},{10,8},{12,14},{14,12},{16,18},{18,... | collective-permute-start | bytes 156680 | tf_op jit(solution)/shard_map/ppermute | solution.py:421
  41.6 9.2 %collective-permute-start.14 = (bf16[912,256]{1,0:T(8,128)(2,1)S(1)}, bf16[912,256]{1,0:T(8,128)(2,1)S(1)}, u32[]{:S(2)}, u32[]{:S(2)}) collective-permute-start(bf16[912,256]{1,0:T(8,128)(2,1)S(1)} %shard_map.99), channel_id=1, source_target_pairs={{4,12},{6,2},{12,20},{14,6},{20,28},{22,14},{28,24},{30,22},{24,16... | collective-permute-start | bytes 1400840 | tf_op jit(solution)/shard_map/ppermute | solution.py:432
  50.8 8.6 %collective-permute-start.18 = (bf16[912,256]{1,0:T(8,128)(2,1)S(1)}, bf16[912,256]{1,0:T(8,128)(2,1)S(1)}, u32[]{:S(2)}, u32[]{:S(2)}) collective-permute-start(bf16[912,256]{1,0:T(8,128)(2,1)S(1)} %collective-permute-done.14.refs_4_.refs_0_), channel_id=1, source_target_pairs={{4,12},{6,2},{12,20},{14,6},{20,28},{22,14},{28,24},{30,22},{24,16... | collective-permute-start | bytes 1400840 | tf_op jit(solution)/shard_map/ppermute | solution.py:432
  52.5 11.1 %collective-permute-start.17 = (bf16[768,256]{1,0:T(8,128)(2,1)S(1)}, bf16[768,256]{1,0:T(8,128)(2,1)S(1)}, u32[]{:S(2)}, u32[]{:S(2)}) collective-permute-start(bf16[768,256]{1,0:T(8,128)(2,1)S(1)} %collective-permute-done.12.refs_2_), channel_id=1, source_target_pairs={{4,12},{6,2},{12,20},{14,6},{20,28},{22,14},{28,24},{30,22},{24,16... | collective-permute-start | bytes 1179656 | tf_op jit(solution)/shard_map/ppermute | solution.py:432
  54.1 18.0 %collective-permute-start.19 = (f32[768,256]{1,0:T(8,128)S(1)}, f32[768,256]{1,0:T(8,128)S(1)}, u32[]{:S(2)}, u32[]{:S(2)}) collective-permute-start(f32[768,256]{1,0:T(8,128)S(1)} %shard_map.97), channel_id=1, source_target_pairs={{0,2},{2,0},{4,6},{6,4},{8,10},{10,8},{12,14},{14,12},{16,18},{18,... | collective-permute-start | bytes 2359304 | tf_op jit(solution)/shard_map/ppermute | solution.py:421
  54.1 13.2 %collective-permute-start.15 = (bf16[768,256]{1,0:T(8,128)(2,1)S(1)}, bf16[768,256]{1,0:T(8,128)(2,1)S(1)}, u32[]{:S(2)}, u32[]{:S(2)}) collective-permute-start(bf16[768,256]{1,0:T(8,128)(2,1)S(1)} %shard_map.86.refs_1_.refs_2_.refs_7_.refs_0_), channel_id=1, source_target_pairs={{0,1},{1,0},{2,3},{3,2},{4,5},{5,4},{6,7},{7,6},{8,9},{9,8},{10,11... | collective-permute-start | bytes 1179656 | tf_op jit(solution)/shard_map/ppermute | solution.py:437
  59.3 9.7 %collective-permute-start.20 = (bf16[912,256]{1,0:T(8,128)(2,1)S(1)}, bf16[912,256]{1,0:T(8,128)(2,1)S(1)}, u32[]{:S(2)}, u32[]{:S(2)}) collective-permute-start(bf16[912,256]{1,0:T(8,128)(2,1)S(1)} %collective-permute-done.18.refs_2_.refs_0_), channel_id=1, source_target_pairs={{4,12},{6,2},{12,20},{14,6},{20,28},{22,14},{28,24},{30,22},{24,16... | collective-permute-start | bytes 1400840 | tf_op jit(solution)/shard_map/ppermute | solution.py:432
  61.1 6.2 %collective-permute-start.16 = (f32[1,768]{1,0:T(1,128)S(1)}, f32[1,768]{1,0:T(1,128)S(1)}, u32[]{:S(2)}, u32[]{:S(2)}) collective-permute-start(f32[1,768]{1,0:T(1,128)S(1)} %get-tuple-element.90.refs_2_), channel_id=1, source_target_pairs={{0,1},{1,0},{2,3},{3,2},{4,5},{5,4},{6,7},{7,6},{8,9},{9,8},{10,11... | collective-permute-start | bytes 9224 | tf_op jit(solution)/shard_map/ppermute | solution.py:437
  63.6 9.9 %collective-permute-start.22 = (bf16[768,256]{1,0:T(8,128)(2,1)S(1)}, bf16[768,256]{1,0:T(8,128)(2,1)S(1)}, u32[]{:S(2)}, u32[]{:S(2)}) collective-permute-start(bf16[768,256]{1,0:T(8,128)(2,1)S(1)} %collective-permute-done.17.refs_1_), channel_id=1, source_target_pairs={{4,12},{6,2},{12,20},{14,6},{20,28},{22,14},{28,24},{30,22},{24,16... | collective-permute-start | bytes 1179656 | tf_op jit(solution)/shard_map/ppermute | solution.py:432
  69.1 4.4 %collective-permute-start.21 = (bf16[48,256]{1,0:T(8,128)(2,1)S(1)}, bf16[48,256]{1,0:T(8,128)(2,1)S(1)}, u32[]{:S(2)}, u32[]{:S(2)}) collective-permute-start(bf16[48,256]{1,0:T(8,128)(2,1)S(1)} %bitcast.7), channel_id=1, source_target_pairs={{4,12},{6,2},{12,20},{14,6},{20,28},{22,14},{28,24},{30,22},{24,16... | collective-permute-start | bytes 73736 | tf_op jit(solution)/shard_map/ppermute | solution.py:575
  74.9 3.0 %collective-permute-start.23 = (f32[768,256]{1,0:T(8,128)S(1)}, f32[768,256]{1,0:T(8,128)S(1)}, u32[]{:S(2)}, u32[]{:S(2)}) collective-permute-start(f32[768,256]{1,0:T(8,128)S(1)} %get-tuple-element.108), channel_id=1, source_target_pairs={{0,2},{2,0},{4,6},{6,4},{8,10},{10,8},{12,14},{14,12},{16,18},{18,... | collective-permute-start | bytes 2359304 | tf_op jit(solution)/shard_map/ppermute | solution.py:421
  75.0 2.9 %collective-permute-start.24 = (bf16[912,256]{1,0:T(8,128)(2,1)S(1)}, bf16[912,256]{1,0:T(8,128)(2,1)S(1)}, u32[]{:S(2)}, u32[]{:S(2)}) collective-permute-start(bf16[912,256]{1,0:T(8,128)(2,1)S(1)} %collective-permute-done.20.refs_2_.near_ref), channel_id=1, source_target_pairs={{0,2},{2,0},{4,6},{6,4},{8,10},{10,8},{12,14},{14,12},{16,18},{18,... | collective-permute-start | bytes 1400840 | tf_op jit(solution)/shard_map/ppermute | solution.py:421
  (9 other events, 28.7 us)

commit v6 on v5

--- a/solution.py
+++ b/solution.py
@@ -369,9 +369,10 @@
     return jnp.concatenate(parts, axis=1)
 
 
-def grad_key_kernel(sources, blocks, carried, number, *refs):
-    queries, messages = refs[:blocks], refs[blocks : -2 - carried]
-    so_far, outs = refs[len(refs) - 2 - carried : len(refs) - 2], refs[-2:]
+def grad_key_kernel(sources, blocks, carried, number, sides, *refs):
+    queries, outs = refs[:blocks], refs[-len(sides) :]
+    messages = refs[blocks : -len(sides) - carried]
+    so_far = refs[len(refs) - len(sides) - carried : len(refs) - len(sides)]
     anchors, width = outs[0].shape
     step = 256
     told = [
@@ -380,10 +381,10 @@
         else messages[at][...]
         for at, distance, half in sources
     ]
-    for side, out in enumerate(outs):
+    for index, (side, out) in enumerate(zip(sides, outs)):
         for start in range(0, anchors, step):
             rows = slice(start, start + step)
-            total = so_far[side][rows, :] if side < carried else jnp.zeros((step, width), F32)
+            total = so_far[index][rows, :] if index < carried else jnp.zeros((step, width), F32)
             for message, block in zip(told, queries):
                 code = message[side : side + 1, :]
                 weight = message[2 + side : 3 + side, :]
@@ -439,8 +440,9 @@
     block = shape((anchors, width), BF16)
     one_block = 2 * anchors * anchors * width
     (key_rows,) = call(unit_kernel, [block], [keys], 5 * keys.size)
-    key_ring = Ring(key_rows, swap(key_rows))
+    key_ring = Ring(key_rows, None)
     key_ring.hop(0)
+    (key_ring.front[1],) = call(unit_kernel, [block], [swap(keys)], 5 * keys.size)
     (query_rows,) = call(unit_kernel, [block], [queries], 5 * queries.size)
     codes, inverse, code_columns = call(
         codes_kernel,
@@ -515,7 +517,7 @@
     )
     query_ring.hop(0)
 
-    def grad_keys_of(steps, sums, *pins):
+    def grad_keys_of(steps, sums, *pins, sides=(0, 1)):
         blocks, sources, messages = [], [], []
         for step in steps:
             for half, slot in enumerate([2 * step - 1, 2 * step] if step else [0]):
@@ -524,8 +526,8 @@
             messages.append(ring[min(2 * step + 1, chips - 1)] if step else home)
         blocks[0] = after(blocks[0], *pins)
         return call(
-            functools.partial(grad_key_kernel, sources, len(blocks), len(sums), each),
-            [shape((anchors, width))] * 2,
+            functools.partial(grad_key_kernel, sources, len(blocks), len(sums), each, sides),
+            [shape((anchors, width))] * len(sides),
             blocks + messages + list(sums),
             2 * len(blocks) * one_block,
         )
@@ -552,7 +554,7 @@
         2 * loop * one_block,
     )
     query_ring.hop(0, summed_q)
-    summed_k = grad_keys_of([0, 1], [], summed_q)
+    summed_k = grad_keys_of([0, 1], [], summed_q, *all_logs[1:])
     query_ring.hop(1)
     (group_k,) = call(
         functools.partial(group_key_kernel, loop),
@@ -560,7 +562,7 @@
         [query_rows] + group_queries + all_logs + [after(key_rows, summed_k[0]), inverse],
         2 * loop * one_block,
     )
-    query_ring.hop(0)
+    query_ring.hop(0, summed_k[0])
     for step in range(2, middle - 1):
         summed_k = grad_keys_of([step], summed_k, group_k)
     (grad_queries, loss) = call(
@@ -571,15 +573,16 @@
     )
     first = 12 * (middle - 1)
     skip = first // 16 * 16
-    opposite = ring[-1][anchors:].reshape(anchors // width, each, width)[:, skip:]
+    opposite = after(ring[-1], grad_queries)[anchors:].reshape(anchors // width, each, width)[:, skip:]
     opposite = lax.ppermute(opposite.reshape(-1, width), "sky", onward)
     facing = swap(ring[-1])
-    summed_k = grad_keys_of([middle - 1], summed_k, grad_queries, opposite)
+    farthest = [middle - 1]
+    (sib_sum,) = grad_keys_of(farthest, summed_k[1:], grad_queries, opposite, sides=(1,))
+    (own_sum,) = grad_keys_of(farthest, summed_k[:1], sib_sum, sides=(0,))
     (grad_keys,) = call(
         functools.partial(grad_key_finish_kernel, each - skip, first - skip),
         [shape((anchors, width))],
-        [keys, group_k, summed_k[0], swap(summed_k[1]), ring[-1], facing]
-        + [opposite],
+        [keys, group_k, own_sum, swap(sib_sum), ring[-1], facing, opposite],
         2 * one_block,
     )
     return (loss, grad_queries, grad_keys)

time: 80 us -> 80 us (level)
  starting transfers between devices: 32.4 us -> 29.1 us
  waiting for transfers between devices: 21 us -> 23.8 us
    ppermute x1, waiting for transfers between devices: 0.01 us -> 2.41 us  [shards(): opposite = lax.ppermute(opposite.reshape(-1, width), 'sky', onward)]
    ppermute x14, starting transfers between devices: 24.9 us -> 22.6 us  [hop(): lax.ppermute(after(self.front[which], *pins), 'sky', onward)]
    ppermute x3, waiting for transfers between devices: 0.01 us -> 1.91 us  [group(): return [lax.ppermute(x, 'loop', pairs) for pairs in shifts]]
    ppermute x3, starting transfers between devices: 4.47 us -> 3.52 us  [group(): return [lax.ppermute(x, 'loop', pairs) for pairs in shifts]]
    pallas_call x21 -> x23, Pallas kernels: 23.5 us -> 24 us  [call(): pl.pallas_call(kernel, out_shape=list(outs), in_specs=specs, out_specs=[p...]
  transfers between devices with their start and end apart: 25 -> 25, of which waited for: 14 -> 16; matrix products, arithmetic and copies ran while one was open for 0% -> 0% of each run, Pallas kernels for 25% -> 27%
where the time goes in v6:
time: 80 us; the launch traced here: 79.8 us
  starting transfers between devices  29.1 us (36%)
  Pallas kernels  24 us (30%)
  waiting for transfers between devices  23.8 us (30%)
  local copies, waits for them, and re-layouts  2.03 us (3%)
  between operations  0.88 us (1%)
    pallas_call x23, Pallas kernels, call(): pl.pallas_call(kernel, out_shape=list(outs), in_specs=specs, out_specs=[p...  24 us
    ppermute x14, starting transfers between devices, hop(): lax.ppermute(after(self.front[which], *pins), 'sky', onward)  22.6 us
    ppermute x14, waiting for transfers between devices, hop(): lax.ppermute(after(self.front[which], *pins), 'sky', onward)  15.3 us
    ppermute x7, waiting for transfers between devices, swap(): return lax.ppermute(x, 'sky', siblings)  4.18 us
    ppermute x3, starting transfers between devices, group(): return [lax.ppermute(x, 'loop', pairs) for pairs in shifts]  3.52 us
    ppermute x1, waiting for transfers between devices, shards(): opposite = lax.ppermute(opposite.reshape(-1, width), 'sky', onward)  2.41 us
    unnamed x16, local copies, waits for them, and re-layouts  2.02 us
    ppermute x3, waiting for transfers between devices, group(): return [lax.ppermute(x, 'loop', pairs) for pairs in shifts]  1.91 us
  transfers between devices with their start and end apart: 25, of which 16 were waited for; matrix products, arithmetic and copies ran while one was open for 0% of the time, Pallas kernels for 27%

profile of v6, /device:TPU:0, one launch (start us, length us, event | category | flops | bytes accessed | tf_op | source)
XLA Modules:
  0.0 79.8 jit_solution(708257098644858080)
XLA Ops:
  2.4 2.6 %collective-permute-start = (bf16[768,256]{1,0:T(8,128)(2,1)S(1)}, bf16[768,256]{1,0:T(8,128)(2,1)S(1)}, u32[]{:S(2)}, u32[]{:S(2)}) collective-permute-start(bf16[768,256]{1,0:T(8,128)(2,1)S(1)} %shard_map.85.refs_0_.k_ref.refs_5_.refs_4_), channel_id=1, source_target_pairs={{4,12},{6,2},{12,20},{14,6},{20,28},{22,14},{28,24},{30,22},{24,16... | collective-permute-start | bytes 1179656 | tf_op jit(solution)/shard_map/ppermute | solution.py:433
  10.8 2.0 %collective-permute-start.5 = (bf16[768,256]{1,0:T(8,128)(2,1)S(1)}, bf16[768,256]{1,0:T(8,128)(2,1)S(1)}, u32[]{:S(2)}, u32[]{:S(2)}) collective-permute-start(bf16[768,256]{1,0:T(8,128)(2,1)S(1)} %collective-permute-done.refs_0_), channel_id=1, source_target_pairs={{4,12},{6,2},{12,20},{14,6},{20,28},{22,14},{28,24},{30,22},{24,16... | collective-permute-start | bytes 1179656 | tf_op jit(solution)/shard_map/ppermute | solution.py:433
  13.7 1.9 %collective-permute-done.4.refs_1_ = bf16[768,256]{1,0:T(8,128)(2,1)S(1)} collective-permute-done((bf16[768,256]{1,0:T(8,128)(2,1)S(1)}, bf16[768,256]{1,0:T(8,128)(2,1)S(1)}, u32[]{:S(2)}, u32[]{:S(2)}) %collective-permute-start.4) | collective-permute-done | bytes 393248 | tf_op jit(solution)/shard_map/ppermute | solution.py:433
  17.0 1.5 %collective-permute-start.9 = (bf16[768,256]{1,0:T(8,128)(2,1)S(1)}, bf16[768,256]{1,0:T(8,128)(2,1)S(1)}, u32[]{:S(2)}, u32[]{:S(2)}) collective-permute-start(bf16[768,256]{1,0:T(8,128)(2,1)S(1)} %shard_map.85.refs_0_.k_ref.refs_5_.refs_4_), channel_id=1, source_target_pairs={{0,1},{1,0},{2,3},{3,2},{4,5},{5,4},{6,7},{7,6},{8,9},{9,8},{10,11... | collective-permute-start | bytes 1179656 | tf_op jit(solution)/shard_map/ppermute | solution.py:438
  18.5 1.7 %shard_map.91 = (bf16[2,1536,256]{2,1,0:T(8,128)(2,1)S(1)}, f32[1536,2]{1,0:T(8,128)S(1)}) custom-call(bf16[768,256]{1,0:T(8,128)(2,1)S(1)} %collective-permute-done.refs_0_, bf16[768,256]{1,0:T(8,128)(2,1)S(1)} %collective-permute-done.4.refs_1_, bf16[768,256]{1,0:T(8,128)(2,1)S(1)} %shard_map.86.refs_1_.refs_2_.refs_7_.refs_0_, ...), custom_call_target="tpu_custom_call" | custom-call | flops 1207959552 | bytes 4718592 | tf_op jit(solution)/shard_map/pallas_call | solution.py:47
  20.2 1.6 %collective-permute-start.7 = (bf16[768,256]{1,0:T(8,128)(2,1)S(1)}, bf16[768,256]{1,0:T(8,128)(2,1)S(1)}, u32[]{:S(2)}, u32[]{:S(2)}) collective-permute-start(bf16[768,256]{1,0:T(8,128)(2,1)S(1)} %collective-permute-done.5.refs_0_), channel_id=1, source_target_pairs={{4,12},{6,2},{12,20},{14,6},{20,28},{22,14},{28,24},{30,22},{24,16... | collective-permute-start | bytes 1179656 | tf_op jit(solution)/shard_map/ppermute | solution.py:433
  21.8 2.2 %collective-permute-done.6.refs_1_ = bf16[768,256]{1,0:T(8,128)(2,1)S(1)} collective-permute-done((bf16[768,256]{1,0:T(8,128)(2,1)S(1)}, bf16[768,256]{1,0:T(8,128)(2,1)S(1)}, u32[]{:S(2)}, u32[]{:S(2)}) %collective-permute-start.6) | collective-permute-done | bytes 393248 | tf_op jit(solution)/shard_map/ppermute | solution.py:433
  24.0 1.6 %shard_map.92 = (bf16[2,1536,256]{2,1,0:T(8,128)(2,1)S(1)}, f32[1536,2]{1,0:T(8,128)S(1)}) custom-call(bf16[768,256]{1,0:T(8,128)(2,1)S(1)} %collective-permute-done.5.refs_0_, bf16[768,256]{1,0:T(8,128)(2,1)S(1)} %collective-permute-done.6.refs_1_, bf16[768,256]{1,0:T(8,128)(2,1)S(1)} %shard_map.86.refs_1_.refs_2_.refs_7_.refs_0_, ...), custom_call_target="tpu_custom_call" | custom-call | flops 1207959552 | bytes 4718592 | tf_op jit(solution)/shard_map/pallas_call | solution.py:47
  30.8 1.6 %collective-permute-start.13 = (bf16[768,256]{1,0:T(8,128)(2,1)S(1)}, bf16[768,256]{1,0:T(8,128)(2,1)S(1)}, u32[]{:S(2)}, u32[]{:S(2)}) collective-permute-start(bf16[768,256]{1,0:T(8,128)(2,1)S(1)} %shard_map.86.refs_1_.refs_2_.refs_7_.refs_0_), channel_id=1, source_target_pairs={{4,12},{6,2},{12,20},{14,6},{20,28},{22,14},{28,24},{30,22},{24,16... | collective-permute-start | bytes 1179656 | tf_op jit(solution)/shard_map/ppermute | solution.py:433
  33.5 1.6 %shard_map.94 = (bf16[2,1536,256]{2,1,0:T(8,128)(2,1)S(1)}, f32[1536,2]{1,0:T(8,128)S(1)}) custom-call(bf16[768,256]{1,0:T(8,128)(2,1)S(1)} %collective-permute-done.7.refs_0_, bf16[768,256]{1,0:T(8,128)(2,1)S(1)} %collective-permute-done.8.refs_1_, bf16[768,256]{1,0:T(8,128)(2,1)S(1)} %shard_map.86.refs_1_.refs_2_.refs_7_.refs_0_, ...), custom_call_target="tpu_custom_call" | custom-call | flops 1207959552 | bytes 4718592 | tf_op jit(solution)/shard_map/pallas_call | solution.py:47
  41.9 1.6 %collective-permute-start.14 = (bf16[912,256]{1,0:T(8,128)(2,1)S(1)}, bf16[912,256]{1,0:T(8,128)(2,1)S(1)}, u32[]{:S(2)}, u32[]{:S(2)}) collective-permute-start(bf16[912,256]{1,0:T(8,128)(2,1)S(1)} %shard_map.100), channel_id=1, source_target_pairs={{4,12},{6,2},{12,20},{14,6},{20,28},{22,14},{28,24},{30,22},{24,16... | collective-permute-start | bytes 1400840 | tf_op jit(solution)/shard_map/ppermute | solution.py:433
  43.6 2.5 %collective-permute-done.12.refs_2_ = bf16[768,256]{1,0:T(8,128)(2,1)S(1)} collective-permute-done((bf16[768,256]{1,0:T(8,128)(2,1)S(1)}, bf16[768,256]{1,0:T(8,128)(2,1)S(1)}, u32[]{:S(2)}, u32[]{:S(2)}) %collective-permute-start.12) | collective-permute-done | bytes 393248 | tf_op jit(solution)/shard_map/ppermute | solution.py:433
  46.9 2.3 %shard_map.99.own_ref = f32[768,256]{1,0:T(8,128)S(1)} custom-call(bf16[1,1536,256]{2,1,0:T(8,128)(2,1)S(1)} %get-tuple-element.60.refs_0_, bf16[2,1536,256]{2,1,0:T(8,128)(2,1)S(1)} %get-tuple-element.64.refs_1_, bf16[2,1536,256]{2,1,0:T(8,128)(2,1)S(1)} %get-tuple-element.68.refs_2_, bf16[2,1536,256]{2,1,0:T(8,128)(2,1)S(1)} %get-tuple-element.75.refs_3_, ...), custom_call_target="tpu_custom_call" | custom-call | flops 1207959552 | bytes 8650752 | tf_op jit(solution)/shard_map/pallas_call | solution.py:47
  49.1 2.0 %collective-permute-done.14.refs_4_.refs_0_ = bf16[912,256]{1,0:T(8,128)(2,1)S(1)} collective-permute-done((bf16[912,256]{1,0:T(8,128)(2,1)S(1)}, bf16[912,256]{1,0:T(8,128)(2,1)S(1)}, u32[]{:S(2)}, u32[]{:S(2)}) %collective-permute-start.14) | collective-permute-done | bytes 466976 | tf_op jit(solution)/shard_map/ppermute | solution.py:433
  52.5 1.6 %collective-permute-start.17 = (bf16[768,256]{1,0:T(8,128)(2,1)S(1)}, bf16[768,256]{1,0:T(8,128)(2,1)S(1)}, u32[]{:S(2)}, u32[]{:S(2)}) collective-permute-start(bf16[768,256]{1,0:T(8,128)(2,1)S(1)} %collective-permute-done.12.refs_2_), channel_id=1, source_target_pairs={{4,12},{6,2},{12,20},{14,6},{20,28},{22,14},{28,24},{30,22},{24,16... | collective-permute-start | bytes 1179656 | tf_op jit(solution)/shard_map/ppermute | solution.py:433
  54.1 1.5 %collective-permute-start.16 = (f32[1,768]{1,0:T(1,128)S(1)}, f32[1,768]{1,0:T(1,128)S(1)}, u32[]{:S(2)}, u32[]{:S(2)}) collective-permute-start(f32[1,768]{1,0:T(1,128)S(1)} %get-tuple-element.91.refs_2_), channel_id=1, source_target_pairs={{0,1},{1,0},{2,3},{3,2},{4,5},{5,4},{6,7},{7,6},{8,9},{9,8},{10,11... | collective-permute-start | bytes 9224 | tf_op jit(solution)/shard_map/ppermute | solution.py:438
  56.1 1.6 %collective-permute-done.16.refs_3_ = f32[1,768]{1,0:T(1,128)S(1)} collective-permute-done((f32[1,768]{1,0:T(1,128)S(1)}, f32[1,768]{1,0:T(1,128)S(1)}, u32[]{:S(2)}, u32[]{:S(2)}) %collective-permute-start.16) | collective-permute-done | bytes 3104 | tf_op jit(solution)/shard_map/ppermute | solution.py:438
  57.7 2.0 %shard_map.101 = (f32[768,256]{1,0:T(8,128)S(1)}, f32[768,256]{1,0:T(8,128)S(1)}) custom-call(bf16[768,256]{1,0:T(8,128)(2,1)S(1)} %shard_map.86.refs_1_.refs_2_.refs_7_.refs_0_, bf16[768,256]{1,0:T(8,128)(2,1)S(1)} %collective-permute-done.13.block_ref.refs_1_, bf16[768,256]{1,0:T(8,128)(2,1)S(1)} %collective-permute-done.12.refs_2_, ...), custom_call_target="tpu_custom_call" | custom-call | flops 1811939328 | bytes 3244032 | tf_op jit(solution)/shard_map/pallas_call | solution.py:47
  59.7 1.6 %collective-permute-start.20 = (bf16[912,256]{1,0:T(8,128)(2,1)S(1)}, bf16[912,256]{1,0:T(8,128)(2,1)S(1)}, u32[]{:S(2)}, u32[]{:S(2)}) collective-permute-start(bf16[912,256]{1,0:T(8,128)(2,1)S(1)} %collective-permute-done.18.refs_2_.refs_0_), channel_id=1, source_target_pairs={{4,12},{6,2},{12,20},{14,6},{20,28},{22,14},{28,24},{30,22},{24,16... | collective-permute-start | bytes 1400840 | tf_op jit(solution)/shard_map/ppermute | solution.py:433
  61.3 2.6 %collective-permute-done.17.refs_1_ = bf16[768,256]{1,0:T(8,128)(2,1)S(1)} collective-permute-done((bf16[768,256]{1,0:T(8,128)(2,1)S(1)}, bf16[768,256]{1,0:T(8,128)(2,1)S(1)}, u32[]{:S(2)}, u32[]{:S(2)}) %collective-permute-start.17) | collective-permute-done | bytes 393248 | tf_op jit(solution)/shard_map/ppermute | solution.py:433
  65.6 1.7 %shard_map.102.group_ref = f32[768,256]{1,0:T(8,128)S(1)} custom-call(bf16[768,256]{1,0:T(8,128)(2,1)S(1)} %shard_map.86.refs_1_.refs_2_.refs_7_.refs_0_, bf16[768,256]{1,0:T(8,128)(2,1)S(1)} %collective-permute-done.15.refs_1_, f32[1,768]{1,0:T(1,128)S(1)} %get-tuple-element.91.refs_2_, f32[1,768]{1,0:T(1,128)S(1)} %collective-permute-done.16.refs_3_, ...), custom_call_target="tpu_custom_call" | custom-call | flops 1207959552 | bytes 2039808 | tf_op jit(solution)/shard_map/pallas_call | solution.py:47
  71.6 2.4 %collective-permute-done.21.message_ref = bf16[48,256]{1,0:T(8,128)(2,1)S(1)} collective-permute-done((bf16[48,256]{1,0:T(8,128)(2,1)S(1)}, bf16[48,256]{1,0:T(8,128)(2,1)S(1)}, u32[]{:S(2)}, u32[]{:S(2)}) %collective-permute-start.21) | collective-permute-done | bytes 24608 | tf_op jit(solution)/shard_map/ppermute | solution.py:577
  76.2 1.6 %collective-permute-done.24.far_ref = bf16[912,256]{1,0:T(8,128)(2,1)S(1)} collective-permute-done((bf16[912,256]{1,0:T(8,128)(2,1)S(1)}, bf16[912,256]{1,0:T(8,128)(2,1)S(1)}, u32[]{:S(2)}, u32[]{:S(2)}) %collective-permute-start.24) | collective-permute-done | bytes 466976 | tf_op jit(solution)/shard_map/ppermute | solution.py:422
  77.9 1.9 %shard_map.107 = f32[768,256]{1,0:T(8,128)} custom-call(bf16[768,256]{1,0:T(8,128)(2,1)S(1)} %copy-done.1, f32[768,256]{1,0:T(8,128)S(1)} %shard_map.102.group_ref, f32[768,256]{1,0:T(8,128)S(1)} %shard_map.106.own_ref, f32[768,256]{1,0:T(8,128)S(1)} %collective-permute-done.23.other_ref, bf16[912,256]{1,0:T(8,128)(2,1)S(1)} %collective-permute-done.20.refs_2_.near_ref, ...), custom_call_target="tpu_custom_call" | custom-call | flops 603979776 | bytes 4497408 | tf_op jit(solution)/shard_map/pallas_call | solution.py:47
  (67 shorter events, 33.7 us)
Async XLA Ops:
  0.6 6.8 %collective-permute-start.3 = (bf16[768,256]{1,0:T(8,128)(2,1)}, bf16[768,256]{1,0:T(8,128)(2,1)S(1)}, u32[]{:S(2)}, u32[]{:S(2)}) collective-permute-start(bf16[768,256]{1,0:T(8,128)(2,1)} %x_ref.7), channel_id=1, source_target_pairs={{0,2},{2,0},{4,6},{6,4},{8,10},{10,8},{12,14},{14,12},{16,18},{18,... | collective-permute-start | bytes 1179656 | tf_op jit(solution)/shard_map/ppermute | solution.py:422
  2.4 8.4 %collective-permute-start = (bf16[768,256]{1,0:T(8,128)(2,1)S(1)}, bf16[768,256]{1,0:T(8,128)(2,1)S(1)}, u32[]{:S(2)}, u32[]{:S(2)}) collective-permute-start(bf16[768,256]{1,0:T(8,128)(2,1)S(1)} %shard_map.85.refs_0_.k_ref.refs_5_.refs_4_), channel_id=1, source_target_pairs={{4,12},{6,2},{12,20},{14,6},{20,28},{22,14},{28,24},{30,22},{24,16... | collective-permute-start | bytes 1179656 | tf_op jit(solution)/shard_map/ppermute | solution.py:433
  6.2 6.5 %collective-permute-start.1 = (bf16[768,256]{1,0:T(8,128)(2,1)S(1)}, bf16[768,256]{1,0:T(8,128)(2,1)S(1)}, u32[]{:S(2)}, u32[]{:S(2)}) collective-permute-start(bf16[768,256]{1,0:T(8,128)(2,1)S(1)} %shard_map.86.refs_1_.refs_2_.refs_7_.refs_0_), channel_id=1, source_target_pairs={{0,2},{2,0},{4,6},{6,4},{8,10},{10,8},{12,14},{14,12},{16,18},{18,... | collective-permute-start | bytes 1179656 | tf_op jit(solution)/shard_map/ppermute | solution.py:422
  7.7 7.8 %collective-permute-start.4 = (bf16[768,256]{1,0:T(8,128)(2,1)S(1)}, bf16[768,256]{1,0:T(8,128)(2,1)S(1)}, u32[]{:S(2)}, u32[]{:S(2)}) collective-permute-start(bf16[768,256]{1,0:T(8,128)(2,1)S(1)} %shard_map.90), channel_id=1, source_target_pairs={{4,12},{6,2},{12,20},{14,6},{20,28},{22,14},{28,24},{30,22},{24,16... | collective-permute-start | bytes 1179656 | tf_op jit(solution)/shard_map/ppermute | solution.py:433
  10.8 9.4 %collective-permute-start.5 = (bf16[768,256]{1,0:T(8,128)(2,1)S(1)}, bf16[768,256]{1,0:T(8,128)(2,1)S(1)}, u32[]{:S(2)}, u32[]{:S(2)}) collective-permute-start(bf16[768,256]{1,0:T(8,128)(2,1)S(1)} %collective-permute-done.refs_0_), channel_id=1, source_target_pairs={{4,12},{6,2},{12,20},{14,6},{20,28},{22,14},{28,24},{30,22},{24,16... | collective-permute-start | bytes 1179656 | tf_op jit(solution)/shard_map/ppermute | solution.py:433
  15.6 8.4 %collective-permute-start.6 = (bf16[768,256]{1,0:T(8,128)(2,1)S(1)}, bf16[768,256]{1,0:T(8,128)(2,1)S(1)}, u32[]{:S(2)}, u32[]{:S(2)}) collective-permute-start(bf16[768,256]{1,0:T(8,128)(2,1)S(1)} %collective-permute-done.4.refs_1_), channel_id=1, source_target_pairs={{4,12},{6,2},{12,20},{14,6},{20,28},{22,14},{28,24},{30,22},{24,16... | collective-permute-start | bytes 1179656 | tf_op jit(solution)/shard_map/ppermute | solution.py:433
  17.0 12.6 %collective-permute-start.9 = (bf16[768,256]{1,0:T(8,128)(2,1)S(1)}, bf16[768,256]{1,0:T(8,128)(2,1)S(1)}, u32[]{:S(2)}, u32[]{:S(2)}) collective-permute-start(bf16[768,256]{1,0:T(8,128)(2,1)S(1)} %shard_map.85.refs_0_.k_ref.refs_5_.refs_4_), channel_id=1, source_target_pairs={{0,1},{1,0},{2,3},{3,2},{4,5},{5,4},{6,7},{7,6},{8,9},{9,8},{10,11... | collective-permute-start | bytes 1179656 | tf_op jit(solution)/shard_map/ppermute | solution.py:438
  20.2 8.0 %collective-permute-start.7 = (bf16[768,256]{1,0:T(8,128)(2,1)S(1)}, bf16[768,256]{1,0:T(8,128)(2,1)S(1)}, u32[]{:S(2)}, u32[]{:S(2)}) collective-permute-start(bf16[768,256]{1,0:T(8,128)(2,1)S(1)} %collective-permute-done.5.refs_0_), channel_id=1, source_target_pairs={{4,12},{6,2},{12,20},{14,6},{20,28},{22,14},{28,24},{30,22},{24,16... | collective-permute-start | bytes 1179656 | tf_op jit(solution)/shard_map/ppermute | solution.py:433
  25.6 7.8 %collective-permute-start.8 = (bf16[768,256]{1,0:T(8,128)(2,1)S(1)}, bf16[768,256]{1,0:T(8,128)(2,1)S(1)}, u32[]{:S(2)}, u32[]{:S(2)}) collective-permute-start(bf16[768,256]{1,0:T(8,128)(2,1)S(1)} %collective-permute-done.6.refs_1_), channel_id=1, source_target_pairs={{4,12},{6,2},{12,20},{14,6},{20,28},{22,14},{28,24},{30,22},{24,16... | collective-permute-start | bytes 1179656 | tf_op jit(solution)/shard_map/ppermute | solution.py:433
  28.2 9.5 %collective-permute-start.10 = (bf16[768,256]{1,0:T(8,128)(2,1)S(1)}, bf16[768,256]{1,0:T(8,128)(2,1)S(1)}, u32[]{:S(2)}, u32[]{:S(2)}) collective-permute-start(bf16[768,256]{1,0:T(8,128)(2,1)S(1)} %collective-permute-done.7.refs_0_), channel_id=1, source_target_pairs={{4,12},{6,2},{12,20},{14,6},{20,28},{22,14},{28,24},{30,22},{24,16... | collective-permute-start | bytes 1179656 | tf_op jit(solution)/shard_map/ppermute | solution.py:433
  30.8 11.1 %collective-permute-start.13 = (bf16[768,256]{1,0:T(8,128)(2,1)S(1)}, bf16[768,256]{1,0:T(8,128)(2,1)S(1)}, u32[]{:S(2)}, u32[]{:S(2)}) collective-permute-start(bf16[768,256]{1,0:T(8,128)(2,1)S(1)} %shard_map.86.refs_1_.refs_2_.refs_7_.refs_0_), channel_id=1, source_target_pairs={{4,12},{6,2},{12,20},{14,6},{20,28},{22,14},{28,24},{30,22},{24,16... | collective-permute-start | bytes 1179656 | tf_op jit(solution)/shard_map/ppermute | solution.py:433
  35.1 11.0 %collective-permute-start.12 = (bf16[768,256]{1,0:T(8,128)(2,1)S(1)}, bf16[768,256]{1,0:T(8,128)(2,1)S(1)}, u32[]{:S(2)}, u32[]{:S(2)}) collective-permute-start(bf16[768,256]{1,0:T(8,128)(2,1)S(1)} %collective-permute-done.1.refs_2_.refs_3_), channel_id=1, source_target_pairs={{4,12},{6,2},{12,20},{14,6},{20,28},{22,14},{28,24},{30,22},{24,16... | collective-permute-start | bytes 1179656 | tf_op jit(solution)/shard_map/ppermute | solution.py:433
  39.6 1.3 %collective-permute-start.11 = (f32[17,768]{1,0:T(8,128)S(1)}, f32[17,768]{1,0:T(8,128)S(1)}, u32[]{:S(2)}, u32[]{:S(2)}) collective-permute-start(f32[17,768]{1,0:T(8,128)S(1)} %get-tuple-element.82), channel_id=1, source_target_pairs={{0,2},{2,0},{4,6},{6,4},{8,10},{10,8},{12,14},{14,12},{16,18},{18,... | collective-permute-start | bytes 156680 | tf_op jit(solution)/shard_map/ppermute | solution.py:422
  41.9 9.2 %collective-permute-start.14 = (bf16[912,256]{1,0:T(8,128)(2,1)S(1)}, bf16[912,256]{1,0:T(8,128)(2,1)S(1)}, u32[]{:S(2)}, u32[]{:S(2)}) collective-permute-start(bf16[912,256]{1,0:T(8,128)(2,1)S(1)} %shard_map.100), channel_id=1, source_target_pairs={{4,12},{6,2},{12,20},{14,6},{20,28},{22,14},{28,24},{30,22},{24,16... | collective-permute-start | bytes 1400840 | tf_op jit(solution)/shard_map/ppermute | solution.py:433
  51.1 8.6 %collective-permute-start.18 = (bf16[912,256]{1,0:T(8,128)(2,1)S(1)}, bf16[912,256]{1,0:T(8,128)(2,1)S(1)}, u32[]{:S(2)}, u32[]{:S(2)}) collective-permute-start(bf16[912,256]{1,0:T(8,128)(2,1)S(1)} %collective-permute-done.14.refs_4_.refs_0_), channel_id=1, source_target_pairs={{4,12},{6,2},{12,20},{14,6},{20,28},{22,14},{28,24},{30,22},{24,16... | collective-permute-start | bytes 1400840 | tf_op jit(solution)/shard_map/ppermute | solution.py:433
  52.5 16.3 %collective-permute-start.19 = (f32[768,256]{1,0:T(8,128)S(1)}, f32[768,256]{1,0:T(8,128)S(1)}, u32[]{:S(2)}, u32[]{:S(2)}) collective-permute-start(f32[768,256]{1,0:T(8,128)S(1)} %shard_map.98), channel_id=1, source_target_pairs={{0,2},{2,0},{4,6},{6,4},{8,10},{10,8},{12,14},{14,12},{16,18},{18,... | collective-permute-start | bytes 2359304 | tf_op jit(solution)/shard_map/ppermute | solution.py:422
  52.5 11.4 %collective-permute-start.17 = (bf16[768,256]{1,0:T(8,128)(2,1)S(1)}, bf16[768,256]{1,0:T(8,128)(2,1)S(1)}, u32[]{:S(2)}, u32[]{:S(2)}) collective-permute-start(bf16[768,256]{1,0:T(8,128)(2,1)S(1)} %collective-permute-done.12.refs_2_), channel_id=1, source_target_pairs={{4,12},{6,2},{12,20},{14,6},{20,28},{22,14},{28,24},{30,22},{24,16... | collective-permute-start | bytes 1179656 | tf_op jit(solution)/shard_map/ppermute | solution.py:433
  54.1 3.6 %collective-permute-start.16 = (f32[1,768]{1,0:T(1,128)S(1)}, f32[1,768]{1,0:T(1,128)S(1)}, u32[]{:S(2)}, u32[]{:S(2)}) collective-permute-start(f32[1,768]{1,0:T(1,128)S(1)} %get-tuple-element.91.refs_2_), channel_id=1, source_target_pairs={{0,1},{1,0},{2,3},{3,2},{4,5},{5,4},{6,7},{7,6},{8,9},{9,8},{10,11... | collective-permute-start | bytes 9224 | tf_op jit(solution)/shard_map/ppermute | solution.py:438
  55.6 10.0 %collective-permute-start.15 = (bf16[768,256]{1,0:T(8,128)(2,1)S(1)}, bf16[768,256]{1,0:T(8,128)(2,1)S(1)}, u32[]{:S(2)}, u32[]{:S(2)}) collective-permute-start(bf16[768,256]{1,0:T(8,128)(2,1)S(1)} %shard_map.86.refs_1_.refs_2_.refs_7_.refs_0_), channel_id=1, source_target_pairs={{0,1},{1,0},{2,3},{3,2},{4,5},{5,4},{6,7},{7,6},{8,9},{9,8},{10,11... | collective-permute-start | bytes 1179656 | tf_op jit(solution)/shard_map/ppermute | solution.py:438
  59.7 10.5 %collective-permute-start.20 = (bf16[912,256]{1,0:T(8,128)(2,1)S(1)}, bf16[912,256]{1,0:T(8,128)(2,1)S(1)}, u32[]{:S(2)}, u32[]{:S(2)}) collective-permute-start(bf16[912,256]{1,0:T(8,128)(2,1)S(1)} %collective-permute-done.18.refs_2_.refs_0_), channel_id=1, source_target_pairs={{4,12},{6,2},{12,20},{14,6},{20,28},{22,14},{28,24},{30,22},{24,16... | collective-permute-start | bytes 1400840 | tf_op jit(solution)/shard_map/ppermute | solution.py:433
  63.9 10.2 %collective-permute-start.22 = (bf16[768,256]{1,0:T(8,128)(2,1)S(1)}, bf16[768,256]{1,0:T(8,128)(2,1)S(1)}, u32[]{:S(2)}, u32[]{:S(2)}) collective-permute-start(bf16[768,256]{1,0:T(8,128)(2,1)S(1)} %collective-permute-done.17.refs_1_), channel_id=1, source_target_pairs={{4,12},{6,2},{12,20},{14,6},{20,28},{22,14},{28,24},{30,22},{24,16... | collective-permute-start | bytes 1179656 | tf_op jit(solution)/shard_map/ppermute | solution.py:433
  70.2 3.9 %collective-permute-start.21 = (bf16[48,256]{1,0:T(8,128)(2,1)S(1)}, bf16[48,256]{1,0:T(8,128)(2,1)S(1)}, u32[]{:S(2)}, u32[]{:S(2)}) collective-permute-start(bf16[48,256]{1,0:T(8,128)(2,1)S(1)} %bitcast.7), channel_id=1, source_target_pairs={{4,12},{6,2},{12,20},{14,6},{20,28},{22,14},{28,24},{30,22},{24,16... | collective-permute-start | bytes 73736 | tf_op jit(solution)/shard_map/ppermute | solution.py:577
  74.9 3.0 %collective-permute-start.23 = (f32[768,256]{1,0:T(8,128)S(1)}, f32[768,256]{1,0:T(8,128)S(1)}, u32[]{:S(2)}, u32[]{:S(2)}) collective-permute-start(f32[768,256]{1,0:T(8,128)S(1)} %shard_map.105), channel_id=1, source_target_pairs={{0,2},{2,0},{4,6},{6,4},{8,10},{10,8},{12,14},{14,12},{16,18},{18,... | collective-permute-start | bytes 2359304 | tf_op jit(solution)/shard_map/ppermute | solution.py:422
  74.9 2.9 %collective-permute-start.24 = (bf16[912,256]{1,0:T(8,128)(2,1)S(1)}, bf16[912,256]{1,0:T(8,128)(2,1)S(1)}, u32[]{:S(2)}, u32[]{:S(2)}) collective-permute-start(bf16[912,256]{1,0:T(8,128)(2,1)S(1)} %collective-permute-done.20.refs_2_.near_ref), channel_id=1, source_target_pairs={{0,2},{2,0},{4,6},{6,4},{8,10},{10,8},{12,14},{14,12},{16,18},{18,... | collective-permute-start | bytes 1400840 | tf_op jit(solution)/shard_map/ppermute | solution.py:422
  (9 other events, 25.4 us)
